TPU v7x, 256 devices: a whole 4x4x8 slice. The times are simulated.
256 devices in a mesh: lat: 8 (over x, core), lon: 16 (over y_hi, z), section: 2 (over y_lo).
Axes of the slice: x: 4, y: 4 (y_hi: 2, y_lo: 2; y = y_hi * 2 + y_lo), z: 8, core: 2. Of those that a mesh axis runs over, the one named last changes fastest.
Arguments:
- fields: bfloat16 [4, 69, 512, 1024], P(None, None, 'lat', 'lon'), may hold values from -6 to 6
- embed_weight: bfloat16 [10, 10, 69, 1024], P('section'), may hold values from -0.078125 to 0.078125
- embed_bias: bfloat16 [1024], replicated, may hold values from -3 to 3
- pos_embed: bfloat16 [64, 128, 1024], P('lat', 'lon'), may hold values from -6 to 6
- member_ids: int32 [4], P('section'), may hold values from 0 to 49
- member_table: bfloat16 [50, 1024], replicated, may hold values from -6 to 6
- norm_gain: float32 [1024], replicated, may hold values from 0.5 to 1.5
- w_qkv: bfloat16 [3, 1024, 1024], P(None, 'lon'), may hold values from -0.1875 to 0.1875
- query_gain: float32 [16, 64], P('lon'), may hold values from 2 to 3
- key_gain: float32 [16, 64], P('lon'), may hold values from 2 to 3
- w_gate_up: bfloat16 [2, 4096, 1024], P(None, 'lon'), may hold values from -0.1875 to 0.1875
- w_out: bfloat16 [1024, 1024], P('lon'), may hold values from -0.1875 to 0.1875
- w_down: bfloat16 [4096, 1024], P('lon'), may hold values from -0.09375 to 0.09375
Outputs:
- processed: bfloat16 [4, 8192, 1024], P('section', ('lat', 'lon'))
All inputs are finite; a program needn't handle non-finite values.
Results may differ from a plain program's by a relative error of at most 0.02.
Values may be sent and summed in bfloat16 or wider, within the bound.
No kernel may reach another device: no remote copies, remote signals or barrier semaphores. Data moves between devices by JAX's collectives and lax.ppermute only.
A program may use at most 128 MiB of HBM per device.

v0:
```python
import functools

import jax
import jax.numpy as jnp
from jax import lax
from jax.experimental import pallas as pl
from jax.experimental.pallas import tpu as pltpu
from jax.sharding import Mesh, PartitionSpec as P

PATCH = 8
layer_epsilon = 1e-05
head_epsilon = 1e-06
LOG2E = 1.4426950408889634
HEAD = 64

X, CORE, YH, Z, YL = 4, 2, 2, 8, 2
LAT = ("x", "core")
LON = ("yh", "z")


def other_half_weights(array):
    return lax.ppermute(array, ("yh", "yl"), [(0, 3), (3, 0), (1, 2), (2, 1)])


def edges_kernel(s_ref, top_ref, left_ref, right_ref, row_ref, low_ref, high_ref, wide):
    row_ref[...] = top_ref[:, 0]
    members, rows, cols, channels = right_ref.shape
    wide[..., :channels] = right_ref[...].reshape(wide.shape[0], cols, channels).astype(jnp.float32)
    low = wide[:, cols - 1, :channels]
    low_ref[...] = low.reshape(low_ref.shape).astype(jnp.bfloat16)
    wide[..., :channels] = left_ref[...].reshape(wide.shape[0], cols, channels).astype(jnp.float32)
    high = wide[:, 0, :channels]
    high_ref[...] = high.reshape(high_ref.shape).astype(jnp.bfloat16)


def edges(f, ids):
    members, rows, cols, channels = f.shape
    column = (members, rows, 16, channels)
    line = jax.ShapeDtypeStruct((members, rows, channels), f.dtype)
    whole = pl.BlockSpec((members, rows, channels), lambda i, s: (0, 0, 0))
    return pl.pallas_call(
        edges_kernel,
        grid_spec=pltpu.PrefetchScalarGridSpec(
            num_scalar_prefetch=1,
            grid=(1,),
            in_specs=[
                pl.BlockSpec(
                    (members, 1, cols, channels), lambda i, s: (0, (1 - s[0]) * (rows - 1), 0, 0)
                ),
                pl.BlockSpec(column, lambda i, s: (0, 0, 0, 0)),
                pl.BlockSpec(column, lambda i, s: (0, 0, cols // 16 - 1, 0)),
            ],
            out_specs=[whole] * 3,
            scratch_shapes=[pltpu.VMEM((members * rows, 16, 128), jnp.float32)],
        ),
        out_shape=[line] * 3,
        compiler_params=pltpu.CompilerParams(vmem_limit_bytes=40 * 2**20),
    )(ids, f, f, f)


def halo(f, ids, section):
    lats, lons = X * CORE, YH * Z
    row, low, high = edges(f, ids)
    to_lat = [(2 * i, 2 * i + 2) for i in range(lats - 1)]
    to_lat += [(2 * i + 1, 2 * i - 1) for i in range(1, lats)]
    forward = [(i, (i + 1) % lons) for i in range(lons)]
    backward = [(target, source) for source, target in forward]
    row = lax.ppermute(row, LAT + ("yl",), to_lat)

    def column(edge, corner, pairs):
        edge = jnp.concatenate([edge, corner[:, None]], 1)
        edge = lax.ppermute(edge, LON, pairs)
        edge = jnp.concatenate([edge[:, -1:], edge, jnp.zeros_like(edge[:, :3])], 1)
        edge = lax.dynamic_slice_in_dim(edge, section * 5, 64, 1)
        edge = edge.reshape(2, 2, 2, 4, 8, edge.shape[-1])[:, :, :, :, :5].astype(jnp.float32)
        return jnp.transpose(edge, (4, 2, 0, 3, 1, 5)).reshape(5, 32, edge.shape[-1])

    return row, column(low, row[:, -1], forward), column(high, row[:, 0], backward)


def embed_kernel(
    ids_ref, f_ref, row_ref, low_ref, high_ref, w_ref, pos_ref, out_ref, xf, rhs, acc
):
    step = pl.program_id(0)
    section = ids_ref[0]
    channels = f_ref.shape[4]
    offset = step - 1 + 5 * section
    shift = jnp.where(offset < 0, -1, jnp.where(offset > 7, 1, 0))

    @pl.when(step == 0)
    def _():
        xf[...] = jnp.zeros_like(xf)
        rhs[...] = jnp.zeros_like(rhs)
        acc[...] = jnp.zeros_like(acc)

    for slot in range(32):
        patch = slot // 16 * 4 + slot // 2 % 4
        member = slot // 8 % 2 * 2 + slot % 2
        at = patch + shift
        value = f_ref[member, jnp.clip(at, 0, 7), 0]
        if patch in (0, 7):
            value = jnp.where((at < 0) | (at > 7), row_ref[member], value)
        xf[slot, 8:72, :channels] = value.astype(jnp.float32)
        xf[slot, 7:8, :channels] = low_ref[0, slot : slot + 1]
        xf[slot, 72:73, :channels] = high_ref[0, slot : slot + 1]
    taps = w_ref.shape[1]
    columns = []
    for b in range(taps):
        rhs[b * 128 : b * 128 + channels, :] = w_ref[0, b]
        column = xf[:, pl.ds(7 + b, 8, stride=8), :]
        columns.append(column.reshape(256, 128).astype(jnp.bfloat16))
    lhs = jnp.concatenate(columns, 1)
    acc[...] += jnp.dot(lhs, rhs[...], preferred_element_type=jnp.float32)

    @pl.when(step == pl.num_programs(0) - 1)
    def _():
        first = jnp.where(section == 0, 1.0, 0.0)
        for slot in range(32):
            patch = slot // 16 * 4 + slot // 2 % 4
            rows = slice(8 * slot, 8 * slot + 8)
            acc[rows, :] += first * pos_ref[patch].astype(jnp.float32)
        out_ref[...] = acc[...].astype(jnp.bfloat16)


def embed(f, row, low, high, weight, pos, ids):
    taps, cols, channels, width = weight.shape
    members, rows, wide, _ = f.shape
    whole = lambda n: (lambda i, s: (0,) * n)
    return pl.pallas_call(
        embed_kernel,
        grid_spec=pltpu.PrefetchScalarGridSpec(
            num_scalar_prefetch=1,
            grid=(taps,),
            in_specs=[
                pl.BlockSpec(
                    (members, 8, 1, wide, channels),
                    lambda i, s: (0, 0, (i + 7 + 5 * s[0]) % 8, 0, 0),
                ),
                pl.BlockSpec(row.shape, whole(3)),
                pl.BlockSpec((1, 32, channels), lambda i, s: (i, 0, 0)),
                pl.BlockSpec((1, 32, channels), lambda i, s: (i, 0, 0)),
                pl.BlockSpec((1, cols, channels, width), lambda i, s: (i, 0, 0, 0)),
                pl.BlockSpec(pos.shape, whole(3)),
            ],
            out_specs=pl.BlockSpec((256, width), whole(2)),
            scratch_shapes=[
                pltpu.VMEM((32, 80, 128), jnp.float32),
                pltpu.VMEM((cols * 128, width), jnp.bfloat16),
                pltpu.VMEM((256, width), jnp.float32),
            ],
        ),
        out_shape=jax.ShapeDtypeStruct((256, width), jnp.bfloat16),
        compiler_params=pltpu.CompilerParams(vmem_limit_bytes=52 * 2**20),
        cost_estimate=pl.CostEstimate(
            flops=8 * 10**9, bytes_accessed=12 * 2**20, transcendentals=0
        ),
    )(ids, f.reshape(members, 8, rows // 8, wide, channels), row, low, high, weight, pos)


def attend_kernel(last, ids_ref, q_ref, kv_ref, *refs):
    acc_refs, o_ref, v1 = refs[:-2], refs[-2], refs[-1]
    blocks, _, nk = kv_ref.shape
    bq = q_ref.shape[0]
    bk = 256

    @pl.when(pl.program_id(0) == 0)
    def _():
        for c in range(blocks):
            rows = kv_ref[c, HEAD:, :]
            stacked = jnp.concatenate([rows, jnp.ones_like(rows)], 0)
            v1[pl.ds(c * nk, nk), :] = stacked.T

    q = q_ref[...]

    def body(c, acc):
        for b in range(0, nk, bk):
            scores = jnp.dot(q, kv_ref[c, :HEAD, b : b + bk], preferred_element_type=jnp.float32)
            weights = jnp.exp2(scores).astype(jnp.bfloat16)
            values = v1[pl.ds(pl.multiple_of(c * nk + b, bk), bk), :]
            acc = acc + jnp.dot(weights, values, preferred_element_type=jnp.float32)
        return acc

    if acc_refs:
        acc = acc_refs[0][...]
    else:
        acc = jnp.zeros((bq, 2 * HEAD), jnp.float32)
    acc = lax.fori_loop(0, blocks, body, acc, unroll=2)
    if last:
        halves = (acc / pltpu.roll(acc, HEAD, 1)).reshape(bq // 64, 2, 32, 2 * HEAD)
        left, right = halves[:, 0], halves[:, 1]
        right = pltpu.roll(right.reshape(bq // 2, 2 * HEAD), HEAD, 1).reshape(left.shape)
        lane = lax.broadcasted_iota(jnp.int32, left.shape, 2)
        packed = jnp.where(lane < HEAD, left, right).astype(jnp.bfloat16)
        half = packed.shape[0] // 2
        yh = ids_ref[3]
        o_ref[pl.ds(yh * half, half)] = packed[:half]
        o_ref[pl.ds(half - yh * half, half)] = packed[half:]
    else:
        o_ref[...] = acc


def attend(ids, q, kv, acc=None, last=False):
    n = q.shape[0]
    bq = n // CORE
    keys = kv.shape[0] * kv.shape[2]
    rows = lambda w: pl.BlockSpec((bq, w), lambda i, s: (i, 0))
    if last:
        out_spec = pl.BlockSpec((bq // 64, 32, 2 * HEAD), lambda i, s: ((i + s[1]) % CORE, 0, 0))
        out_shape = jax.ShapeDtypeStruct((n // 64, 32, 2 * HEAD), jnp.bfloat16)
    else:
        out_spec = rows(2 * HEAD)
        out_shape = jax.ShapeDtypeStruct((n, 2 * HEAD), jnp.float32)
    return pl.pallas_call(
        functools.partial(attend_kernel, last),
        grid_spec=pltpu.PrefetchScalarGridSpec(
            num_scalar_prefetch=1,
            grid=(CORE,),
            in_specs=[rows(HEAD), pl.BlockSpec(kv.shape, lambda i, s: (0, 0, 0))]
            + ([rows(2 * HEAD)] if acc is not None else []),
            out_specs=out_spec,
            scratch_shapes=[pltpu.VMEM((keys, 2 * HEAD), jnp.bfloat16)],
        ),
        out_shape=out_shape,
        compiler_params=pltpu.CompilerParams(vmem_limit_bytes=40 * 2**20),
        cost_estimate=pl.CostEstimate(
            flops=64 * n * keys * HEAD, bytes_accessed=4 * 2**20, transcendentals=n * keys
        ),
    )(ids, q, kv, *([acc] if acc is not None else []))


def ring_z(own, beside, parts=1):
    z = lax.axis_index("z")
    rows, members, cols, width = own.shape
    size = rows // parts
    forward = [(i, (i + 1) % Z) for i in range(Z)]
    backward = [(target, source) for source, target in forward]
    out = jnp.zeros((rows, members, Z * cols, width), own.dtype)

    def place(out, shard, part, at):
        return lax.dynamic_update_slice(out, shard, (part * size, 0, (at % Z) * cols, 0))

    out = place(out, own, 0, z)
    ups = [own[p * size : (p + 1) * size] for p in range(parts)]
    downs = list(ups)
    for step in range(1, Z // 2 + 1):
        for p in range(parts):
            ups[p] = lax.ppermute(ups[p], "z", forward)
            if step < Z // 2:
                downs[p] = lax.ppermute(downs[p], "z", backward)
        if step == 2:
            ups, downs, beside = lax.optimization_barrier((ups, downs, beside))
        for p in range(parts):
            out = place(out, ups[p], p, z - step + Z)
            if step < Z // 2:
                out = place(out, downs[p], p, z + step)
    return out, beside


def project_kernel(ids_ref, x_ref, own_ref, other_ref, gain_ref, *out_refs):
    core = ids_ref[1]
    for rel_core in range(2):
        member = core if rel_core == 0 else 1 - core
        x = x_ref[:, member].reshape(-1, x_ref.shape[3])
        for rel_head, w in enumerate((own_ref[...], other_ref[: 3 * HEAD])):
            out = lax.dot_general(
                w, x, (((1,), (1,)), ((), ())), preferred_element_type=jnp.float32
            )
            out_ref = out_refs[2 * rel_core + rel_head]
            for kind in range(2):
                part = out[kind * HEAD : (kind + 1) * HEAD]
                mean = jnp.mean(part * part, axis=0, keepdims=True)
                part = part * lax.rsqrt(mean + head_epsilon) * gain_ref[rel_head, kind]
                if kind == 0:
                    part = part * (LOG2E / 8.0)
                out_ref[kind * HEAD : (kind + 1) * HEAD, :] = part.astype(jnp.bfloat16)
            out_ref[2 * HEAD :, :] = out[2 * HEAD :].astype(jnp.bfloat16)


def project(x, own, other, gains, ids):
    tokens = x.shape[0] * x.shape[2]
    whole = lambda a: pl.BlockSpec(a.shape, lambda i, s: (0,) * a.ndim)
    out = jax.ShapeDtypeStruct((3 * HEAD, tokens), jnp.bfloat16)
    return pl.pallas_call(
        project_kernel,
        grid_spec=pltpu.PrefetchScalarGridSpec(
            num_scalar_prefetch=1,
            grid=(1,),
            in_specs=[whole(x), whole(own), whole(other), whole(gains)],
            out_specs=[whole(out)] * 4,
        ),
        out_shape=[out] * 4,
        compiler_params=pltpu.CompilerParams(vmem_limit_bytes=32 * 2**20),
        cost_estimate=pl.CostEstimate(flops=3 * 10**9, bytes_accessed=4 * 2**20, transcendentals=0),
    )(ids, x, own, other, gains)


def mlp_kernel(ids_ref, x_ref, tok_ref, gu_ref, down_ref, other_ref, o_ref, acc):
    rows, members, cols, width = x_ref.shape
    units = down_ref.shape[0]
    x = x_ref[...].reshape(-1, width)
    contract = (((1,), (1,)), ((), ()))
    other = [other_ref[n * units : (n + 1) * units] for n in range(3)]
    total = None
    for gate_w, up_w, down_w in ((gu_ref[0], gu_ref[1], down_ref[...]), other):
        gate = lax.dot_general(x, gate_w, contract, preferred_element_type=jnp.float32)
        up = lax.dot_general(x, up_w, contract, preferred_element_type=jnp.float32)
        hidden = (gate / (1.0 + jnp.exp(-gate)) * up).astype(jnp.bfloat16)
        term = jnp.dot(hidden, down_w, preferred_element_type=jnp.float32)
        total = term if total is None else total + term
    acc[...] = total.reshape(acc.shape)
    at = pl.multiple_of(ids_ref[2] * 8, 8)
    acc[:, :, pl.ds(at, 8), :] += tok_ref[...].astype(jnp.float32)
    o_ref[...] = acc[...].astype(jnp.bfloat16)


def mlp(x, tokens, gu, down, other, ids, rows=4):
    whole = lambda a: pl.BlockSpec(a.shape, lambda i, s: (0,) * a.ndim)
    block = lambda a: pl.BlockSpec((rows,) + a.shape[1:], lambda i, s: (i, 0, 0, 0))
    return pl.pallas_call(
        mlp_kernel,
        grid_spec=pltpu.PrefetchScalarGridSpec(
            num_scalar_prefetch=1,
            grid=(x.shape[0] // rows,),
            in_specs=[block(x), block(tokens)] + [whole(a) for a in (gu, down, other)],
            out_specs=block(x),
            scratch_shapes=[pltpu.VMEM((rows,) + x.shape[1:], jnp.float32)],
        ),
        out_shape=jax.ShapeDtypeStruct(x.shape, jnp.bfloat16),
        compiler_params=pltpu.CompilerParams(vmem_limit_bytes=32 * 2**20),
        cost_estimate=pl.CostEstimate(flops=6 * 10**9, bytes_accessed=8 * 2**20, transcendentals=0),
    )(ids, x, tokens, gu, down, other)


def shards(
    fields,
    embed_weight,
    embed_bias,
    pos_embed,
    member_ids,
    member_table,
    norm_gain,
    w_qkv,
    query_gain,
    key_gain,
    w_gate_up,
    w_out,
    w_down,
):
    f32, bf16 = jnp.float32, jnp.bfloat16
    width = embed_weight.shape[3]
    yl = lax.axis_index("yl")
    yh = lax.axis_index("yh")
    core = lax.axis_index("core")

    gains = jnp.concatenate([query_gain, key_gain], 0)
    coarse = lax.reduce_precision(gains, 8, 7)
    middle = lax.reduce_precision(gains - coarse, 8, 7)
    fine = gains - coarse - middle
    terms = jnp.stack([coarse, middle, fine], 0).astype(bf16).reshape(1, 6 * HEAD)
    terms = jnp.pad(terms, ((0, 15), (0, width - 6 * HEAD)))
    qkv_other = other_half_weights(jnp.concatenate([w_qkv.reshape(-1, width), terms], 0))
    mlp_other = other_half_weights(
        jnp.concatenate([w_gate_up.reshape(-1, width), w_down], 0)
    )
    terms = qkv_other[-16:, : 6 * HEAD][0].astype(f32).reshape(3, 2, HEAD)
    gains_other = terms[0] + terms[1] + terms[2]
    gain_both = jnp.stack([gains, gains_other], 0)[..., None]
    w_out_half = lax.all_gather(w_out, "z", axis=0, tiled=True)
    ids = jnp.stack([yl, core, lax.axis_index("z"), yh]).astype(jnp.int32)

    f = jnp.transpose(fields, (0, 2, 3, 1))
    row, low, high = halo(f, ids, yl)
    part = embed(f, row, low, high, embed_weight, pos_embed, ids)
    part = lax.all_to_all(part, ("yh", "yl"), 0, 0, tiled=True)
    part = part.reshape(YH, YL, 4, 2, 8, width).astype(f32)
    embedded = jnp.transpose(part[:, 0] + part[:, 1], (1, 0, 2, 3, 4)).reshape(8, 2, 8, width)
    one_hot = (
        member_ids[:, None] == jnp.arange(member_table.shape[0], dtype=jnp.int32)[None, :]
    ).astype(bf16)
    member_vecs = jnp.dot(one_hot, member_table, preferred_element_type=f32)
    tokens = (
        embedded
        + embed_bias.astype(f32)
        + member_vecs[None, :, None, :]
    ).astype(bf16)
    residual = tokens.astype(f32)
    average = jnp.mean(residual, axis=-1, keepdims=True)
    centered = residual - average
    variance = jnp.mean(centered * centered, axis=-1, keepdims=True)
    normed = (centered * lax.rsqrt(variance + layer_epsilon) * norm_gain).astype(bf16)

    normed_all, (w_out_half, qkv_other) = ring_z(normed, (w_out_half, qkv_other))

    normed_all, mlp_other = lax.optimization_barrier((normed_all, mlp_other))

    mine, mine_yh, theirs, theirs_yh = project(
        normed_all, w_qkv.reshape(3 * HEAD, width), qkv_other, gain_both, ids
    )
    pair = ("core", "yh")
    got_core = lax.ppermute(theirs, pair, [(0, 2), (2, 0), (1, 3), (3, 1)])
    got_yh = lax.ppermute(mine_yh, pair, [(0, 1), (1, 0), (2, 3), (3, 2)])
    got_both = lax.ppermute(theirs_yh, pair, [(0, 3), (3, 0), (1, 2), (2, 1)])
    got_core, normed_all = lax.optimization_barrier((got_core, normed_all))
    blocks = jnp.stack([mine, got_yh, got_core, got_both], 0)
    kv_own = blocks[:, HEAD:]

    x_up = [(i, (i + 1) % X) for i in range(X)]
    x_down = [(target, source) for source, target in x_up]
    first, second = kv_own[:2], kv_own[2:]
    near = [lax.ppermute(first, "x", x_up), lax.ppermute(second, "x", x_down)]
    late = [lax.ppermute(second, "x", x_up), lax.ppermute(first, "x", x_down)]
    far = [lax.ppermute(near[0], "x", x_up), lax.ppermute(near[1], "x", x_down)]

    q = jnp.transpose(blocks[:, :HEAD], (0, 2, 1)).reshape(-1, HEAD)

    update = mlp(normed_all, tokens, w_gate_up, w_down, mlp_other, ids)
    summed = lax.psum_scatter(update, "z", scatter_dimension=0, tiled=True)[0]

    acc = attend(ids, q, kv_own)
    acc, w_out_half = lax.optimization_barrier((acc, w_out_half))
    w_out_other = other_half_weights(w_out_half)
    acc = attend(ids, q, jnp.concatenate(near, 0), acc)
    acc = attend(ids, q, jnp.concatenate(late, 0), acc)
    attended = attend(ids, q, jnp.concatenate(far, 0), acc, last=True)
    attended = lax.all_to_all(attended, ("core", "yh", "z"), 0, 0, tiled=True)
    attended = attended.reshape(CORE, YH, Z, 32, 2, HEAD)
    attended = jnp.transpose(attended, (0, 4, 3, 1, 2, 5)).reshape(CORE * 64, YH * Z * HEAD)
    half = Z * HEAD
    own_cols = lax.dynamic_slice_in_dim(attended, yh * half, half, 1)
    other_cols = lax.dynamic_slice_in_dim(attended, half - yh * half, half, 1)
    mixed = jnp.dot(own_cols, w_out_half, preferred_element_type=f32)
    mixed = mixed + jnp.dot(other_cols, w_out_other, preferred_element_type=f32)
    mixed = mixed.reshape(2, 64, width)
    return (summed.astype(f32) + mixed).astype(bf16)


def solution(mesh):
    chips = Mesh(mesh.devices.reshape(X, CORE, YH, Z, YL), ("x", "core", "yh", "z", "yl"))
    return jax.shard_map(
        shards,
        mesh=chips,
        in_specs=(
            P(None, None, LAT, LON),
            P("yl", None, None, None),
            P(),
            P(LAT, LON, None),
            P("yl"),
            P(),
            P(),
            P(None, LON, None),
            P(LON, None),
            P(LON, None),
            P(None, LON, None),
            P(LON, None),
            P(LON, None),
        ),
        out_specs=P("yl", LAT + LON, None),
        check_vma=False,
    )
```

profile of v0, /device:TPU:1, one launch (start us, length us, event | category | flops | bytes accessed | tf_op | source)
XLA Modules:
  0.0 196.8 jit_solution(9464855961381995298)
XLA Ops:
  6.6 2.2 %copy-done.1 = bf16[4,69,64,64]{1,3,2,0:T(8,128)(2,1)S(1)} copy-done((bf16[4,69,64,64]{1,3,2,0:T(8,128)(2,1)S(1)}, bf16[4,69,64,64]{1,3,2,0:T(8,128)(2,1)}, u32[]{:S(2)}) %copy-start.1) | copy-done | bytes 2261016
  10.2 4.5 %collective-permute-start = (bf16[4,64,69]{2,1,0:T(8,128)(2,1)S(1)}, bf16[4,64,69]{2,1,0:T(8,128)(2,1)S(1)}, u32[]{:S(2)}, u32[]{:S(2)}) collective-permute-start(bf16[4,64,69]{2,1,0:T(8,128)(2,1)S(1)} %get-tuple-element.22), channel_id=1, source_target_pairs={{0,32},{32,64},{64,96},{96,128},{128,160},{160,192},{192,224},{33,... | collective-permute-start | bytes 105992 | tf_op jit(solution)/shard_map/ppermute | solution.py:68
  16.1 1.7 collective-permute-start.1
  17.8 6.7 %collective-permute-start.2 = (bf16[4,65,69]{2,1,0:T(8,128)(2,1)S(1)}, bf16[4,65,69]{2,1,0:T(8,128)(2,1)S(1)}, u32[]{:S(2)}, u32[]{:S(2)}) collective-permute-start(bf16[4,65,69]{2,1,0:T(8,128)(2,1)S(1)} %pad_maximum_fusion.10), channel_id=1, source_target_pairs={{2,0},{4,2},{6,4},{8,6},{10,8},{12,10},{14,12},{16,14},{18,16},{20... | collective-permute-start | bytes 107648 | tf_op jit(solution)/shard_map/ppermute | solution.py:72
  26.4 9.3 %shard_map.128 = bf16[256,1024]{1,0:T(8,128)(2,1)} custom-call(s32[4]{0:T(128)S(1)} %pad_add_fusion.s_ref.ids_ref, bf16[4,8,8,64,69]{4,3,2,1,0:T(8,128)(2,1)} %bitcast.58, bf16[4,64,69]{2,1,0:T(8,128)(2,1)S(1)} %collective-permute-done.row_ref, f32[5,32,69]{2,1,0:T(8,128)S(1)} %bitcast.73, f32[5,32,69]{2,1,0:T(8,128)S(1)} %bitcast.72, ...), custom_call_target="tpu_custom_call" | custom-call | flops 8000000000 | bytes 12582912 | tf_op jit(solution)/shard_map/pallas_call | solution.py:129
  35.7 3.6 %all-to-all-start = ((bf16[4,64,1024]{2,1,0:T(8,128)(2,1)}), bf16[4,64,1024]{2,1,0:T(8,128)(2,1)S(1)}, u32[]{:S(2)}, u32[]{:S(2)}) async-start(bf16[4,64,1024]{2,1,0:T(8,128)(2,1)} %bitcast.12), calls=%async_computation | async-start | bytes 1048576 | tf_op jit(solution)/shard_map/all_to_all | solution.py:374
  40.2 2.6 %collective-permute-start.7 = (bf16[208,1024]{1,0:T(8,128)(2,1)}, bf16[208,1024]{1,0:T(8,128)(2,1)}, u32[]{:S(2)}, u32[]{:S(2)}) collective-permute-start(bf16[208,1024]{1,0:T(8,128)(2,1)} %fusion.7), channel_id=1, source_target_pairs={{0,17},{17,0},{1,16},{16,1},{2,19},{19,2},{3,18},{18,3},{4,21},{21... | collective-permute-start | bytes 1277960 | tf_op jit(solution)/shard_map/ppermute | solution.py:22
  44.4 4.3 %all-to-all-done = bf16[4,64,1024]{2,1,0:T(8,128)(2,1)S(1)} async-done(((bf16[4,64,1024]{2,1,0:T(8,128)(2,1)}), bf16[4,64,1024]{2,1,0:T(8,128)(2,1)S(1)}, u32[]{:S(2)}, u32[]{:S(2)}) %all-to-all-start) | async-done | bytes 524320 | tf_op jit(solution)/shard_map/all_to_all | solution.py:374
  50.6 4.3 %collective-permute-start.4 = (bf16[8,2,8,1024]{3,2,1,0:T(8,128)(2,1)}, bf16[8,2,8,1024]{3,2,1,0:T(8,128)(2,1)}, u32[]{:S(2)}, u32[]{:S(2)}) collective-permute-start(bf16[8,2,8,1024]{3,2,1,0:T(8,128)(2,1)} %get-tuple-element.40), channel_id=1, source_target_pairs={{2,0},{4,2},{6,4},{8,6},{10,8},{12,10},{14,12},{0,14},{3,1},{5,3},... | collective-permute-start | bytes 786440 | tf_op jit(solution)/shard_map/ppermute | solution.py:249
  54.8 8.3 %collective-permute-done.3 = bf16[8,2,8,1024]{3,2,1,0:T(8,128)(2,1)} collective-permute-done((bf16[8,2,8,1024]{3,2,1,0:T(8,128)(2,1)}, bf16[8,2,8,1024]{3,2,1,0:T(8,128)(2,1)}, u32[]{:S(2)}, u32[]{:S(2)}) %collective-permute-start.3) | collective-permute-done | bytes 262176 | tf_op jit(solution)/shard_map/ppermute | solution.py:247
  63.1 2.7 %collective-permute-start.6 = (bf16[8,2,8,1024]{3,2,1,0:T(8,128)(2,1)}, bf16[8,2,8,1024]{3,2,1,0:T(8,128)(2,1)}, u32[]{:S(2)}, u32[]{:S(2)}) collective-permute-start(bf16[8,2,8,1024]{3,2,1,0:T(8,128)(2,1)} %collective-permute-done.4), channel_id=1, source_target_pairs={{2,0},{4,2},{6,4},{8,6},{10,8},{12,10},{14,12},{0,14},{3,1},{5,3},... | collective-permute-start | bytes 786440 | tf_op jit(solution)/shard_map/ppermute | solution.py:249
  67.4 7.5 %collective-permute-done.5 = bf16[8,2,8,1024]{3,2,1,0:T(8,128)(2,1)} collective-permute-done((bf16[8,2,8,1024]{3,2,1,0:T(8,128)(2,1)}, bf16[8,2,8,1024]{3,2,1,0:T(8,128)(2,1)}, u32[]{:S(2)}, u32[]{:S(2)}) %collective-permute-start.5) | collective-permute-done | bytes 262176 | tf_op jit(solution)/shard_map/ppermute | solution.py:247
  74.9 5.7 %all-gather.2.cloned.1.call-done = bf16[512,1024]{1,0:T(8,128)(2,1)} async-done(((bf16[64,1024]{1,0:T(8,128)(2,1)}), bf16[512,1024]{1,0:T(8,128)(2,1)}) %all-gather.2.cloned.1.call-update) | async-done | bytes 1048592 | tf_op jit(solution)/shard_map/all_gather | solution.py:368
  83.4 1.9 collective-permute-start.9
  89.4 4.8 %collective-permute-done.10 = bf16[8,2,8,1024]{3,2,1,0:T(8,128)(2,1)S(1)} collective-permute-done((bf16[8,2,8,1024]{3,2,1,0:T(8,128)(2,1)S(1)}, bf16[8,2,8,1024]{3,2,1,0:T(8,128)(2,1)S(1)}, u32[]{:S(2)}, u32[]{:S(2)}) %collective-permute-start.10) | collective-permute-done | bytes 262176 | tf_op jit(solution)/shard_map/ppermute | solution.py:247
  94.2 3.1 %shard_map.129 = (bf16[192,512]{1,0:T(8,128)(2,1)S(1)}, bf16[192,512]{1,0:T(8,128)(2,1)S(1)}, bf16[192,512]{1,0:T(8,128)(2,1)S(1)}, bf16[192,512]{1,0:T(8,128)(2,1)S(1)}) custom-call(s32[4]{0:T(128)S(1)} %pad_add_fusion.s_ref.ids_ref, bf16[8,2,64,1024]{3,2,1,0:T(8,128)(2,1)S(1)} %constant_dynamic-update-slice_fusion.x_ref, bf16[192,1024]{1,0:T(8,128)(2,1)S(1)} %bitcast.71, ...), custom_call_target="tpu_custom_call" | custom-call | flops 3000000000 | bytes 4194304 | tf_op jit(solution)/shard_map/pallas_call | solution.py:283
  97.3 5.1 %collective-permute-start.12 = (bf16[192,512]{1,0:T(8,128)(2,1)S(1)}, bf16[192,512]{1,0:T(8,128)(2,1)S(1)}, u32[]{:S(2)}, u32[]{:S(2)}) collective-permute-start(bf16[192,512]{1,0:T(8,128)(2,1)S(1)} %get-tuple-element.29), channel_id=1, source_target_pairs={{0,32},{32,0},{16,48},{48,16},{1,33},{33,1},{17,49},{49,17},{2,34}... | collective-permute-start | bytes 589832 | tf_op jit(solution)/shard_map/ppermute | solution.py:400
  102.4 3.2 %collective-permute-start.13 = (bf16[192,512]{1,0:T(8,128)(2,1)S(1)}, bf16[192,512]{1,0:T(8,128)(2,1)S(1)}, u32[]{:S(2)}, u32[]{:S(2)}) collective-permute-start(bf16[192,512]{1,0:T(8,128)(2,1)S(1)} %get-tuple-element.33), channel_id=1, source_target_pairs={{0,16},{16,0},{32,48},{48,32},{1,17},{17,1},{33,49},{49,33},{2,18}... | collective-permute-start | bytes 589832 | tf_op jit(solution)/shard_map/ppermute | solution.py:401
  105.7 5.1 %collective-permute-done.13 = bf16[192,512]{1,0:T(8,128)(2,1)S(1)} collective-permute-done((bf16[192,512]{1,0:T(8,128)(2,1)S(1)}, bf16[192,512]{1,0:T(8,128)(2,1)S(1)}, u32[]{:S(2)}, u32[]{:S(2)}) %collective-permute-start.13) | collective-permute-done | bytes 196640 | tf_op jit(solution)/shard_map/ppermute | solution.py:401
  111.5 3.5 %collective-permute-done.14 = bf16[192,512]{1,0:T(8,128)(2,1)S(1)} collective-permute-done((bf16[192,512]{1,0:T(8,128)(2,1)S(1)}, bf16[192,512]{1,0:T(8,128)(2,1)S(1)}, u32[]{:S(2)}, u32[]{:S(2)}) %collective-permute-start.14) | collective-permute-done | bytes 196640 | tf_op jit(solution)/shard_map/ppermute | solution.py:402
  121.4 5.9 %shard_map.130 = bf16[8,2,64,1024]{3,2,1,0:T(8,128)(2,1)S(1)} custom-call(s32[4]{0:T(128)S(1)} %pad_add_fusion.s_ref.ids_ref, bf16[8,2,64,1024]{3,2,1,0:T(8,128)(2,1)S(1)} %constant_dynamic-update-slice_fusion.x_ref, bf16[8,2,8,1024]{3,2,1,0:T(8,128)(2,1)S(1)} %get-tuple-element.50.tok_ref, bf16[2,256,1024]{2,1,0:T(8,128)(2,1)S(1)} %copy-done.3, ...), custom_call_target="tpu_custom_call" | custom-call | flops 6000000000 | bytes 8388608 | tf_op jit(solution)/shard_map/pallas_call | solution.py:319
  129.9 6.4 %shard_map.131.refs_0_ = f32[2048,128]{1,0:T(8,128)S(1)} custom-call(s32[4]{0:T(128)S(1)} %pad_add_fusion.s_ref.ids_ref, bf16[2048,64]{1,0:T(8,128)(2,1)S(1)} %bitcast.66, bf16[4,128,512]{2,1,0:T(8,128)(2,1)S(1)} %copy-done.4), custom_call_target="tpu_custom_call" | custom-call | flops 17179869184 | bytes 4194304 | tf_op jit(solution)/shard_map/pallas_call | solution.py:213
  136.4 2.4 %collective-permute-start.21 = (bf16[512,1024]{1,0:T(8,128)(2,1)}, bf16[512,1024]{1,0:T(8,128)(2,1)}, u32[]{:S(2)}, u32[]{:S(2)}) collective-permute-start(bf16[512,1024]{1,0:T(8,128)(2,1)} %all-gather.2.cloned.1.call-done), channel_id=1, source_target_pairs={{0,17},{17,0},{1,16},{16,1},{2,19},{19,2},{3,18},{18,3},{4,21},{21... | collective-permute-start | bytes 3145736 | tf_op jit(solution)/shard_map/ppermute | solution.py:22
  139.9 6.5 %shard_map.132.refs_0_ = f32[2048,128]{1,0:T(8,128)S(1)} custom-call(s32[4]{0:T(128)S(1)} %pad_add_fusion.s_ref.ids_ref, bf16[2048,64]{1,0:T(8,128)(2,1)S(1)} %bitcast.67, bf16[4,128,512]{2,1,0:T(8,128)(2,1)S(1)} %pad_maximum_fusion.6.kv_ref, f32[2048,128]{1,0:T(8,128)S(1)} %shard_map.131.refs_0_), custom_call_target="tpu_custom_call" | custom-call | flops 17179869184 | bytes 4194304 | tf_op jit(solution)/shard_map/pallas_call | solution.py:213
  147.4 2.0 %collective-permute-start.18 = (bf16[2,128,512]{2,1,0:T(8,128)(2,1)}, bf16[2,128,512]{2,1,0:T(8,128)(2,1)S(1)}, u32[]{:S(2)}, u32[]{:S(2)}) collective-permute-start(bf16[2,128,512]{2,1,0:T(8,128)(2,1)} %collective-permute-done.17), channel_id=1, source_target_pairs={{64,0},{128,64},{192,128},{0,192},{65,1},{129,65},{193,129},{1,193... | collective-permute-start | bytes 786440 | tf_op jit(solution)/shard_map/ppermute | solution.py:412
  150.5 6.5 %shard_map.133.refs_0_ = f32[2048,128]{1,0:T(8,128)S(1)} custom-call(s32[4]{0:T(128)S(1)} %pad_add_fusion.s_ref.ids_ref, bf16[2048,64]{1,0:T(8,128)(2,1)S(1)} %bitcast.68, bf16[4,128,512]{2,1,0:T(8,128)(2,1)S(1)} %pad_maximum_fusion.5.kv_ref, f32[2048,128]{1,0:T(8,128)S(1)} %shard_map.132.refs_0_), custom_call_target="tpu_custom_call" | custom-call | flops 17179869184 | bytes 4194304 | tf_op jit(solution)/shard_map/pallas_call | solution.py:213
  157.0 7.7 %shard_map.134 = bf16[32,32,128]{2,1,0:T(8,128)(2,1)} custom-call(s32[4]{0:T(128)S(1)} %pad_add_fusion.s_ref.ids_ref, bf16[2048,64]{1,0:T(8,128)(2,1)S(1)} %bitcast.69, bf16[4,128,512]{2,1,0:T(8,128)(2,1)S(1)} %pad_maximum_fusion.4.kv_ref, f32[2048,128]{1,0:T(8,128)S(1)} %shard_map.133.refs_0_), custom_call_target="tpu_custom_call" | custom-call | flops 17179869184 | bytes 4194304 | tf_op jit(solution)/shard_map/pallas_call | solution.py:213
  164.7 7.7 %all-to-all-start.1 = ((bf16[32,32,128]{2,1,0:T(8,128)(2,1)}), bf16[32,32,128]{2,1,0:T(8,128)(2,1)S(1)}, u32[]{:S(2)}, u32[]{:S(2)}) async-start(bf16[32,32,128]{2,1,0:T(8,128)(2,1)} %shard_map.134), calls=%async_computation.2 | async-start | bytes 524288 | tf_op jit(solution)/shard_map/all_to_all | solution.py:425
  172.4 11.8 %all-to-all-done.1 = bf16[32,32,128]{2,1,0:T(8,128)(2,1)S(1)} async-done(((bf16[32,32,128]{2,1,0:T(8,128)(2,1)}), bf16[32,32,128]{2,1,0:T(8,128)(2,1)S(1)}, u32[]{:S(2)}, u32[]{:S(2)}) %all-to-all-start.1) | async-done | bytes 262176 | tf_op jit(solution)/shard_map/all_to_all | solution.py:425
  185.2 1.5 fusion.9
  186.7 1.5 convolution_add_fusion
  188.3 1.7 fusion.4
  (124 shorter events, 31.3 us)
Async XLA Ops:
  6.5 37.7 %copy-start = (bf16[50,1024]{1,0:T(8,128)(2,1)S(1)}, bf16[50,1024]{1,0:T(8,128)(2,1)}, u32[]{:S(2)}) copy-start(bf16[50,1024]{1,0:T(8,128)(2,1)} %param.18) | copy-start | bytes 307204
  8.8 17.6 %copy-start.10 = (bf16[8,8,1024]{2,1,0:T(8,128)(2,1)S(1)}, bf16[8,8,1024]{2,1,0:T(8,128)(2,1)}, u32[]{:S(2)}) copy-start(bf16[8,8,1024]{2,1,0:T(8,128)(2,1)} %pos_ref.1) | copy-start | bytes 393220
  10.2 5.8 %collective-permute-start = (bf16[4,64,69]{2,1,0:T(8,128)(2,1)S(1)}, bf16[4,64,69]{2,1,0:T(8,128)(2,1)S(1)}, u32[]{:S(2)}, u32[]{:S(2)}) collective-permute-start(bf16[4,64,69]{2,1,0:T(8,128)(2,1)S(1)} %get-tuple-element.22), channel_id=1, source_target_pairs={{0,32},{32,64},{64,96},{96,128},{128,160},{160,192},{192,224},{33,... | collective-permute-start | bytes 105992 | tf_op jit(solution)/shard_map/ppermute | solution.py:68
  16.1 10.0 %collective-permute-start.1 = (bf16[4,65,69]{2,1,0:T(8,128)(2,1)S(1)}, bf16[4,65,69]{2,1,0:T(8,128)(2,1)S(1)}, u32[]{:S(2)}, u32[]{:S(2)}) collective-permute-start(bf16[4,65,69]{2,1,0:T(8,128)(2,1)S(1)} %pad_maximum_fusion.9), channel_id=1, source_target_pairs={{0,2},{2,4},{4,6},{6,8},{8,10},{10,12},{12,14},{14,16},{16,18},{18... | collective-permute-start | bytes 107648 | tf_op jit(solution)/shard_map/ppermute | solution.py:72
  17.8 8.3 %collective-permute-start.2 = (bf16[4,65,69]{2,1,0:T(8,128)(2,1)S(1)}, bf16[4,65,69]{2,1,0:T(8,128)(2,1)S(1)}, u32[]{:S(2)}, u32[]{:S(2)}) collective-permute-start(bf16[4,65,69]{2,1,0:T(8,128)(2,1)S(1)} %pad_maximum_fusion.10), channel_id=1, source_target_pairs={{2,0},{4,2},{6,4},{8,6},{10,8},{12,10},{14,12},{16,14},{18,16},{20... | collective-permute-start | bytes 107648 | tf_op jit(solution)/shard_map/ppermute | solution.py:72
  26.4 13.0 %copy-start.7 = (bf16[3,64,1024]{2,1,0:T(8,128)(2,1)S(1)}, bf16[3,64,1024]{2,1,0:T(8,128)(2,1)}, u32[]{:S(2)}) copy-start(bf16[3,64,1024]{2,1,0:T(8,128)(2,1)} %param.20) | copy-start | bytes 1179652
  35.7 13.1 %all-to-all-start = ((bf16[4,64,1024]{2,1,0:T(8,128)(2,1)}), bf16[4,64,1024]{2,1,0:T(8,128)(2,1)S(1)}, u32[]{:S(2)}, u32[]{:S(2)}) async-start(bf16[4,64,1024]{2,1,0:T(8,128)(2,1)} %bitcast.12), calls=%async_computation | async-start | bytes 1048576 | tf_op jit(solution)/shard_map/all_to_all | solution.py:374
  39.3 41.3 %all-gather.2.cloned.1.call-start = ((), (), s32[]{:S(2)}) async-start(), calls=%async_computation.3 | async-start | bytes 1179648 | tf_op jit(solution)/shard_map/all_gather | solution.py:368
  40.2 25.6 %collective-permute-start.7 = (bf16[208,1024]{1,0:T(8,128)(2,1)}, bf16[208,1024]{1,0:T(8,128)(2,1)}, u32[]{:S(2)}, u32[]{:S(2)}) collective-permute-start(bf16[208,1024]{1,0:T(8,128)(2,1)} %fusion.7), channel_id=1, source_target_pairs={{0,17},{17,0},{1,16},{16,1},{2,19},{19,2},{3,18},{18,3},{4,21},{21... | collective-permute-start | bytes 1277960 | tf_op jit(solution)/shard_map/ppermute | solution.py:22
  42.8 145.5 %reduce-scatter.2.cloned.1.call-start = ((), (), s32[]{:S(2)}) async-start(), calls=%async_computation.4 | async-start | bytes 2359296 | tf_op jit(solution)/shard_map/reduce_scatter | solution.py:417
  44.2 50.0 %collective-permute-start.11 = (bf16[768,1024]{1,0:T(8,128)(2,1)}, bf16[768,1024]{1,0:T(8,128)(2,1)}, u32[]{:S(2)}, u32[]{:S(2)}) collective-permute-start(bf16[768,1024]{1,0:T(8,128)(2,1)} %pad_maximum_fusion), channel_id=1, source_target_pairs={{0,17},{17,0},{1,16},{16,1},{2,19},{19,2},{3,18},{18,3},{4,21},{21... | collective-permute-start | bytes 4718600 | tf_op jit(solution)/shard_map/ppermute | solution.py:22
  50.6 12.5 %collective-permute-start.3 = (bf16[8,2,8,1024]{3,2,1,0:T(8,128)(2,1)}, bf16[8,2,8,1024]{3,2,1,0:T(8,128)(2,1)}, u32[]{:S(2)}, u32[]{:S(2)}) collective-permute-start(bf16[8,2,8,1024]{3,2,1,0:T(8,128)(2,1)} %get-tuple-element.40), channel_id=1, source_target_pairs={{0,2},{2,4},{4,6},{6,8},{8,10},{10,12},{12,14},{14,0},{1,3},{3,5},... | collective-permute-start | bytes 786440 | tf_op jit(solution)/shard_map/ppermute | solution.py:247
  50.6 12.5 %collective-permute-start.4 = (bf16[8,2,8,1024]{3,2,1,0:T(8,128)(2,1)}, bf16[8,2,8,1024]{3,2,1,0:T(8,128)(2,1)}, u32[]{:S(2)}, u32[]{:S(2)}) collective-permute-start(bf16[8,2,8,1024]{3,2,1,0:T(8,128)(2,1)} %get-tuple-element.40), channel_id=1, source_target_pairs={{2,0},{4,2},{6,4},{8,6},{10,8},{12,10},{14,12},{0,14},{3,1},{5,3},... | collective-permute-start | bytes 786440 | tf_op jit(solution)/shard_map/ppermute | solution.py:249
  63.1 11.8 %collective-permute-start.5 = (bf16[8,2,8,1024]{3,2,1,0:T(8,128)(2,1)}, bf16[8,2,8,1024]{3,2,1,0:T(8,128)(2,1)}, u32[]{:S(2)}, u32[]{:S(2)}) collective-permute-start(bf16[8,2,8,1024]{3,2,1,0:T(8,128)(2,1)} %collective-permute-done.3), channel_id=1, source_target_pairs={{0,2},{2,4},{4,6},{6,8},{8,10},{10,12},{12,14},{14,0},{1,3},{3,5},... | collective-permute-start | bytes 786440 | tf_op jit(solution)/shard_map/ppermute | solution.py:247
  63.1 11.8 %collective-permute-start.6 = (bf16[8,2,8,1024]{3,2,1,0:T(8,128)(2,1)}, bf16[8,2,8,1024]{3,2,1,0:T(8,128)(2,1)}, u32[]{:S(2)}, u32[]{:S(2)}) collective-permute-start(bf16[8,2,8,1024]{3,2,1,0:T(8,128)(2,1)} %collective-permute-done.4), channel_id=1, source_target_pairs={{2,0},{4,2},{6,4},{8,6},{10,8},{12,10},{14,12},{0,14},{3,1},{5,3},... | collective-permute-start | bytes 786440 | tf_op jit(solution)/shard_map/ppermute | solution.py:249
  80.6 13.5 %copy-start.8 = (bf16[3,64,1024]{2,1,0:T(8,128)(2,1)S(1)}, bf16[3,64,1024]{2,1,0:T(8,128)(2,1)}, u32[]{:S(2)}) copy-start(bf16[3,64,1024]{2,1,0:T(8,128)(2,1)} %param.20) | copy-start | bytes 1179652
  80.6 13.5 %copy-start.9 = (f32[2,2,64,1]{3,2,1,0:T(8,128)S(1)}, f32[2,2,64,1]{3,2,1,0:T(8,128)}, u32[]{:S(2)}) copy-start(f32[2,2,64,1]{3,2,1,0:T(8,128)} %copy.54.gain_ref) | copy-start | bytes 3076
  80.6 7.0 %collective-permute-start.8 = (bf16[8,2,8,1024]{3,2,1,0:T(8,128)(2,1)}, bf16[8,2,8,1024]{3,2,1,0:T(8,128)(2,1)S(1)}, u32[]{:S(2)}, u32[]{:S(2)}) collective-permute-start(bf16[8,2,8,1024]{3,2,1,0:T(8,128)(2,1)} %collective-permute-done.5), channel_id=1, source_target_pairs={{0,2},{2,4},{4,6},{6,8},{8,10},{10,12},{12,14},{14,0},{1,3},{3,5},... | collective-permute-start | bytes 786440 | tf_op jit(solution)/shard_map/ppermute | solution.py:247
  83.4 5.9 %collective-permute-start.9 = (bf16[8,2,8,1024]{3,2,1,0:T(8,128)(2,1)}, bf16[8,2,8,1024]{3,2,1,0:T(8,128)(2,1)S(1)}, u32[]{:S(2)}, u32[]{:S(2)}) collective-permute-start(bf16[8,2,8,1024]{3,2,1,0:T(8,128)(2,1)} %collective-permute-done.6), channel_id=1, source_target_pairs={{2,0},{4,2},{6,4},{8,6},{10,8},{12,10},{14,12},{0,14},{3,1},{5,3},... | collective-permute-start | bytes 786440 | tf_op jit(solution)/shard_map/ppermute | solution.py:249
  87.7 6.4 %collective-permute-start.10 = (bf16[8,2,8,1024]{3,2,1,0:T(8,128)(2,1)S(1)}, bf16[8,2,8,1024]{3,2,1,0:T(8,128)(2,1)S(1)}, u32[]{:S(2)}, u32[]{:S(2)}) collective-permute-start(bf16[8,2,8,1024]{3,2,1,0:T(8,128)(2,1)S(1)} %collective-permute-done.8), channel_id=1, source_target_pairs={{0,2},{2,4},{4,6},{6,8},{8,10},{10,12},{12,14},{14,0},{1,3},{3,5},... | collective-permute-start | bytes 786440 | tf_op jit(solution)/shard_map/ppermute | solution.py:247
  97.3 24.1 %copy-start.6 = (bf16[256,1024]{1,0:T(8,128)(2,1)S(1)}, bf16[256,1024]{1,0:T(8,128)(2,1)}, u32[]{:S(2)}) copy-start(bf16[256,1024]{1,0:T(8,128)(2,1)} %down_ref.1) | copy-start | bytes 1572868
  97.3 8.4 %collective-permute-start.12 = (bf16[192,512]{1,0:T(8,128)(2,1)S(1)}, bf16[192,512]{1,0:T(8,128)(2,1)S(1)}, u32[]{:S(2)}, u32[]{:S(2)}) collective-permute-start(bf16[192,512]{1,0:T(8,128)(2,1)S(1)} %get-tuple-element.29), channel_id=1, source_target_pairs={{0,32},{32,0},{16,48},{48,16},{1,33},{33,1},{17,49},{49,17},{2,34}... | collective-permute-start | bytes 589832 | tf_op jit(solution)/shard_map/ppermute | solution.py:400
  102.4 8.3 %collective-permute-start.13 = (bf16[192,512]{1,0:T(8,128)(2,1)S(1)}, bf16[192,512]{1,0:T(8,128)(2,1)S(1)}, u32[]{:S(2)}, u32[]{:S(2)}) collective-permute-start(bf16[192,512]{1,0:T(8,128)(2,1)S(1)} %get-tuple-element.33), channel_id=1, source_target_pairs={{0,16},{16,0},{32,48},{48,32},{1,17},{17,1},{33,49},{49,33},{2,18}... | collective-permute-start | bytes 589832 | tf_op jit(solution)/shard_map/ppermute | solution.py:401
  105.6 9.4 %collective-permute-start.14 = (bf16[192,512]{1,0:T(8,128)(2,1)S(1)}, bf16[192,512]{1,0:T(8,128)(2,1)S(1)}, u32[]{:S(2)}, u32[]{:S(2)}) collective-permute-start(bf16[192,512]{1,0:T(8,128)(2,1)S(1)} %get-tuple-element.35), channel_id=1, source_target_pairs={{0,48},{48,0},{16,32},{32,16},{1,49},{49,1},{17,33},{33,17},{2,50}... | collective-permute-start | bytes 589832 | tf_op jit(solution)/shard_map/ppermute | solution.py:402
  117.3 21.5 %collective-permute-start.15 = (bf16[2,128,512]{2,1,0:T(8,128)(2,1)}, bf16[2,128,512]{2,1,0:T(8,128)(2,1)}, u32[]{:S(2)}, u32[]{:S(2)}) collective-permute-start(bf16[2,128,512]{2,1,0:T(8,128)(2,1)} %pad_maximum_fusion.8), channel_id=1, source_target_pairs={{0,64},{64,128},{128,192},{192,0},{1,65},{65,129},{129,193},{193,1... | collective-permute-start | bytes 786440 | tf_op jit(solution)/shard_map/ppermute | solution.py:410
  118.6 30.8 %collective-permute-start.20 = (bf16[2,128,512]{2,1,0:T(8,128)(2,1)}, bf16[2,128,512]{2,1,0:T(8,128)(2,1)}, u32[]{:S(2)}, u32[]{:S(2)}) collective-permute-start(bf16[2,128,512]{2,1,0:T(8,128)(2,1)} %pad_maximum_fusion.8), channel_id=1, source_target_pairs={{64,0},{128,64},{192,128},{0,192},{65,1},{129,65},{193,129},{1,193... | collective-permute-start | bytes 786440 | tf_op jit(solution)/shard_map/ppermute | solution.py:411
  119.9 18.9 %collective-permute-start.17 = (bf16[2,128,512]{2,1,0:T(8,128)(2,1)}, bf16[2,128,512]{2,1,0:T(8,128)(2,1)}, u32[]{:S(2)}, u32[]{:S(2)}) collective-permute-start(bf16[2,128,512]{2,1,0:T(8,128)(2,1)} %pad_maximum_fusion.7), channel_id=1, source_target_pairs={{64,0},{128,64},{192,128},{0,192},{65,1},{129,65},{193,129},{1,193... | collective-permute-start | bytes 786440 | tf_op jit(solution)/shard_map/ppermute | solution.py:410
  121.2 28.2 %collective-permute-start.19 = (bf16[2,128,512]{2,1,0:T(8,128)(2,1)}, bf16[2,128,512]{2,1,0:T(8,128)(2,1)}, u32[]{:S(2)}, u32[]{:S(2)}) collective-permute-start(bf16[2,128,512]{2,1,0:T(8,128)(2,1)} %pad_maximum_fusion.7), channel_id=1, source_target_pairs={{0,64},{64,128},{128,192},{192,0},{1,65},{65,129},{129,193},{193,1... | collective-permute-start | bytes 786440 | tf_op jit(solution)/shard_map/ppermute | solution.py:411
  136.4 50.3 %collective-permute-start.21 = (bf16[512,1024]{1,0:T(8,128)(2,1)}, bf16[512,1024]{1,0:T(8,128)(2,1)}, u32[]{:S(2)}, u32[]{:S(2)}) collective-permute-start(bf16[512,1024]{1,0:T(8,128)(2,1)} %all-gather.2.cloned.1.call-done), channel_id=1, source_target_pairs={{0,17},{17,0},{1,16},{16,1},{2,19},{19,2},{3,18},{18,3},{4,21},{21... | collective-permute-start | bytes 3145736 | tf_op jit(solution)/shard_map/ppermute | solution.py:22
  146.4 10.6 %collective-permute-start.16 = (bf16[2,128,512]{2,1,0:T(8,128)(2,1)}, bf16[2,128,512]{2,1,0:T(8,128)(2,1)S(1)}, u32[]{:S(2)}, u32[]{:S(2)}) collective-permute-start(bf16[2,128,512]{2,1,0:T(8,128)(2,1)} %collective-permute-done.15), channel_id=1, source_target_pairs={{0,64},{64,128},{128,192},{192,0},{1,65},{65,129},{129,193},{193,1... | collective-permute-start | bytes 786440 | tf_op jit(solution)/shard_map/ppermute | solution.py:412
  147.4 9.6 %collective-permute-start.18 = (bf16[2,128,512]{2,1,0:T(8,128)(2,1)}, bf16[2,128,512]{2,1,0:T(8,128)(2,1)S(1)}, u32[]{:S(2)}, u32[]{:S(2)}) collective-permute-start(bf16[2,128,512]{2,1,0:T(8,128)(2,1)} %collective-permute-done.17), channel_id=1, source_target_pairs={{64,0},{128,64},{192,128},{0,192},{65,1},{129,65},{193,129},{1,193... | collective-permute-start | bytes 786440 | tf_op jit(solution)/shard_map/ppermute | solution.py:412
  164.7 19.5 %all-to-all-start.1 = ((bf16[32,32,128]{2,1,0:T(8,128)(2,1)}), bf16[32,32,128]{2,1,0:T(8,128)(2,1)S(1)}, u32[]{:S(2)}, u32[]{:S(2)}) async-start(bf16[32,32,128]{2,1,0:T(8,128)(2,1)} %shard_map.134), calls=%async_computation.2 | async-start | bytes 524288 | tf_op jit(solution)/shard_map/all_to_all | solution.py:425
  (11 other events, 42.6 us)
Sparse Core Ops, SparseCore 0:
  42.9 37.6 all-gather.1
  128.8 37.8 reduce-scatter.1
where the time goes:
time: 198 us; the launch traced here: 197 us
  waiting for transfers between devices  55.7 us (28%)
  starting transfers between devices  54.6 us (28%)
  Pallas kernels  46.8 us (24%)
  between operations  13.9 us (7%)
  other arithmetic  11.4 us (6%)
  local copies, waits for them, and re-layouts  11.2 us (6%)
  matrix products  3.26 us (2%)
    pallas_call x4, Pallas kernels, attend(): pl.pallas_call(functools.partial(attend_kernel, last), grid_spec=pltpu.Pr...  27.1 us
    ppermute x4, waiting for transfers between devices, ring_z(): ups[p] = lax.ppermute(ups[p], 'z', forward)  21.9 us
    all_to_all x1, waiting for transfers between devices, shards(): attended = lax.all_to_all(attended, ('core', 'yh', 'z'), 0, 0, tiled=True)  11.8 us
    pallas_call x1, Pallas kernels, embed(): pl.pallas_call(embed_kernel, grid_spec=pltpu.PrefetchScalarGridSpec(num_s...  9.28 us
    ppermute x3, starting transfers between devices, ring_z(): downs[p] = lax.ppermute(downs[p], 'z', backward)  8.87 us
    ppermute x2, starting transfers between devices, column(): edge = lax.ppermute(edge, LON, pairs)  8.38 us
    all_to_all x1, starting transfers between devices, shards(): attended = lax.all_to_all(attended, ('core', 'yh', 'z'), 0, 0, tiled=True)  7.69 us
    pallas_call x1, Pallas kernels, mlp(): pl.pallas_call(mlp_kernel, grid_spec=pltpu.PrefetchScalarGridSpec(num_sca...  5.9 us
  transfers between devices with their start and end apart: 26, of which 12 were waited for; matrix products, arithmetic and copies ran while one was open for 9% of the time, Pallas kernels for 17%

commit v1 on v0

--- a/solution.py
+++ b/solution.py
@@ -157,7 +157,7 @@
     )(ids, f.reshape(members, 8, rows // 8, wide, channels), row, low, high, weight, pos)
 
 
-def attend_kernel(last, ids_ref, q_ref, kv_ref, *refs):
+def attend_kernel(last, ids_ref, q_ref, kv_ref, kv2_ref, *refs):
     acc_refs, o_ref, v1 = refs[:-2], refs[-2], refs[-1]
     blocks, _, nk = kv_ref.shape
     bq = q_ref.shape[0]
@@ -165,26 +165,28 @@
 
     @pl.when(pl.program_id(0) == 0)
     def _():
-        for c in range(blocks):
-            rows = kv_ref[c, HEAD:, :]
+        for c in range(2 * blocks):
+            rows = (kv_ref if c < blocks else kv2_ref)[c % blocks, HEAD:, :]
             stacked = jnp.concatenate([rows, jnp.ones_like(rows)], 0)
             v1[pl.ds(c * nk, nk), :] = stacked.T
 
     q = q_ref[...]
 
     def body(c, acc):
-        for b in range(0, nk, bk):
-            scores = jnp.dot(q, kv_ref[c, :HEAD, b : b + bk], preferred_element_type=jnp.float32)
-            weights = jnp.exp2(scores).astype(jnp.bfloat16)
-            values = v1[pl.ds(pl.multiple_of(c * nk + b, bk), bk), :]
-            acc = acc + jnp.dot(weights, values, preferred_element_type=jnp.float32)
+        for n, ref in enumerate((kv_ref, kv2_ref)):
+            for b in range(0, nk, bk):
+                scores = jnp.dot(q, ref[c, :HEAD, b : b + bk], preferred_element_type=jnp.float32)
+                weights = jnp.exp2(scores).astype(jnp.bfloat16)
+                at = pl.multiple_of((n * blocks + c) * nk + b, bk)
+                values = v1[pl.ds(at, bk), :]
+                acc = acc + jnp.dot(weights, values, preferred_element_type=jnp.float32)
         return acc
 
     if acc_refs:
         acc = acc_refs[0][...]
     else:
         acc = jnp.zeros((bq, 2 * HEAD), jnp.float32)
-    acc = lax.fori_loop(0, blocks, body, acc, unroll=2)
+    acc = lax.fori_loop(0, blocks, body, acc)
     if last:
         halves = (acc / pltpu.roll(acc, HEAD, 1)).reshape(bq // 64, 2, 32, 2 * HEAD)
         left, right = halves[:, 0], halves[:, 1]
@@ -202,7 +204,7 @@
 def attend(ids, q, kv, acc=None, last=False):
     n = q.shape[0]
     bq = n // CORE
-    keys = kv.shape[0] * kv.shape[2]
+    keys = 2 * kv[0].shape[0] * kv[0].shape[2]
     rows = lambda w: pl.BlockSpec((bq, w), lambda i, s: (i, 0))
     if last:
         out_spec = pl.BlockSpec((bq // 64, 32, 2 * HEAD), lambda i, s: ((i + s[1]) % CORE, 0, 0))
@@ -215,7 +217,8 @@
         grid_spec=pltpu.PrefetchScalarGridSpec(
             num_scalar_prefetch=1,
             grid=(CORE,),
-            in_specs=[rows(HEAD), pl.BlockSpec(kv.shape, lambda i, s: (0, 0, 0))]
+            in_specs=[rows(HEAD)]
+            + [pl.BlockSpec(a.shape, lambda i, s: (0, 0, 0)) for a in kv]
             + ([rows(2 * HEAD)] if acc is not None else []),
             out_specs=out_spec,
             scratch_shapes=[pltpu.VMEM((keys, 2 * HEAD), jnp.bfloat16)],
@@ -223,9 +226,9 @@
         out_shape=out_shape,
         compiler_params=pltpu.CompilerParams(vmem_limit_bytes=40 * 2**20),
         cost_estimate=pl.CostEstimate(
-            flops=64 * n * keys * HEAD, bytes_accessed=4 * 2**20, transcendentals=n * keys
-        ),
-    )(ids, q, kv, *([acc] if acc is not None else []))
+            flops=12 * n * keys * HEAD, bytes_accessed=4 * 2**20, transcendentals=n * keys
+        ),
+    )(ids, q, *kv, *([acc] if acc is not None else []))
 
 
 def ring_z(own, beside, parts=1):
@@ -365,7 +368,6 @@
     terms = qkv_other[-16:, : 6 * HEAD][0].astype(f32).reshape(3, 2, HEAD)
     gains_other = terms[0] + terms[1] + terms[2]
     gain_both = jnp.stack([gains, gains_other], 0)[..., None]
-    w_out_half = lax.all_gather(w_out, "z", axis=0, tiled=True)
     ids = jnp.stack([yl, core, lax.axis_index("z"), yh]).astype(jnp.int32)
 
     f = jnp.transpose(fields, (0, 2, 3, 1))
@@ -389,9 +391,9 @@
     variance = jnp.mean(centered * centered, axis=-1, keepdims=True)
     normed = (centered * lax.rsqrt(variance + layer_epsilon) * norm_gain).astype(bf16)
 
-    normed_all, (w_out_half, qkv_other) = ring_z(normed, (w_out_half, qkv_other))
-
-    normed_all, mlp_other = lax.optimization_barrier((normed_all, mlp_other))
+    normed_all, qkv_other = ring_z(normed, qkv_other)
+    normed_all, mlp_other, w_out = lax.optimization_barrier((normed_all, mlp_other, w_out))
+    w_out_half = lax.all_gather(w_out, "z", axis=0, tiled=True)
 
     mine, mine_yh, theirs, theirs_yh = project(
         normed_all, w_qkv.reshape(3 * HEAD, width), qkv_other, gain_both, ids
@@ -400,28 +402,29 @@
     got_core = lax.ppermute(theirs, pair, [(0, 2), (2, 0), (1, 3), (3, 1)])
     got_yh = lax.ppermute(mine_yh, pair, [(0, 1), (1, 0), (2, 3), (3, 2)])
     got_both = lax.ppermute(theirs_yh, pair, [(0, 3), (3, 0), (1, 2), (2, 1)])
-    got_core, normed_all = lax.optimization_barrier((got_core, normed_all))
-    blocks = jnp.stack([mine, got_yh, got_core, got_both], 0)
-    kv_own = blocks[:, HEAD:]
+
+    update = mlp(normed_all, tokens, w_gate_up, w_down, mlp_other, ids)
+    got_core, got_yh, got_both, update = lax.optimization_barrier(
+        (got_core, got_yh, got_both, update)
+    )
+    summed = lax.psum_scatter(update, "z", scatter_dimension=0, tiled=True)[0]
+    first = jnp.stack([mine[HEAD:], got_yh[HEAD:]], 0)
+    second = jnp.stack([got_core[HEAD:], got_both[HEAD:]], 0)
+    q = jnp.stack([a[:HEAD] for a in (mine, got_yh, got_core, got_both)], 0)
+    q = jnp.transpose(q, (0, 2, 1)).reshape(-1, HEAD)
 
     x_up = [(i, (i + 1) % X) for i in range(X)]
     x_down = [(target, source) for source, target in x_up]
-    first, second = kv_own[:2], kv_own[2:]
     near = [lax.ppermute(first, "x", x_up), lax.ppermute(second, "x", x_down)]
     late = [lax.ppermute(second, "x", x_up), lax.ppermute(first, "x", x_down)]
     far = [lax.ppermute(near[0], "x", x_up), lax.ppermute(near[1], "x", x_down)]
 
-    q = jnp.transpose(blocks[:, :HEAD], (0, 2, 1)).reshape(-1, HEAD)
-
-    update = mlp(normed_all, tokens, w_gate_up, w_down, mlp_other, ids)
-    summed = lax.psum_scatter(update, "z", scatter_dimension=0, tiled=True)[0]
-
-    acc = attend(ids, q, kv_own)
+    acc = attend(ids, q, (first, second))
+    acc = attend(ids, q, near, acc)
+    acc = attend(ids, q, late, acc)
     acc, w_out_half = lax.optimization_barrier((acc, w_out_half))
     w_out_other = other_half_weights(w_out_half)
-    acc = attend(ids, q, jnp.concatenate(near, 0), acc)
-    acc = attend(ids, q, jnp.concatenate(late, 0), acc)
-    attended = attend(ids, q, jnp.concatenate(far, 0), acc, last=True)
+    attended = attend(ids, q, far, acc, last=True)
     attended = lax.all_to_all(attended, ("core", "yh", "z"), 0, 0, tiled=True)
     attended = attended.reshape(CORE, YH, Z, 32, 2, HEAD)
     attended = jnp.transpose(attended, (0, 4, 3, 1, 2, 5)).reshape(CORE * 64, YH * Z * HEAD)

time: 198 us -> 196 us (0.990)
  local copies, waits for them, and re-layouts: 11.2 us -> 18.7 us
  other arithmetic: 11.4 us -> 5.52 us
  starting transfers between devices: 54.6 us -> 50.8 us
    all_to_all x1, waiting for transfers between devices: 4.32 us -> 20.8 us  [shards(): part = lax.all_to_all(part, ('yh', 'yl'), 0, 0, tiled=True)]
    ppermute x4, waiting for transfers between devices: 21.9 us -> 13.5 us  [ring_z(): ups[p] = lax.ppermute(ups[p], 'z', forward)]
    all_gather x1, waiting for transfers between devices: 5.7 us -> 0.01 us  [shards(): w_out_half = lax.all_gather(w_out, 'z', axis=0, tiled=True)]
    ppermute x1, waiting for transfers between devices: 5.06 us -> 0.01 us  [shards(): got_yh = lax.ppermute(mine_yh, pair, [(0, 1), (1, 0), (2, 3), (3, 2)])]
    ppermute x3, waiting for transfers between devices: 0.01 us -> 4.11 us  [other_half_weights(): return lax.ppermute(array, ('yh', 'yl'), [(0, 3), (3, 0), (1, 2), (2, 1)])]
    unnamed x34 -> x40, local copies, waits for them, and re-layouts: 4.6 us -> 8.44 us
    another operation x1 -> x7, local copies, waits for them, and re-layouts: 0.01 us -> 3.64 us  [the longest x3 1.73 us: shards(): q = jnp.stack([a[:HEAD] for a in (mine, got_yh, got_core, got_both)], 0)]
    another operation x4 -> x3, other arithmetic: 2.32 us -> 0.07 us  [the longest x1 0.03 us: shards(): first = jnp.stack([mine[HEAD:], got_yh[HEAD:]], 0)]
  transfers between devices with their start and end apart: 26 -> 26, of which waited for: 12 -> 10; matrix products, arithmetic and copies ran while one was open for 9% -> 8% of each run, Pallas kernels for 17% -> 24%
where the time goes in v1:
time: 196 us; the launch traced here: 195 us
  waiting for transfers between devices  56 us (29%)
  starting transfers between devices  50.8 us (26%)
  Pallas kernels  47.5 us (24%)
  local copies, waits for them, and re-layouts  18.7 us (10%)
  between operations  14 us (7%)
  other arithmetic  5.52 us (3%)
  matrix products  2.04 us (1%)
    pallas_call x4, Pallas kernels, attend(): pl.pallas_call(functools.partial(attend_kernel, last), grid_spec=pltpu.Pr...  27.1 us
    all_to_all x1, waiting for transfers between devices, shards(): part = lax.all_to_all(part, ('yh', 'yl'), 0, 0, tiled=True)  20.8 us
    all_to_all x1, waiting for transfers between devices, shards(): attended = lax.all_to_all(attended, ('core', 'yh', 'z'), 0, 0, tiled=True)  13.6 us
    ppermute x4, waiting for transfers between devices, ring_z(): ups[p] = lax.ppermute(ups[p], 'z', forward)  13.5 us
    ppermute x3, starting transfers between devices, ring_z(): downs[p] = lax.ppermute(downs[p], 'z', backward)  10.4 us
    pallas_call x1, Pallas kernels, embed(): pl.pallas_call(embed_kernel, grid_spec=pltpu.PrefetchScalarGridSpec(num_s...  9.32 us
    unnamed x40, local copies, waits for them, and re-layouts  8.44 us
    ppermute x2, starting transfers between devices, column(): edge = lax.ppermute(edge, LON, pairs)  6.74 us
  transfers between devices with their start and end apart: 26, of which 10 were waited for; matrix products, arithmetic and copies ran while one was open for 8% of the time, Pallas kernels for 24%

profile of v1, /device:TPU:1, one launch (start us, length us, event | category | flops | bytes accessed | tf_op | source)
XLA Modules:
  0.0 194.7 jit_solution(11540970466997556320)
XLA Ops:
  6.6 2.2 %copy-done.1 = bf16[4,69,64,64]{1,3,2,0:T(8,128)(2,1)S(1)} copy-done((bf16[4,69,64,64]{1,3,2,0:T(8,128)(2,1)S(1)}, bf16[4,69,64,64]{1,3,2,0:T(8,128)(2,1)}, u32[]{:S(2)}) %copy-start.1) | copy-done | bytes 2261016
  10.2 4.5 %collective-permute-start = (bf16[4,64,69]{2,1,0:T(8,128)(2,1)S(1)}, bf16[4,64,69]{2,1,0:T(8,128)(2,1)S(1)}, u32[]{:S(2)}, u32[]{:S(2)}) collective-permute-start(bf16[4,64,69]{2,1,0:T(8,128)(2,1)S(1)} %get-tuple-element.24), channel_id=1, source_target_pairs={{0,32},{32,64},{64,96},{96,128},{128,160},{160,192},{192,224},{33,... | collective-permute-start | bytes 105992 | tf_op jit(solution)/shard_map/ppermute | solution.py:68
  16.0 1.6 collective-permute-start.11
  17.7 1.7 collective-permute-start.1
  19.4 5.0 %collective-permute-start.2 = (bf16[4,65,69]{2,1,0:T(8,128)(2,1)S(1)}, bf16[4,65,69]{2,1,0:T(8,128)(2,1)S(1)}, u32[]{:S(2)}, u32[]{:S(2)}) collective-permute-start(bf16[4,65,69]{2,1,0:T(8,128)(2,1)S(1)} %pad_maximum_fusion.4), channel_id=1, source_target_pairs={{2,0},{4,2},{6,4},{8,6},{10,8},{12,10},{14,12},{16,14},{18,16},{20... | collective-permute-start | bytes 107648 | tf_op jit(solution)/shard_map/ppermute | solution.py:72
  24.6 1.6 collective-permute-done.1
  26.5 9.3 %shard_map.128 = bf16[256,1024]{1,0:T(8,128)(2,1)} custom-call(s32[4]{0:T(128)S(1)} %pad_add_fusion.s_ref.ids_ref, bf16[4,8,8,64,69]{4,3,2,1,0:T(8,128)(2,1)} %bitcast.70, bf16[4,64,69]{2,1,0:T(8,128)(2,1)S(1)} %collective-permute-done.row_ref, f32[5,32,69]{2,1,0:T(8,128)S(1)} %bitcast.82, f32[5,32,69]{2,1,0:T(8,128)S(1)} %bitcast.81, ...), custom_call_target="tpu_custom_call" | custom-call | flops 8000000000 | bytes 12582912 | tf_op jit(solution)/shard_map/pallas_call | solution.py:129
  35.8 3.7 %all-to-all-start = ((bf16[4,64,1024]{2,1,0:T(8,128)(2,1)}), bf16[4,64,1024]{2,1,0:T(8,128)(2,1)S(1)}, u32[]{:S(2)}, u32[]{:S(2)}) async-start(bf16[4,64,1024]{2,1,0:T(8,128)(2,1)} %bitcast.12), calls=%async_computation | async-start | bytes 1048576 | tf_op jit(solution)/shard_map/all_to_all | solution.py:376
  39.9 20.8 %all-to-all-done = bf16[4,64,1024]{2,1,0:T(8,128)(2,1)S(1)} async-done(((bf16[4,64,1024]{2,1,0:T(8,128)(2,1)}), bf16[4,64,1024]{2,1,0:T(8,128)(2,1)S(1)}, u32[]{:S(2)}, u32[]{:S(2)}) %all-to-all-start) | async-done | bytes 524320 | tf_op jit(solution)/shard_map/all_to_all | solution.py:376
  61.9 5.0 %collective-permute-start.4 = (bf16[8,2,8,1024]{3,2,1,0:T(8,128)(2,1)S(1)}, bf16[8,2,8,1024]{3,2,1,0:T(8,128)(2,1)}, u32[]{:S(2)}, u32[]{:S(2)}) collective-permute-start(bf16[8,2,8,1024]{3,2,1,0:T(8,128)(2,1)S(1)} %get-tuple-element.44), channel_id=1, source_target_pairs={{2,0},{4,2},{6,4},{8,6},{10,8},{12,10},{14,12},{0,14},{3,1},{5,3},... | collective-permute-start | bytes 786440 | tf_op jit(solution)/shard_map/ppermute | solution.py:252
  67.6 2.4 %collective-permute-start.7 = (bf16[208,1024]{1,0:T(8,128)(2,1)}, bf16[208,1024]{1,0:T(8,128)(2,1)}, u32[]{:S(2)}, u32[]{:S(2)}) collective-permute-start(bf16[208,1024]{1,0:T(8,128)(2,1)} %fusion.7), channel_id=1, source_target_pairs={{0,17},{17,0},{1,16},{16,1},{2,19},{19,2},{3,18},{18,3},{4,21},{21... | collective-permute-start | bytes 1277960 | tf_op jit(solution)/shard_map/ppermute | solution.py:22
  70.1 3.6 %collective-permute-done.3 = bf16[8,2,8,1024]{3,2,1,0:T(8,128)(2,1)} collective-permute-done((bf16[8,2,8,1024]{3,2,1,0:T(8,128)(2,1)S(1)}, bf16[8,2,8,1024]{3,2,1,0:T(8,128)(2,1)}, u32[]{:S(2)}, u32[]{:S(2)}) %collective-permute-start.3) | collective-permute-done | bytes 262176 | tf_op jit(solution)/shard_map/ppermute | solution.py:250
  73.6 2.7 %collective-permute-start.6 = (bf16[8,2,8,1024]{3,2,1,0:T(8,128)(2,1)}, bf16[8,2,8,1024]{3,2,1,0:T(8,128)(2,1)}, u32[]{:S(2)}, u32[]{:S(2)}) collective-permute-start(bf16[8,2,8,1024]{3,2,1,0:T(8,128)(2,1)} %collective-permute-done.4), channel_id=1, source_target_pairs={{2,0},{4,2},{6,4},{8,6},{10,8},{12,10},{14,12},{0,14},{3,1},{5,3},... | collective-permute-start | bytes 786440 | tf_op jit(solution)/shard_map/ppermute | solution.py:252
  76.3 4.1 %collective-permute-done.7.other_ref = bf16[208,1024]{1,0:T(8,128)(2,1)} collective-permute-done((bf16[208,1024]{1,0:T(8,128)(2,1)}, bf16[208,1024]{1,0:T(8,128)(2,1)}, u32[]{:S(2)}, u32[]{:S(2)}) %collective-permute-start.7) | collective-permute-done | bytes 426016 | tf_op jit(solution)/shard_map/ppermute | solution.py:22
  80.4 2.1 %collective-permute-done.5 = bf16[8,2,8,1024]{3,2,1,0:T(8,128)(2,1)} collective-permute-done((bf16[8,2,8,1024]{3,2,1,0:T(8,128)(2,1)}, bf16[8,2,8,1024]{3,2,1,0:T(8,128)(2,1)}, u32[]{:S(2)}, u32[]{:S(2)}) %collective-permute-start.5) | collective-permute-done | bytes 262176 | tf_op jit(solution)/shard_map/ppermute | solution.py:250
  84.5 2.8 %collective-permute-start.9 = (bf16[8,2,8,1024]{3,2,1,0:T(8,128)(2,1)}, bf16[8,2,8,1024]{3,2,1,0:T(8,128)(2,1)S(1)}, u32[]{:S(2)}, u32[]{:S(2)}) collective-permute-start(bf16[8,2,8,1024]{3,2,1,0:T(8,128)(2,1)} %collective-permute-done.6), channel_id=1, source_target_pairs={{2,0},{4,2},{6,4},{8,6},{10,8},{12,10},{14,12},{0,14},{3,1},{5,3},... | collective-permute-start | bytes 786440 | tf_op jit(solution)/shard_map/ppermute | solution.py:252
  88.2 2.2 %collective-permute-done.8 = bf16[8,2,8,1024]{3,2,1,0:T(8,128)(2,1)S(1)} collective-permute-done((bf16[8,2,8,1024]{3,2,1,0:T(8,128)(2,1)}, bf16[8,2,8,1024]{3,2,1,0:T(8,128)(2,1)S(1)}, u32[]{:S(2)}, u32[]{:S(2)}) %collective-permute-start.8) | collective-permute-done | bytes 262176 | tf_op jit(solution)/shard_map/ppermute | solution.py:250
  91.6 5.6 %collective-permute-done.10 = bf16[8,2,8,1024]{3,2,1,0:T(8,128)(2,1)S(1)} collective-permute-done((bf16[8,2,8,1024]{3,2,1,0:T(8,128)(2,1)S(1)}, bf16[8,2,8,1024]{3,2,1,0:T(8,128)(2,1)S(1)}, u32[]{:S(2)}, u32[]{:S(2)}) %collective-permute-start.10) | collective-permute-done | bytes 262176 | tf_op jit(solution)/shard_map/ppermute | solution.py:250
  100.8 3.8 %shard_map.129 = (bf16[192,512]{1,0:T(8,128)(2,1)S(1)}, bf16[192,512]{1,0:T(8,128)(2,1)}, bf16[192,512]{1,0:T(8,128)(2,1)}, bf16[192,512]{1,0:T(8,128)(2,1)}) custom-call(s32[4]{0:T(128)S(1)} %pad_add_fusion.s_ref.ids_ref, bf16[8,2,64,1024]{3,2,1,0:T(8,128)(2,1)S(1)} %constant_dynamic-update-slice_fusion.x_ref, bf16[192,1024]{1,0:T(8,128)(2,1)S(1)} %bitcast.80, ...), custom_call_target="tpu_custom_call" | custom-call | flops 3000000000 | bytes 4194304 | tf_op jit(solution)/shard_map/pallas_call | solution.py:286
  105.3 3.2 %collective-permute-start.12 = (bf16[192,512]{1,0:T(8,128)(2,1)}, bf16[192,512]{1,0:T(8,128)(2,1)}, u32[]{:S(2)}, u32[]{:S(2)}) collective-permute-start(bf16[192,512]{1,0:T(8,128)(2,1)} %get-tuple-element.31), channel_id=1, source_target_pairs={{0,32},{32,0},{16,48},{48,16},{1,33},{33,1},{17,49},{49,17},{2,34}... | collective-permute-start | bytes 589832 | tf_op jit(solution)/shard_map/ppermute | solution.py:402
  108.4 1.7 collective-permute-start.13
  111.6 5.9 %shard_map.130 = bf16[8,2,64,1024]{3,2,1,0:T(8,128)(2,1)S(1)} custom-call(s32[4]{0:T(128)S(1)} %pad_add_fusion.s_ref.ids_ref, bf16[8,2,64,1024]{3,2,1,0:T(8,128)(2,1)S(1)} %constant_dynamic-update-slice_fusion.x_ref, bf16[8,2,8,1024]{3,2,1,0:T(8,128)(2,1)S(1)} %get-tuple-element.54.tok_ref, bf16[2,256,1024]{2,1,0:T(8,128)(2,1)S(1)} %copy-done.3, ...), custom_call_target="tpu_custom_call" | custom-call | flops 6000000000 | bytes 8388608 | tf_op jit(solution)/shard_map/pallas_call | solution.py:322
  118.8 2.3 %collective-permute-done.14 = bf16[192,512]{1,0:T(8,128)(2,1)} collective-permute-done((bf16[192,512]{1,0:T(8,128)(2,1)}, bf16[192,512]{1,0:T(8,128)(2,1)}, u32[]{:S(2)}, u32[]{:S(2)}) %collective-permute-start.14) | collective-permute-done | bytes 196640 | tf_op jit(solution)/shard_map/ppermute | solution.py:404
  123.1 1.8 collective-permute-start.20
  129.5 6.4 %shard_map.131.refs_0_ = f32[2048,128]{1,0:T(8,128)S(1)} custom-call(s32[4]{0:T(128)S(1)} %pad_add_fusion.s_ref.ids_ref, bf16[2048,64]{1,0:T(8,128)(2,1)S(1)} %bitcast.75, bf16[2,128,512]{2,1,0:T(8,128)(2,1)S(1)} %pad_maximum_fusion.1.kv_ref, bf16[2,128,512]{2,1,0:T(8,128)(2,1)S(1)} %pad_maximum_fusion.2.kv2_ref), custom_call_target="tpu_custom_call" | custom-call | flops 3221225472 | bytes 4194304 | tf_op jit(solution)/shard_map/pallas_call | solution.py:215
  136.1 2.9 %collective-permute-start.18 = (bf16[2,128,512]{2,1,0:T(8,128)(2,1)S(1)}, bf16[2,128,512]{2,1,0:T(8,128)(2,1)S(1)}, u32[]{:S(2)}, u32[]{:S(2)}) collective-permute-start(bf16[2,128,512]{2,1,0:T(8,128)(2,1)S(1)} %collective-permute-done.17.kv2_ref), channel_id=1, source_target_pairs={{64,0},{128,64},{192,128},{0,192},{65,1},{129,65},{193,129},{1,193... | collective-permute-start | bytes 786440 | tf_op jit(solution)/shard_map/ppermute | solution.py:420
  139.0 6.5 %shard_map.132.refs_0_ = f32[2048,128]{1,0:T(8,128)S(1)} custom-call(s32[4]{0:T(128)S(1)} %pad_add_fusion.s_ref.ids_ref, bf16[2048,64]{1,0:T(8,128)(2,1)S(1)} %bitcast.76, bf16[2,128,512]{2,1,0:T(8,128)(2,1)S(1)} %collective-permute-done.15.kv_ref, bf16[2,128,512]{2,1,0:T(8,128)(2,1)S(1)} %collective-permute-done.17.kv2_ref, f32[2048,128]{1,0:T(8,128)S(1)} %shard_map.131.refs_0_), custom_call_target="tpu_custom_call" | custom-call | flops 3221225472 | bytes 4194304 | tf_op jit(solution)/shard_map/pallas_call | solution.py:215
  145.5 6.5 %shard_map.133.refs_0_ = f32[2048,128]{1,0:T(8,128)S(1)} custom-call(s32[4]{0:T(128)S(1)} %pad_add_fusion.s_ref.ids_ref, bf16[2048,64]{1,0:T(8,128)(2,1)S(1)} %bitcast.77, bf16[2,128,512]{2,1,0:T(8,128)(2,1)S(1)} %collective-permute-done.19.kv_ref, bf16[2,128,512]{2,1,0:T(8,128)(2,1)S(1)} %collective-permute-done.20.kv2_ref, f32[2048,128]{1,0:T(8,128)S(1)} %shard_map.132.refs_0_), custom_call_target="tpu_custom_call" | custom-call | flops 3221225472 | bytes 4194304 | tf_op jit(solution)/shard_map/pallas_call | solution.py:215
  155.7 7.7 %shard_map.134 = bf16[32,32,128]{2,1,0:T(8,128)(2,1)} custom-call(s32[4]{0:T(128)S(1)} %pad_add_fusion.s_ref.ids_ref, bf16[2048,64]{1,0:T(8,128)(2,1)S(1)} %bitcast.78, bf16[2,128,512]{2,1,0:T(8,128)(2,1)S(1)} %collective-permute-done.16.kv_ref, bf16[2,128,512]{2,1,0:T(8,128)(2,1)S(1)} %collective-permute-done.18.kv2_ref, f32[2048,128]{1,0:T(8,128)S(1)} %copy-done.13), custom_call_target="tpu_custom_call" | custom-call | flops 3221225472 | bytes 4194304 | tf_op jit(solution)/shard_map/pallas_call | solution.py:215
  163.4 6.3 %all-to-all-start.1 = ((bf16[32,32,128]{2,1,0:T(8,128)(2,1)}), bf16[32,32,128]{2,1,0:T(8,128)(2,1)S(1)}, u32[]{:S(2)}, u32[]{:S(2)}) async-start(bf16[32,32,128]{2,1,0:T(8,128)(2,1)} %shard_map.134), calls=%async_computation.2 | async-start | bytes 524288 | tf_op jit(solution)/shard_map/all_to_all | solution.py:428
  169.7 13.6 %all-to-all-done.1 = bf16[32,32,128]{2,1,0:T(8,128)(2,1)S(1)} async-done(((bf16[32,32,128]{2,1,0:T(8,128)(2,1)}), bf16[32,32,128]{2,1,0:T(8,128)(2,1)S(1)}, u32[]{:S(2)}, u32[]{:S(2)}) %all-to-all-start.1) | async-done | bytes 262176 | tf_op jit(solution)/shard_map/all_to_all | solution.py:428
  186.1 1.7 fusion.4
  (132 shorter events, 29.6 us)
Async XLA Ops:
  6.5 33.2 %copy-start = (bf16[50,1024]{1,0:T(8,128)(2,1)S(1)}, bf16[50,1024]{1,0:T(8,128)(2,1)}, u32[]{:S(2)}) copy-start(bf16[50,1024]{1,0:T(8,128)(2,1)} %param.18) | copy-start | bytes 307204
  10.2 7.5 %collective-permute-start = (bf16[4,64,69]{2,1,0:T(8,128)(2,1)S(1)}, bf16[4,64,69]{2,1,0:T(8,128)(2,1)S(1)}, u32[]{:S(2)}, u32[]{:S(2)}) collective-permute-start(bf16[4,64,69]{2,1,0:T(8,128)(2,1)S(1)} %get-tuple-element.24), channel_id=1, source_target_pairs={{0,32},{32,64},{64,96},{96,128},{128,160},{160,192},{192,224},{33,... | collective-permute-start | bytes 105992 | tf_op jit(solution)/shard_map/ppermute | solution.py:68
  16.0 81.2 %collective-permute-start.11 = (bf16[768,1024]{1,0:T(8,128)(2,1)}, bf16[768,1024]{1,0:T(8,128)(2,1)}, u32[]{:S(2)}, u32[]{:S(2)}) collective-permute-start(bf16[768,1024]{1,0:T(8,128)(2,1)} %pad_maximum_fusion), channel_id=1, source_target_pairs={{0,17},{17,0},{1,16},{16,1},{2,19},{19,2},{3,18},{18,3},{4,21},{21... | collective-permute-start | bytes 4718600 | tf_op jit(solution)/shard_map/ppermute | solution.py:22
  17.7 8.5 %collective-permute-start.1 = (bf16[4,65,69]{2,1,0:T(8,128)(2,1)S(1)}, bf16[4,65,69]{2,1,0:T(8,128)(2,1)S(1)}, u32[]{:S(2)}, u32[]{:S(2)}) collective-permute-start(bf16[4,65,69]{2,1,0:T(8,128)(2,1)S(1)} %pad_maximum_fusion.3), channel_id=1, source_target_pairs={{0,2},{2,4},{4,6},{6,8},{8,10},{10,12},{12,14},{14,16},{16,18},{18... | collective-permute-start | bytes 107648 | tf_op jit(solution)/shard_map/ppermute | solution.py:72
  19.4 6.7 %collective-permute-start.2 = (bf16[4,65,69]{2,1,0:T(8,128)(2,1)S(1)}, bf16[4,65,69]{2,1,0:T(8,128)(2,1)S(1)}, u32[]{:S(2)}, u32[]{:S(2)}) collective-permute-start(bf16[4,65,69]{2,1,0:T(8,128)(2,1)S(1)} %pad_maximum_fusion.4), channel_id=1, source_target_pairs={{2,0},{4,2},{6,4},{8,6},{10,8},{12,10},{14,12},{16,14},{18,16},{20... | collective-permute-start | bytes 107648 | tf_op jit(solution)/shard_map/ppermute | solution.py:72
  26.5 13.0 %copy-start.17 = (f32[1,64]{1,0:T(1,128)S(1)}, f32[1,64]{1,0:T(1,128)}, u32[]{:S(2)}) copy-start(f32[1,64]{1,0:T(1,128)} %param.22) | copy-start | bytes 772
  26.5 13.0 %copy-start.18 = (f32[1,64]{1,0:T(1,128)S(1)}, f32[1,64]{1,0:T(1,128)}, u32[]{:S(2)}) copy-start(f32[1,64]{1,0:T(1,128)} %param.21) | copy-start | bytes 772
  26.5 13.1 %copy-start.16 = (bf16[1024]{0:T(1024)(128)(2,1)S(1)}, bf16[1024]{0:T(1024)(128)(2,1)}, u32[]{:S(2)}) copy-start(bf16[1024]{0:T(1024)(128)(2,1)} %param.15) | copy-start | bytes 6148
  26.5 13.2 %copy-start.19 = (s32[2]{0:T(128)S(1)}, s32[2]{0:T(128)}, u32[]{:S(2)}) copy-start(s32[2]{0:T(128)} %param.17) | copy-start | bytes 28
  35.8 24.8 %all-to-all-start = ((bf16[4,64,1024]{2,1,0:T(8,128)(2,1)}), bf16[4,64,1024]{2,1,0:T(8,128)(2,1)S(1)}, u32[]{:S(2)}, u32[]{:S(2)}) async-start(bf16[4,64,1024]{2,1,0:T(8,128)(2,1)} %bitcast.12), calls=%async_computation | async-start | bytes 1048576 | tf_op jit(solution)/shard_map/all_to_all | solution.py:376
  39.5 113.5 %all-gather.2.cloned.1.call-start = ((), (), s32[]{:S(2)}) async-start(), calls=%async_computation.4 | async-start | bytes 1179648 | tf_op jit(solution)/shard_map/all_gather | solution.py:396
  61.8 11.8 %collective-permute-start.3 = (bf16[8,2,8,1024]{3,2,1,0:T(8,128)(2,1)S(1)}, bf16[8,2,8,1024]{3,2,1,0:T(8,128)(2,1)}, u32[]{:S(2)}, u32[]{:S(2)}) collective-permute-start(bf16[8,2,8,1024]{3,2,1,0:T(8,128)(2,1)S(1)} %get-tuple-element.44), channel_id=1, source_target_pairs={{0,2},{2,4},{4,6},{6,8},{8,10},{10,12},{12,14},{14,0},{1,3},{3,5},... | collective-permute-start | bytes 786440 | tf_op jit(solution)/shard_map/ppermute | solution.py:250
  61.9 11.8 %collective-permute-start.4 = (bf16[8,2,8,1024]{3,2,1,0:T(8,128)(2,1)S(1)}, bf16[8,2,8,1024]{3,2,1,0:T(8,128)(2,1)}, u32[]{:S(2)}, u32[]{:S(2)}) collective-permute-start(bf16[8,2,8,1024]{3,2,1,0:T(8,128)(2,1)S(1)} %get-tuple-element.44), channel_id=1, source_target_pairs={{2,0},{4,2},{6,4},{8,6},{10,8},{12,10},{14,12},{0,14},{3,1},{5,3},... | collective-permute-start | bytes 786440 | tf_op jit(solution)/shard_map/ppermute | solution.py:252
  67.6 12.8 %collective-permute-start.7 = (bf16[208,1024]{1,0:T(8,128)(2,1)}, bf16[208,1024]{1,0:T(8,128)(2,1)}, u32[]{:S(2)}, u32[]{:S(2)}) collective-permute-start(bf16[208,1024]{1,0:T(8,128)(2,1)} %fusion.7), channel_id=1, source_target_pairs={{0,17},{17,0},{1,16},{16,1},{2,19},{19,2},{3,18},{18,3},{4,21},{21... | collective-permute-start | bytes 1277960 | tf_op jit(solution)/shard_map/ppermute | solution.py:22
  73.6 8.9 %collective-permute-start.5 = (bf16[8,2,8,1024]{3,2,1,0:T(8,128)(2,1)}, bf16[8,2,8,1024]{3,2,1,0:T(8,128)(2,1)}, u32[]{:S(2)}, u32[]{:S(2)}) collective-permute-start(bf16[8,2,8,1024]{3,2,1,0:T(8,128)(2,1)} %collective-permute-done.3), channel_id=1, source_target_pairs={{0,2},{2,4},{4,6},{6,8},{8,10},{10,12},{12,14},{14,0},{1,3},{3,5},... | collective-permute-start | bytes 786440 | tf_op jit(solution)/shard_map/ppermute | solution.py:250
  73.6 8.9 %collective-permute-start.6 = (bf16[8,2,8,1024]{3,2,1,0:T(8,128)(2,1)}, bf16[8,2,8,1024]{3,2,1,0:T(8,128)(2,1)}, u32[]{:S(2)}, u32[]{:S(2)}) collective-permute-start(bf16[8,2,8,1024]{3,2,1,0:T(8,128)(2,1)} %collective-permute-done.4), channel_id=1, source_target_pairs={{2,0},{4,2},{6,4},{8,6},{10,8},{12,10},{14,12},{0,14},{3,1},{5,3},... | collective-permute-start | bytes 786440 | tf_op jit(solution)/shard_map/ppermute | solution.py:252
  82.5 7.9 %collective-permute-start.8 = (bf16[8,2,8,1024]{3,2,1,0:T(8,128)(2,1)}, bf16[8,2,8,1024]{3,2,1,0:T(8,128)(2,1)S(1)}, u32[]{:S(2)}, u32[]{:S(2)}) collective-permute-start(bf16[8,2,8,1024]{3,2,1,0:T(8,128)(2,1)} %collective-permute-done.5), channel_id=1, source_target_pairs={{0,2},{2,4},{4,6},{6,8},{8,10},{10,12},{12,14},{14,0},{1,3},{3,5},... | collective-permute-start | bytes 786440 | tf_op jit(solution)/shard_map/ppermute | solution.py:250
  84.5 7.1 %collective-permute-start.9 = (bf16[8,2,8,1024]{3,2,1,0:T(8,128)(2,1)}, bf16[8,2,8,1024]{3,2,1,0:T(8,128)(2,1)S(1)}, u32[]{:S(2)}, u32[]{:S(2)}) collective-permute-start(bf16[8,2,8,1024]{3,2,1,0:T(8,128)(2,1)} %collective-permute-done.6), channel_id=1, source_target_pairs={{2,0},{4,2},{6,4},{8,6},{10,8},{12,10},{14,12},{0,14},{3,1},{5,3},... | collective-permute-start | bytes 786440 | tf_op jit(solution)/shard_map/ppermute | solution.py:252
  90.4 6.8 %collective-permute-start.10 = (bf16[8,2,8,1024]{3,2,1,0:T(8,128)(2,1)S(1)}, bf16[8,2,8,1024]{3,2,1,0:T(8,128)(2,1)S(1)}, u32[]{:S(2)}, u32[]{:S(2)}) collective-permute-start(bf16[8,2,8,1024]{3,2,1,0:T(8,128)(2,1)S(1)} %collective-permute-done.8), channel_id=1, source_target_pairs={{0,2},{2,4},{4,6},{6,8},{8,10},{10,12},{12,14},{14,0},{1,3},{3,5},... | collective-permute-start | bytes 786440 | tf_op jit(solution)/shard_map/ppermute | solution.py:250
  97.2 88.9 %reduce-scatter.2.cloned.1.call-start = ((), (), s32[]{:S(2)}) async-start(), calls=%async_computation.3 | async-start | bytes 2359296 | tf_op jit(solution)/shard_map/reduce_scatter | solution.py:410
  105.3 13.6 %collective-permute-start.12 = (bf16[192,512]{1,0:T(8,128)(2,1)}, bf16[192,512]{1,0:T(8,128)(2,1)}, u32[]{:S(2)}, u32[]{:S(2)}) collective-permute-start(bf16[192,512]{1,0:T(8,128)(2,1)} %get-tuple-element.31), channel_id=1, source_target_pairs={{0,32},{32,0},{16,48},{48,16},{1,33},{33,1},{17,49},{49,17},{2,34}... | collective-permute-start | bytes 589832 | tf_op jit(solution)/shard_map/ppermute | solution.py:402
  108.4 10.4 %collective-permute-start.13 = (bf16[192,512]{1,0:T(8,128)(2,1)}, bf16[192,512]{1,0:T(8,128)(2,1)}, u32[]{:S(2)}, u32[]{:S(2)}) collective-permute-start(bf16[192,512]{1,0:T(8,128)(2,1)} %get-tuple-element.32), channel_id=1, source_target_pairs={{0,16},{16,0},{32,48},{48,32},{1,17},{17,1},{33,49},{49,33},{2,18}... | collective-permute-start | bytes 589832 | tf_op jit(solution)/shard_map/ppermute | solution.py:403
  110.1 11.0 %collective-permute-start.14 = (bf16[192,512]{1,0:T(8,128)(2,1)}, bf16[192,512]{1,0:T(8,128)(2,1)}, u32[]{:S(2)}, u32[]{:S(2)}) collective-permute-start(bf16[192,512]{1,0:T(8,128)(2,1)} %get-tuple-element.33), channel_id=1, source_target_pairs={{0,48},{48,0},{16,32},{32,16},{1,49},{49,1},{17,33},{33,17},{2,50}... | collective-permute-start | bytes 589832 | tf_op jit(solution)/shard_map/ppermute | solution.py:404
  122.1 13.8 %collective-permute-start.15 = (bf16[2,128,512]{2,1,0:T(8,128)(2,1)S(1)}, bf16[2,128,512]{2,1,0:T(8,128)(2,1)S(1)}, u32[]{:S(2)}, u32[]{:S(2)}) collective-permute-start(bf16[2,128,512]{2,1,0:T(8,128)(2,1)S(1)} %pad_maximum_fusion.1.kv_ref), channel_id=1, source_target_pairs={{0,64},{64,128},{128,192},{192,0},{1,65},{65,129},{129,193},{193,1... | collective-permute-start | bytes 786440 | tf_op jit(solution)/shard_map/ppermute | solution.py:418
  123.1 22.4 %collective-permute-start.20 = (bf16[2,128,512]{2,1,0:T(8,128)(2,1)S(1)}, bf16[2,128,512]{2,1,0:T(8,128)(2,1)S(1)}, u32[]{:S(2)}, u32[]{:S(2)}) collective-permute-start(bf16[2,128,512]{2,1,0:T(8,128)(2,1)S(1)} %pad_maximum_fusion.1.kv_ref), channel_id=1, source_target_pairs={{64,0},{128,64},{192,128},{0,192},{65,1},{129,65},{193,129},{1,193... | collective-permute-start | bytes 786440 | tf_op jit(solution)/shard_map/ppermute | solution.py:419
  125.9 10.2 %collective-permute-start.17 = (bf16[2,128,512]{2,1,0:T(8,128)(2,1)S(1)}, bf16[2,128,512]{2,1,0:T(8,128)(2,1)S(1)}, u32[]{:S(2)}, u32[]{:S(2)}) collective-permute-start(bf16[2,128,512]{2,1,0:T(8,128)(2,1)S(1)} %pad_maximum_fusion.2.kv2_ref), channel_id=1, source_target_pairs={{64,0},{128,64},{192,128},{0,192},{65,1},{129,65},{193,129},{1,193... | collective-permute-start | bytes 786440 | tf_op jit(solution)/shard_map/ppermute | solution.py:418
  126.0 19.5 %collective-permute-start.19 = (bf16[2,128,512]{2,1,0:T(8,128)(2,1)S(1)}, bf16[2,128,512]{2,1,0:T(8,128)(2,1)S(1)}, u32[]{:S(2)}, u32[]{:S(2)}) collective-permute-start(bf16[2,128,512]{2,1,0:T(8,128)(2,1)S(1)} %pad_maximum_fusion.2.kv2_ref), channel_id=1, source_target_pairs={{0,64},{64,128},{128,192},{192,0},{1,65},{65,129},{129,193},{193,1... | collective-permute-start | bytes 786440 | tf_op jit(solution)/shard_map/ppermute | solution.py:419
  136.0 18.5 %collective-permute-start.16 = (bf16[2,128,512]{2,1,0:T(8,128)(2,1)S(1)}, bf16[2,128,512]{2,1,0:T(8,128)(2,1)S(1)}, u32[]{:S(2)}, u32[]{:S(2)}) collective-permute-start(bf16[2,128,512]{2,1,0:T(8,128)(2,1)S(1)} %collective-permute-done.15.kv_ref), channel_id=1, source_target_pairs={{0,64},{64,128},{128,192},{192,0},{1,65},{65,129},{129,193},{193,1... | collective-permute-start | bytes 786440 | tf_op jit(solution)/shard_map/ppermute | solution.py:420
  136.1 18.4 %collective-permute-start.18 = (bf16[2,128,512]{2,1,0:T(8,128)(2,1)S(1)}, bf16[2,128,512]{2,1,0:T(8,128)(2,1)S(1)}, u32[]{:S(2)}, u32[]{:S(2)}) collective-permute-start(bf16[2,128,512]{2,1,0:T(8,128)(2,1)S(1)} %collective-permute-done.17.kv2_ref), channel_id=1, source_target_pairs={{64,0},{128,64},{192,128},{0,192},{65,1},{129,65},{193,129},{1,193... | collective-permute-start | bytes 786440 | tf_op jit(solution)/shard_map/ppermute | solution.py:420
  153.0 31.2 %collective-permute-start.21 = (bf16[512,1024]{1,0:T(8,128)(2,1)}, bf16[512,1024]{1,0:T(8,128)(2,1)}, u32[]{:S(2)}, u32[]{:S(2)}) collective-permute-start(bf16[512,1024]{1,0:T(8,128)(2,1)} %all-gather.2.cloned.1.call-done), channel_id=1, source_target_pairs={{0,17},{17,0},{1,16},{16,1},{2,19},{19,2},{3,18},{18,3},{4,21},{21... | collective-permute-start | bytes 3145736 | tf_op jit(solution)/shard_map/ppermute | solution.py:22
  163.4 19.9 %all-to-all-start.1 = ((bf16[32,32,128]{2,1,0:T(8,128)(2,1)}), bf16[32,32,128]{2,1,0:T(8,128)(2,1)S(1)}, u32[]{:S(2)}, u32[]{:S(2)}) async-start(bf16[32,32,128]{2,1,0:T(8,128)(2,1)} %shard_map.134), calls=%async_computation.2 | async-start | bytes 524288 | tf_op jit(solution)/shard_map/all_to_all | solution.py:428
  169.7 16.1 %copy-start.14 = (bf16[512,1024]{1,0:T(8,128)(2,1)S(1)}, bf16[512,1024]{1,0:T(8,128)(2,1)}, u32[]{:S(2)}) copy-start(bf16[512,1024]{1,0:T(8,128)(2,1)} %all-gather.2.cloned.1.call-done) | copy-start | bytes 3145732
  (14 other events, 51.5 us)
Sparse Core Ops, SparseCore 0:
  97.4 32.8 all-gather.1
  132.8 40.6 reduce-scatter.1

commit v2 on v1

--- a/solution.py
+++ b/solution.py
@@ -177,8 +177,8 @@
             for b in range(0, nk, bk):
                 scores = jnp.dot(q, ref[c, :HEAD, b : b + bk], preferred_element_type=jnp.float32)
                 weights = jnp.exp2(scores).astype(jnp.bfloat16)
-                at = pl.multiple_of((n * blocks + c) * nk + b, bk)
-                values = v1[pl.ds(at, bk), :]
+                at = (n * blocks + c) * nk + b
+                values = v1[at : at + bk, :]
                 acc = acc + jnp.dot(weights, values, preferred_element_type=jnp.float32)
         return acc
 
@@ -186,7 +186,8 @@
         acc = acc_refs[0][...]
     else:
         acc = jnp.zeros((bq, 2 * HEAD), jnp.float32)
-    acc = lax.fori_loop(0, blocks, body, acc)
+    for c in range(blocks):
+        acc = body(c, acc)
     if last:
         halves = (acc / pltpu.roll(acc, HEAD, 1)).reshape(bq // 64, 2, 32, 2 * HEAD)
         left, right = halves[:, 0], halves[:, 1]
@@ -297,12 +298,15 @@
     )(ids, x, own, other, gains)
 
 
-def mlp_kernel(ids_ref, x_ref, tok_ref, gu_ref, down_ref, other_ref, o_ref, acc):
+def mlp_kernel(ids_ref, x_ref, tok_ref, gu_ref, down_ref, some_ref, rest_ref, o_ref, acc):
     rows, members, cols, width = x_ref.shape
-    units = down_ref.shape[0]
+    units = down_ref.shape[0] // 2
     x = x_ref[...].reshape(-1, width)
     contract = (((1,), (1,)), ((), ()))
-    other = [other_ref[n * units : (n + 1) * units] for n in range(3)]
+    other = []
+    for n in range(3):
+        rows_n = slice(n * units, (n + 1) * units)
+        other.append(jnp.concatenate([some_ref[rows_n], rest_ref[rows_n]], 0))
     total = None
     for gate_w, up_w, down_w in ((gu_ref[0], gu_ref[1], down_ref[...]), other):
         gate = lax.dot_general(x, gate_w, contract, preferred_element_type=jnp.float32)
@@ -316,7 +320,7 @@
     o_ref[...] = acc[...].astype(jnp.bfloat16)
 
 
-def mlp(x, tokens, gu, down, other, ids, rows=4):
+def mlp(x, tokens, gu, down, some, rest, ids, rows=4):
     whole = lambda a: pl.BlockSpec(a.shape, lambda i, s: (0,) * a.ndim)
     block = lambda a: pl.BlockSpec((rows,) + a.shape[1:], lambda i, s: (i, 0, 0, 0))
     return pl.pallas_call(
@@ -324,14 +328,14 @@
         grid_spec=pltpu.PrefetchScalarGridSpec(
             num_scalar_prefetch=1,
             grid=(x.shape[0] // rows,),
-            in_specs=[block(x), block(tokens)] + [whole(a) for a in (gu, down, other)],
+            in_specs=[block(x), block(tokens)] + [whole(a) for a in (gu, down, some, rest)],
             out_specs=block(x),
             scratch_shapes=[pltpu.VMEM((rows,) + x.shape[1:], jnp.float32)],
         ),
         out_shape=jax.ShapeDtypeStruct(x.shape, jnp.bfloat16),
         compiler_params=pltpu.CompilerParams(vmem_limit_bytes=32 * 2**20),
         cost_estimate=pl.CostEstimate(flops=6 * 10**9, bytes_accessed=8 * 2**20, transcendentals=0),
-    )(ids, x, tokens, gu, down, other)
+    )(ids, x, tokens, gu, down, some, rest)
 
 
 def shards(
@@ -361,19 +365,25 @@
     fine = gains - coarse - middle
     terms = jnp.stack([coarse, middle, fine], 0).astype(bf16).reshape(1, 6 * HEAD)
     terms = jnp.pad(terms, ((0, 15), (0, width - 6 * HEAD)))
+    ids = jnp.stack([yl, core, lax.axis_index("z"), yh]).astype(jnp.int32)
+
+    f = jnp.transpose(fields, (0, 2, 3, 1))
+    row, low, high = halo(f, ids, yl)
+    part = embed(f, row, low, high, embed_weight, pos_embed, ids)
+    part = lax.all_to_all(part, ("yh", "yl"), 0, 0, tiled=True)
+    part, terms, w_qkv, w_gate_up, w_down = lax.optimization_barrier(
+        (part, terms, w_qkv, w_gate_up, w_down)
+    )
     qkv_other = other_half_weights(jnp.concatenate([w_qkv.reshape(-1, width), terms], 0))
+    units = w_down.shape[0] // 2
+    some_gu = lax.dynamic_slice_in_dim(w_gate_up, core * units, units, 1)
+    some_down = lax.dynamic_slice_in_dim(w_down, core * units, units, 0)
     mlp_other = other_half_weights(
-        jnp.concatenate([w_gate_up.reshape(-1, width), w_down], 0)
+        jnp.concatenate([some_gu.reshape(-1, width), some_down], 0)
     )
     terms = qkv_other[-16:, : 6 * HEAD][0].astype(f32).reshape(3, 2, HEAD)
     gains_other = terms[0] + terms[1] + terms[2]
     gain_both = jnp.stack([gains, gains_other], 0)[..., None]
-    ids = jnp.stack([yl, core, lax.axis_index("z"), yh]).astype(jnp.int32)
-
-    f = jnp.transpose(fields, (0, 2, 3, 1))
-    row, low, high = halo(f, ids, yl)
-    part = embed(f, row, low, high, embed_weight, pos_embed, ids)
-    part = lax.all_to_all(part, ("yh", "yl"), 0, 0, tiled=True)
     part = part.reshape(YH, YL, 4, 2, 8, width).astype(f32)
     embedded = jnp.transpose(part[:, 0] + part[:, 1], (1, 0, 2, 3, 4)).reshape(8, 2, 8, width)
     one_hot = (
@@ -403,7 +413,8 @@
     got_yh = lax.ppermute(mine_yh, pair, [(0, 1), (1, 0), (2, 3), (3, 2)])
     got_both = lax.ppermute(theirs_yh, pair, [(0, 3), (3, 0), (1, 2), (2, 1)])
 
-    update = mlp(normed_all, tokens, w_gate_up, w_down, mlp_other, ids)
+    mlp_rest = lax.ppermute(mlp_other, "core", [(0, 1), (1, 0)])
+    update = mlp(normed_all, tokens, w_gate_up, w_down, mlp_other, mlp_rest, ids)
     got_core, got_yh, got_both, update = lax.optimization_barrier(
         (got_core, got_yh, got_both, update)
     )

time: 196 us -> 180 us (0.918)
  waiting for transfers between devices: 56 us -> 48.4 us
  local copies, waits for them, and re-layouts: 18.7 us -> 12.9 us
  Pallas kernels: 47.5 us -> 43.7 us
    all_to_all x1, waiting for transfers between devices: 20.8 us -> 8.9 us  [shards(): part = lax.all_to_all(part, ('yh', 'yl'), 0, 0, tiled=True)]
    pallas_call x4, Pallas kernels: 27.1 us -> 23.6 us  [attend(): pl.pallas_call(functools.partial(attend_kernel, last), grid_spec=pltpu.Pr...]
    ppermute x1, starting transfers between devices: 3.17 us -> 0.03 us  [shards(): got_core = lax.ppermute(theirs, pair, [(0, 2), (2, 0), (1, 3), (3, 1)])]
    ppermute x0 -> x1, starting transfers between devices: none -> 3.13 us  [shards(): mlp_rest = lax.ppermute(mlp_other, 'core', [(0, 1), (1, 0)])]
    ppermute x3, starting transfers between devices: 5.49 us -> 2.76 us  [other_half_weights(): return lax.ppermute(array, ('yh', 'yl'), [(0, 3), (3, 0), (1, 2), (2, 1)])]
    unnamed x40 -> x32, local copies, waits for them, and re-layouts: 8.44 us -> 5.87 us
    ppermute x3, waiting for transfers between devices: 4.11 us -> 1.97 us  [other_half_weights(): return lax.ppermute(array, ('yh', 'yl'), [(0, 3), (3, 0), (1, 2), (2, 1)])]
    ppermute x2, waiting for transfers between devices: 0.01 us -> 2.07 us  [shards(): near = [lax.ppermute(first, 'x', x_up), lax.ppermute(second, 'x', x_down)]]
  transfers between devices with their start and end apart: 26 -> 27, of which waited for: 10 -> 13; matrix products, arithmetic and copies ran while one was open for 8% -> 6% of each run, Pallas kernels for 24% -> 19%
where the time goes in v2:
time: 180 us; the launch traced here: 177 us
  starting transfers between devices  51.1 us (28%)
  waiting for transfers between devices  48.4 us (27%)
  Pallas kernels  43.7 us (24%)
  between operations  14 us (8%)
  local copies, waits for them, and re-layouts  12.9 us (7%)
  other arithmetic  4.99 us (3%)
  matrix products  2.05 us (1%)
    pallas_call x4, Pallas kernels, attend(): pl.pallas_call(functools.partial(attend_kernel, last), grid_spec=pltpu.Pr...  23.6 us
    ppermute x4, waiting for transfers between devices, ring_z(): ups[p] = lax.ppermute(ups[p], 'z', forward)  15.2 us
    all_to_all x1, waiting for transfers between devices, shards(): attended = lax.all_to_all(attended, ('core', 'yh', 'z'), 0, 0, tiled=True)  14.8 us
    ppermute x3, starting transfers between devices, ring_z(): downs[p] = lax.ppermute(downs[p], 'z', backward)  9.74 us
    pallas_call x1, Pallas kernels, embed(): pl.pallas_call(embed_kernel, grid_spec=pltpu.PrefetchScalarGridSpec(num_s...  9.31 us
    all_to_all x1, waiting for transfers between devices, shards(): part = lax.all_to_all(part, ('yh', 'yl'), 0, 0, tiled=True)  8.9 us
    ppermute x2, starting transfers between devices, column(): edge = lax.ppermute(edge, LON, pairs)  8.38 us
    unnamed x32, local copies, waits for them, and re-layouts  5.87 us
  transfers between devices with their start and end apart: 27, of which 13 were waited for; matrix products, arithmetic and copies ran while one was open for 6% of the time, Pallas kernels for 19%

profile of v2, /device:TPU:1, one launch (start us, length us, event | category | flops | bytes accessed | tf_op | source)
XLA Modules:
  0.0 177.2 jit_solution(3597971104919254244)
XLA Ops:
  6.6 2.2 %copy-done.1 = bf16[4,69,64,64]{1,3,2,0:T(8,128)(2,1)S(1)} copy-done((bf16[4,69,64,64]{1,3,2,0:T(8,128)(2,1)S(1)}, bf16[4,69,64,64]{1,3,2,0:T(8,128)(2,1)}, u32[]{:S(2)}) %copy-start.1) | copy-done | bytes 2261016
  10.2 4.5 %collective-permute-start = (bf16[4,64,69]{2,1,0:T(8,128)(2,1)S(1)}, bf16[4,64,69]{2,1,0:T(8,128)(2,1)S(1)}, u32[]{:S(2)}, u32[]{:S(2)}) collective-permute-start(bf16[4,64,69]{2,1,0:T(8,128)(2,1)S(1)} %get-tuple-element.29), channel_id=1, source_target_pairs={{0,32},{32,64},{64,96},{96,128},{128,160},{160,192},{192,224},{33,... | collective-permute-start | bytes 105992 | tf_op jit(solution)/shard_map/ppermute | solution.py:68
  16.0 1.7 collective-permute-start.1
  17.8 6.7 %collective-permute-start.2 = (bf16[4,65,69]{2,1,0:T(8,128)(2,1)S(1)}, bf16[4,65,69]{2,1,0:T(8,128)(2,1)S(1)}, u32[]{:S(2)}, u32[]{:S(2)}) collective-permute-start(bf16[4,65,69]{2,1,0:T(8,128)(2,1)S(1)} %pad_maximum_fusion.5), channel_id=1, source_target_pairs={{2,0},{4,2},{6,4},{8,6},{10,8},{12,10},{14,12},{16,14},{18,16},{20... | collective-permute-start | bytes 107648 | tf_op jit(solution)/shard_map/ppermute | solution.py:72
  24.5 1.5 collective-permute-done.1
  26.4 9.3 %shard_map.128 = bf16[256,1024]{1,0:T(8,128)(2,1)} custom-call(s32[4]{0:T(128)S(1)} %pad_add_fusion.s_ref.ids_ref, bf16[4,8,8,64,69]{4,3,2,1,0:T(8,128)(2,1)} %bitcast.72, bf16[4,64,69]{2,1,0:T(8,128)(2,1)S(1)} %collective-permute-done.row_ref, f32[5,32,69]{2,1,0:T(8,128)S(1)} %bitcast.83, f32[5,32,69]{2,1,0:T(8,128)S(1)} %bitcast.82, ...), custom_call_target="tpu_custom_call" | custom-call | flops 8000000000 | bytes 12582912 | tf_op jit(solution)/shard_map/pallas_call | solution.py:129
  35.7 3.5 %all-to-all-start = ((bf16[4,64,1024]{2,1,0:T(8,128)(2,1)}), bf16[4,64,1024]{2,1,0:T(8,128)(2,1)S(1)}, u32[]{:S(2)}, u32[]{:S(2)}) async-start(bf16[4,64,1024]{2,1,0:T(8,128)(2,1)} %bitcast.12), calls=%async_computation | async-start | bytes 1048576 | tf_op jit(solution)/shard_map/all_to_all | solution.py:373
  39.7 8.9 %all-to-all-done = bf16[4,64,1024]{2,1,0:T(8,128)(2,1)S(1)} async-done(((bf16[4,64,1024]{2,1,0:T(8,128)(2,1)}), bf16[4,64,1024]{2,1,0:T(8,128)(2,1)S(1)}, u32[]{:S(2)}, u32[]{:S(2)}) %all-to-all-start) | async-done | bytes 524320 | tf_op jit(solution)/shard_map/all_to_all | solution.py:373
  50.4 4.3 %collective-permute-start.4 = (bf16[8,2,8,1024]{3,2,1,0:T(8,128)(2,1)}, bf16[8,2,8,1024]{3,2,1,0:T(8,128)(2,1)}, u32[]{:S(2)}, u32[]{:S(2)}) collective-permute-start(bf16[8,2,8,1024]{3,2,1,0:T(8,128)(2,1)} %get-tuple-element.54), channel_id=1, source_target_pairs={{2,0},{4,2},{6,4},{8,6},{10,8},{12,10},{14,12},{0,14},{3,1},{5,3},... | collective-permute-start | bytes 786440 | tf_op jit(solution)/shard_map/ppermute | solution.py:253
  56.4 4.9 %collective-permute-done.3 = bf16[8,2,8,1024]{3,2,1,0:T(8,128)(2,1)} collective-permute-done((bf16[8,2,8,1024]{3,2,1,0:T(8,128)(2,1)}, bf16[8,2,8,1024]{3,2,1,0:T(8,128)(2,1)}, u32[]{:S(2)}, u32[]{:S(2)}) %collective-permute-start.3) | collective-permute-done | bytes 262176 | tf_op jit(solution)/shard_map/ppermute | solution.py:251
  61.3 2.7 %collective-permute-start.6 = (bf16[8,2,8,1024]{3,2,1,0:T(8,128)(2,1)}, bf16[8,2,8,1024]{3,2,1,0:T(8,128)(2,1)S(1)}, u32[]{:S(2)}, u32[]{:S(2)}) collective-permute-start(bf16[8,2,8,1024]{3,2,1,0:T(8,128)(2,1)} %collective-permute-done.4), channel_id=1, source_target_pairs={{2,0},{4,2},{6,4},{8,6},{10,8},{12,10},{14,12},{0,14},{3,1},{5,3},... | collective-permute-start | bytes 786440 | tf_op jit(solution)/shard_map/ppermute | solution.py:253
  66.1 1.5 collective-permute-done.7.other_ref
  67.6 1.9 %collective-permute-done.5 = bf16[8,2,8,1024]{3,2,1,0:T(8,128)(2,1)S(1)} collective-permute-done((bf16[8,2,8,1024]{3,2,1,0:T(8,128)(2,1)}, bf16[8,2,8,1024]{3,2,1,0:T(8,128)(2,1)S(1)}, u32[]{:S(2)}, u32[]{:S(2)}) %collective-permute-start.5) | collective-permute-done | bytes 262176 | tf_op jit(solution)/shard_map/ppermute | solution.py:251
  71.4 2.8 %collective-permute-start.9 = (bf16[8,2,8,1024]{3,2,1,0:T(8,128)(2,1)S(1)}, bf16[8,2,8,1024]{3,2,1,0:T(8,128)(2,1)S(1)}, u32[]{:S(2)}, u32[]{:S(2)}) collective-permute-start(bf16[8,2,8,1024]{3,2,1,0:T(8,128)(2,1)S(1)} %collective-permute-done.6), channel_id=1, source_target_pairs={{2,0},{4,2},{6,4},{8,6},{10,8},{12,10},{14,12},{0,14},{3,1},{5,3},... | collective-permute-start | bytes 786440 | tf_op jit(solution)/shard_map/ppermute | solution.py:253
  74.2 2.4 %collective-permute-done.8 = bf16[8,2,8,1024]{3,2,1,0:T(8,128)(2,1)S(1)} collective-permute-done((bf16[8,2,8,1024]{3,2,1,0:T(8,128)(2,1)S(1)}, bf16[8,2,8,1024]{3,2,1,0:T(8,128)(2,1)S(1)}, u32[]{:S(2)}, u32[]{:S(2)}) %collective-permute-start.8) | collective-permute-done | bytes 262176 | tf_op jit(solution)/shard_map/ppermute | solution.py:251
  77.5 6.0 %collective-permute-done.10 = bf16[8,2,8,1024]{3,2,1,0:T(8,128)(2,1)S(1)} collective-permute-done((bf16[8,2,8,1024]{3,2,1,0:T(8,128)(2,1)S(1)}, bf16[8,2,8,1024]{3,2,1,0:T(8,128)(2,1)S(1)}, u32[]{:S(2)}, u32[]{:S(2)}) %collective-permute-start.10) | collective-permute-done | bytes 262176 | tf_op jit(solution)/shard_map/ppermute | solution.py:251
  84.0 3.1 %collective-permute-start.15 = (bf16[384,1024]{1,0:T(8,128)(2,1)}, bf16[384,1024]{1,0:T(8,128)(2,1)}, u32[]{:S(2)}, u32[]{:S(2)}) collective-permute-start(bf16[384,1024]{1,0:T(8,128)(2,1)} %collective-permute-done.11.some_ref), channel_id=1, source_target_pairs={{0,32},{32,0},{1,33},{33,1},{2,34},{34,2},{3,35},{35,3},{4,36},{36... | collective-permute-start | bytes 2359304 | tf_op jit(solution)/shard_map/ppermute | solution.py:416
  88.1 3.5 %shard_map.129 = (bf16[192,512]{1,0:T(8,128)(2,1)S(1)}, bf16[192,512]{1,0:T(8,128)(2,1)}, bf16[192,512]{1,0:T(8,128)(2,1)}, bf16[192,512]{1,0:T(8,128)(2,1)S(1)}) custom-call(s32[4]{0:T(128)S(1)} %pad_add_fusion.s_ref.ids_ref, bf16[8,2,64,1024]{3,2,1,0:T(8,128)(2,1)S(1)} %constant_dynamic-update-slice_fusion.x_ref, bf16[192,1024]{1,0:T(8,128)(2,1)S(1)} %bitcast.81, ...), custom_call_target="tpu_custom_call" | custom-call | flops 3000000000 | bytes 4194304 | tf_op jit(solution)/shard_map/pallas_call | solution.py:287
  92.0 3.3 %collective-permute-start.14 = (bf16[192,512]{1,0:T(8,128)(2,1)S(1)}, bf16[192,512]{1,0:T(8,128)(2,1)}, u32[]{:S(2)}, u32[]{:S(2)}) collective-permute-start(bf16[192,512]{1,0:T(8,128)(2,1)S(1)} %get-tuple-element.43), channel_id=1, source_target_pairs={{0,48},{48,0},{16,32},{32,16},{1,49},{49,1},{17,33},{33,17},{2,50}... | collective-permute-start | bytes 589832 | tf_op jit(solution)/shard_map/ppermute | solution.py:414
  95.3 5.9 %shard_map.130 = bf16[8,2,64,1024]{3,2,1,0:T(8,128)(2,1)S(1)} custom-call(s32[4]{0:T(128)S(1)} %pad_add_fusion.s_ref.ids_ref, bf16[8,2,64,1024]{3,2,1,0:T(8,128)(2,1)S(1)} %constant_dynamic-update-slice_fusion.x_ref, bf16[8,2,8,1024]{3,2,1,0:T(8,128)(2,1)S(1)} %get-tuple-element.64.tok_ref, bf16[2,256,1024]{2,1,0:T(8,128)(2,1)S(1)} %copy-done.4, ...), custom_call_target="tpu_custom_call" | custom-call | flops 6000000000 | bytes 8388608 | tf_op jit(solution)/shard_map/pallas_call | solution.py:326
  102.6 1.8 %collective-permute-done.14 = bf16[192,512]{1,0:T(8,128)(2,1)} collective-permute-done((bf16[192,512]{1,0:T(8,128)(2,1)S(1)}, bf16[192,512]{1,0:T(8,128)(2,1)}, u32[]{:S(2)}, u32[]{:S(2)}) %collective-permute-start.14) | collective-permute-done | bytes 196640 | tf_op jit(solution)/shard_map/ppermute | solution.py:414
  104.6 5.2 %collective-permute-start.21 = (bf16[2,128,512]{2,1,0:T(8,128)(2,1)S(1)}, bf16[2,128,512]{2,1,0:T(8,128)(2,1)S(1)}, u32[]{:S(2)}, u32[]{:S(2)}) collective-permute-start(bf16[2,128,512]{2,1,0:T(8,128)(2,1)S(1)} %pad_maximum_fusion.2.kv_ref), channel_id=1, source_target_pairs={{64,0},{128,64},{192,128},{0,192},{65,1},{129,65},{193,129},{1,193... | collective-permute-start | bytes 786440 | tf_op jit(solution)/shard_map/ppermute | solution.py:430
  113.5 5.7 %shard_map.131.refs_0_ = f32[2048,128]{1,0:T(8,128)S(1)} custom-call(s32[4]{0:T(128)S(1)} %pad_add_fusion.s_ref.ids_ref, bf16[2048,64]{1,0:T(8,128)(2,1)S(1)} %bitcast.76, bf16[2,128,512]{2,1,0:T(8,128)(2,1)S(1)} %pad_maximum_fusion.2.kv_ref, bf16[2,128,512]{2,1,0:T(8,128)(2,1)S(1)} %pad_maximum_fusion.3.kv2_ref), custom_call_target="tpu_custom_call" | custom-call | flops 3221225472 | bytes 4194304 | tf_op jit(solution)/shard_map/pallas_call | solution.py:216
  119.2 2.1 %collective-permute-done.18.kv2_ref = bf16[2,128,512]{2,1,0:T(8,128)(2,1)S(1)} collective-permute-done((bf16[2,128,512]{2,1,0:T(8,128)(2,1)S(1)}, bf16[2,128,512]{2,1,0:T(8,128)(2,1)S(1)}, u32[]{:S(2)}, u32[]{:S(2)}) %collective-permute-start.18) | collective-permute-done | bytes 262176 | tf_op jit(solution)/shard_map/ppermute | solution.py:429
  121.3 3.4 %collective-permute-start.19 = (bf16[2,128,512]{2,1,0:T(8,128)(2,1)S(1)}, bf16[2,128,512]{2,1,0:T(8,128)(2,1)S(1)}, u32[]{:S(2)}, u32[]{:S(2)}) collective-permute-start(bf16[2,128,512]{2,1,0:T(8,128)(2,1)S(1)} %collective-permute-done.18.kv2_ref), channel_id=1, source_target_pairs={{64,0},{128,64},{192,128},{0,192},{65,1},{129,65},{193,129},{1,193... | collective-permute-start | bytes 786440 | tf_op jit(solution)/shard_map/ppermute | solution.py:431
  124.7 5.7 %shard_map.132.refs_0_ = f32[2048,128]{1,0:T(8,128)S(1)} custom-call(s32[4]{0:T(128)S(1)} %pad_add_fusion.s_ref.ids_ref, bf16[2048,64]{1,0:T(8,128)(2,1)S(1)} %bitcast.77, bf16[2,128,512]{2,1,0:T(8,128)(2,1)S(1)} %collective-permute-done.16.kv_ref, bf16[2,128,512]{2,1,0:T(8,128)(2,1)S(1)} %collective-permute-done.18.kv2_ref, f32[2048,128]{1,0:T(8,128)S(1)} %shard_map.131.refs_0_), custom_call_target="tpu_custom_call" | custom-call | flops 3221225472 | bytes 4194304 | tf_op jit(solution)/shard_map/pallas_call | solution.py:216
  130.4 5.7 %shard_map.133.refs_0_ = f32[2048,128]{1,0:T(8,128)S(1)} custom-call(s32[4]{0:T(128)S(1)} %pad_add_fusion.s_ref.ids_ref, bf16[2048,64]{1,0:T(8,128)(2,1)S(1)} %bitcast.78, bf16[2,128,512]{2,1,0:T(8,128)(2,1)S(1)} %collective-permute-done.20.kv_ref, bf16[2,128,512]{2,1,0:T(8,128)(2,1)S(1)} %collective-permute-done.21.kv2_ref, f32[2048,128]{1,0:T(8,128)S(1)} %shard_map.132.refs_0_), custom_call_target="tpu_custom_call" | custom-call | flops 3221225472 | bytes 4194304 | tf_op jit(solution)/shard_map/pallas_call | solution.py:216
  139.2 6.6 %shard_map.134 = bf16[32,32,128]{2,1,0:T(8,128)(2,1)} custom-call(s32[4]{0:T(128)S(1)} %pad_add_fusion.s_ref.ids_ref, bf16[2048,64]{1,0:T(8,128)(2,1)S(1)} %bitcast.79, bf16[2,128,512]{2,1,0:T(8,128)(2,1)S(1)} %collective-permute-done.17.kv_ref, bf16[2,128,512]{2,1,0:T(8,128)(2,1)S(1)} %collective-permute-done.19.kv2_ref, f32[2048,128]{1,0:T(8,128)S(1)} %copy-done.9), custom_call_target="tpu_custom_call" | custom-call | flops 3221225472 | bytes 4194304 | tf_op jit(solution)/shard_map/pallas_call | solution.py:216
  145.8 5.1 %all-to-all-start.1 = ((bf16[32,32,128]{2,1,0:T(8,128)(2,1)}), bf16[32,32,128]{2,1,0:T(8,128)(2,1)S(1)}, u32[]{:S(2)}, u32[]{:S(2)}) async-start(bf16[32,32,128]{2,1,0:T(8,128)(2,1)} %shard_map.134), calls=%async_computation.2 | async-start | bytes 524288 | tf_op jit(solution)/shard_map/all_to_all | solution.py:439
  150.9 14.8 %all-to-all-done.1 = bf16[32,32,128]{2,1,0:T(8,128)(2,1)S(1)} async-done(((bf16[32,32,128]{2,1,0:T(8,128)(2,1)}), bf16[32,32,128]{2,1,0:T(8,128)(2,1)S(1)}, u32[]{:S(2)}, u32[]{:S(2)}) %all-to-all-start.1) | async-done | bytes 262176 | tf_op jit(solution)/shard_map/all_to_all | solution.py:439
  166.7 1.5 fusion.6
  168.6 1.7 fusion.3
  (129 shorter events, 23.4 us)
Async XLA Ops:
  6.5 32.9 %copy-start = (bf16[50,1024]{1,0:T(8,128)(2,1)S(1)}, bf16[50,1024]{1,0:T(8,128)(2,1)}, u32[]{:S(2)}) copy-start(bf16[50,1024]{1,0:T(8,128)(2,1)} %param.18) | copy-start | bytes 307204
  8.8 17.6 %copy-start.7 = (bf16[8,8,1024]{2,1,0:T(8,128)(2,1)S(1)}, bf16[8,8,1024]{2,1,0:T(8,128)(2,1)}, u32[]{:S(2)}) copy-start(bf16[8,8,1024]{2,1,0:T(8,128)(2,1)} %pos_ref.1) | copy-start | bytes 393220
  10.2 5.8 %collective-permute-start = (bf16[4,64,69]{2,1,0:T(8,128)(2,1)S(1)}, bf16[4,64,69]{2,1,0:T(8,128)(2,1)S(1)}, u32[]{:S(2)}, u32[]{:S(2)}) collective-permute-start(bf16[4,64,69]{2,1,0:T(8,128)(2,1)S(1)} %get-tuple-element.29), channel_id=1, source_target_pairs={{0,32},{32,64},{64,96},{96,128},{128,160},{160,192},{192,224},{33,... | collective-permute-start | bytes 105992 | tf_op jit(solution)/shard_map/ppermute | solution.py:68
  16.0 10.0 %collective-permute-start.1 = (bf16[4,65,69]{2,1,0:T(8,128)(2,1)S(1)}, bf16[4,65,69]{2,1,0:T(8,128)(2,1)S(1)}, u32[]{:S(2)}, u32[]{:S(2)}) collective-permute-start(bf16[4,65,69]{2,1,0:T(8,128)(2,1)S(1)} %pad_maximum_fusion.4), channel_id=1, source_target_pairs={{0,2},{2,4},{4,6},{6,8},{8,10},{10,12},{12,14},{14,16},{16,18},{18... | collective-permute-start | bytes 107648 | tf_op jit(solution)/shard_map/ppermute | solution.py:72
  17.8 8.3 %collective-permute-start.2 = (bf16[4,65,69]{2,1,0:T(8,128)(2,1)S(1)}, bf16[4,65,69]{2,1,0:T(8,128)(2,1)S(1)}, u32[]{:S(2)}, u32[]{:S(2)}) collective-permute-start(bf16[4,65,69]{2,1,0:T(8,128)(2,1)S(1)} %pad_maximum_fusion.5), channel_id=1, source_target_pairs={{2,0},{4,2},{6,4},{8,6},{10,8},{12,10},{14,12},{16,14},{18,16},{20... | collective-permute-start | bytes 107648 | tf_op jit(solution)/shard_map/ppermute | solution.py:72
  26.4 13.0 %copy-start.15 = (s32[2]{0:T(128)S(1)}, s32[2]{0:T(128)}, u32[]{:S(2)}) copy-start(s32[2]{0:T(128)} %param.17) | copy-start | bytes 28
  35.7 12.8 %all-to-all-start = ((bf16[4,64,1024]{2,1,0:T(8,128)(2,1)}), bf16[4,64,1024]{2,1,0:T(8,128)(2,1)S(1)}, u32[]{:S(2)}, u32[]{:S(2)}) async-start(bf16[4,64,1024]{2,1,0:T(8,128)(2,1)} %bitcast.12), calls=%async_computation | async-start | bytes 1048576 | tf_op jit(solution)/shard_map/all_to_all | solution.py:373
  39.2 97.8 %all-gather.2.cloned.1.call-start = ((), (), s32[]{:S(2)}) async-start(), calls=%async_computation.4 | async-start | bytes 1179648 | tf_op jit(solution)/shard_map/all_gather | solution.py:406
  49.2 14.7 %copy-start.5 = (bf16[256,1024]{1,0:T(8,128)(2,1)S(1)}, bf16[256,1024]{1,0:T(8,128)(2,1)}, u32[]{:S(2)}) copy-start(bf16[256,1024]{1,0:T(8,128)(2,1)} %down_ref) | copy-start | bytes 1572868
  50.4 10.9 %collective-permute-start.3 = (bf16[8,2,8,1024]{3,2,1,0:T(8,128)(2,1)}, bf16[8,2,8,1024]{3,2,1,0:T(8,128)(2,1)}, u32[]{:S(2)}, u32[]{:S(2)}) collective-permute-start(bf16[8,2,8,1024]{3,2,1,0:T(8,128)(2,1)} %get-tuple-element.54), channel_id=1, source_target_pairs={{0,2},{2,4},{4,6},{6,8},{8,10},{10,12},{12,14},{14,0},{1,3},{3,5},... | collective-permute-start | bytes 786440 | tf_op jit(solution)/shard_map/ppermute | solution.py:251
  50.4 10.9 %collective-permute-start.4 = (bf16[8,2,8,1024]{3,2,1,0:T(8,128)(2,1)}, bf16[8,2,8,1024]{3,2,1,0:T(8,128)(2,1)}, u32[]{:S(2)}, u32[]{:S(2)}) collective-permute-start(bf16[8,2,8,1024]{3,2,1,0:T(8,128)(2,1)} %get-tuple-element.54), channel_id=1, source_target_pairs={{2,0},{4,2},{6,4},{8,6},{10,8},{12,10},{14,12},{0,14},{3,1},{5,3},... | collective-permute-start | bytes 786440 | tf_op jit(solution)/shard_map/ppermute | solution.py:253
  55.5 12.1 %collective-permute-start.7 = (bf16[208,1024]{1,0:T(8,128)(2,1)}, bf16[208,1024]{1,0:T(8,128)(2,1)}, u32[]{:S(2)}, u32[]{:S(2)}) collective-permute-start(bf16[208,1024]{1,0:T(8,128)(2,1)} %pad_maximum_fusion.1), channel_id=1, source_target_pairs={{0,17},{17,0},{1,16},{16,1},{2,19},{19,2},{3,18},{18,3},{4,21},{21... | collective-permute-start | bytes 1277960 | tf_op jit(solution)/shard_map/ppermute | solution.py:22
  61.2 8.2 %collective-permute-start.5 = (bf16[8,2,8,1024]{3,2,1,0:T(8,128)(2,1)}, bf16[8,2,8,1024]{3,2,1,0:T(8,128)(2,1)S(1)}, u32[]{:S(2)}, u32[]{:S(2)}) collective-permute-start(bf16[8,2,8,1024]{3,2,1,0:T(8,128)(2,1)} %collective-permute-done.3), channel_id=1, source_target_pairs={{0,2},{2,4},{4,6},{6,8},{8,10},{10,12},{12,14},{14,0},{1,3},{3,5},... | collective-permute-start | bytes 786440 | tf_op jit(solution)/shard_map/ppermute | solution.py:251
  61.3 8.2 %collective-permute-start.6 = (bf16[8,2,8,1024]{3,2,1,0:T(8,128)(2,1)}, bf16[8,2,8,1024]{3,2,1,0:T(8,128)(2,1)S(1)}, u32[]{:S(2)}, u32[]{:S(2)}) collective-permute-start(bf16[8,2,8,1024]{3,2,1,0:T(8,128)(2,1)} %collective-permute-done.4), channel_id=1, source_target_pairs={{2,0},{4,2},{6,4},{8,6},{10,8},{12,10},{14,12},{0,14},{3,1},{5,3},... | collective-permute-start | bytes 786440 | tf_op jit(solution)/shard_map/ppermute | solution.py:253
  65.1 18.9 %collective-permute-start.11 = (bf16[384,1024]{1,0:T(8,128)(2,1)S(1)}, bf16[384,1024]{1,0:T(8,128)(2,1)}, u32[]{:S(2)}, u32[]{:S(2)}) collective-permute-start(bf16[384,1024]{1,0:T(8,128)(2,1)S(1)} %pad_maximum_fusion), channel_id=1, source_target_pairs={{0,17},{17,0},{1,16},{16,1},{2,19},{19,2},{3,18},{18,3},{4,21},{21... | collective-permute-start | bytes 2359304 | tf_op jit(solution)/shard_map/ppermute | solution.py:22
  69.5 7.2 %collective-permute-start.8 = (bf16[8,2,8,1024]{3,2,1,0:T(8,128)(2,1)S(1)}, bf16[8,2,8,1024]{3,2,1,0:T(8,128)(2,1)S(1)}, u32[]{:S(2)}, u32[]{:S(2)}) collective-permute-start(bf16[8,2,8,1024]{3,2,1,0:T(8,128)(2,1)S(1)} %collective-permute-done.5), channel_id=1, source_target_pairs={{0,2},{2,4},{4,6},{6,8},{8,10},{10,12},{12,14},{14,0},{1,3},{3,5},... | collective-permute-start | bytes 786440 | tf_op jit(solution)/shard_map/ppermute | solution.py:251
  71.4 6.1 %collective-permute-start.9 = (bf16[8,2,8,1024]{3,2,1,0:T(8,128)(2,1)S(1)}, bf16[8,2,8,1024]{3,2,1,0:T(8,128)(2,1)S(1)}, u32[]{:S(2)}, u32[]{:S(2)}) collective-permute-start(bf16[8,2,8,1024]{3,2,1,0:T(8,128)(2,1)S(1)} %collective-permute-done.6), channel_id=1, source_target_pairs={{2,0},{4,2},{6,4},{8,6},{10,8},{12,10},{14,12},{0,14},{3,1},{5,3},... | collective-permute-start | bytes 786440 | tf_op jit(solution)/shard_map/ppermute | solution.py:253
  76.6 6.8 %collective-permute-start.10 = (bf16[8,2,8,1024]{3,2,1,0:T(8,128)(2,1)S(1)}, bf16[8,2,8,1024]{3,2,1,0:T(8,128)(2,1)S(1)}, u32[]{:S(2)}, u32[]{:S(2)}) collective-permute-start(bf16[8,2,8,1024]{3,2,1,0:T(8,128)(2,1)S(1)} %collective-permute-done.8), channel_id=1, source_target_pairs={{0,2},{2,4},{4,6},{6,8},{8,10},{10,12},{12,14},{14,0},{1,3},{3,5},... | collective-permute-start | bytes 786440 | tf_op jit(solution)/shard_map/ppermute | solution.py:251
  84.0 84.6 %reduce-scatter.2.cloned.1.call-start = ((), (), s32[]{:S(2)}) async-start(), calls=%async_computation.3 | async-start | bytes 2359296 | tf_op jit(solution)/shard_map/reduce_scatter | solution.py:421
  84.0 11.3 %collective-permute-start.15 = (bf16[384,1024]{1,0:T(8,128)(2,1)}, bf16[384,1024]{1,0:T(8,128)(2,1)}, u32[]{:S(2)}, u32[]{:S(2)}) collective-permute-start(bf16[384,1024]{1,0:T(8,128)(2,1)} %collective-permute-done.11.some_ref), channel_id=1, source_target_pairs={{0,32},{32,0},{1,33},{33,1},{2,34},{34,2},{3,35},{35,3},{4,36},{36... | collective-permute-start | bytes 2359304 | tf_op jit(solution)/shard_map/ppermute | solution.py:416
  91.7 10.9 %collective-permute-start.12 = (bf16[192,512]{1,0:T(8,128)(2,1)}, bf16[192,512]{1,0:T(8,128)(2,1)S(1)}, u32[]{:S(2)}, u32[]{:S(2)}) collective-permute-start(bf16[192,512]{1,0:T(8,128)(2,1)} %get-tuple-element.41), channel_id=1, source_target_pairs={{0,32},{32,0},{16,48},{48,16},{1,33},{33,1},{17,49},{49,17},{2,34}... | collective-permute-start | bytes 589832 | tf_op jit(solution)/shard_map/ppermute | solution.py:412
  91.7 10.9 %collective-permute-start.13 = (bf16[192,512]{1,0:T(8,128)(2,1)}, bf16[192,512]{1,0:T(8,128)(2,1)S(1)}, u32[]{:S(2)}, u32[]{:S(2)}) collective-permute-start(bf16[192,512]{1,0:T(8,128)(2,1)} %get-tuple-element.42), channel_id=1, source_target_pairs={{0,16},{16,0},{32,48},{48,32},{1,17},{17,1},{33,49},{49,33},{2,18}... | collective-permute-start | bytes 589832 | tf_op jit(solution)/shard_map/ppermute | solution.py:413
  92.0 12.4 %collective-permute-start.14 = (bf16[192,512]{1,0:T(8,128)(2,1)S(1)}, bf16[192,512]{1,0:T(8,128)(2,1)}, u32[]{:S(2)}, u32[]{:S(2)}) collective-permute-start(bf16[192,512]{1,0:T(8,128)(2,1)S(1)} %get-tuple-element.43), channel_id=1, source_target_pairs={{0,48},{48,0},{16,32},{32,16},{1,49},{49,1},{17,33},{33,17},{2,50}... | collective-permute-start | bytes 589832 | tf_op jit(solution)/shard_map/ppermute | solution.py:414
  104.5 14.6 %collective-permute-start.16 = (bf16[2,128,512]{2,1,0:T(8,128)(2,1)S(1)}, bf16[2,128,512]{2,1,0:T(8,128)(2,1)S(1)}, u32[]{:S(2)}, u32[]{:S(2)}) collective-permute-start(bf16[2,128,512]{2,1,0:T(8,128)(2,1)S(1)} %pad_maximum_fusion.2.kv_ref), channel_id=1, source_target_pairs={{0,64},{64,128},{128,192},{192,0},{1,65},{65,129},{129,193},{193,1... | collective-permute-start | bytes 786440 | tf_op jit(solution)/shard_map/ppermute | solution.py:429
  104.6 25.8 %collective-permute-start.21 = (bf16[2,128,512]{2,1,0:T(8,128)(2,1)S(1)}, bf16[2,128,512]{2,1,0:T(8,128)(2,1)S(1)}, u32[]{:S(2)}, u32[]{:S(2)}) collective-permute-start(bf16[2,128,512]{2,1,0:T(8,128)(2,1)S(1)} %pad_maximum_fusion.2.kv_ref), channel_id=1, source_target_pairs={{64,0},{128,64},{192,128},{0,192},{65,1},{129,65},{193,129},{1,193... | collective-permute-start | bytes 786440 | tf_op jit(solution)/shard_map/ppermute | solution.py:430
  110.7 10.6 %collective-permute-start.18 = (bf16[2,128,512]{2,1,0:T(8,128)(2,1)S(1)}, bf16[2,128,512]{2,1,0:T(8,128)(2,1)S(1)}, u32[]{:S(2)}, u32[]{:S(2)}) collective-permute-start(bf16[2,128,512]{2,1,0:T(8,128)(2,1)S(1)} %pad_maximum_fusion.3.kv2_ref), channel_id=1, source_target_pairs={{64,0},{128,64},{192,128},{0,192},{65,1},{129,65},{193,129},{1,193... | collective-permute-start | bytes 786440 | tf_op jit(solution)/shard_map/ppermute | solution.py:429
  112.2 18.2 %collective-permute-start.20 = (bf16[2,128,512]{2,1,0:T(8,128)(2,1)S(1)}, bf16[2,128,512]{2,1,0:T(8,128)(2,1)S(1)}, u32[]{:S(2)}, u32[]{:S(2)}) collective-permute-start(bf16[2,128,512]{2,1,0:T(8,128)(2,1)S(1)} %pad_maximum_fusion.3.kv2_ref), channel_id=1, source_target_pairs={{0,64},{64,128},{128,192},{192,0},{1,65},{65,129},{129,193},{193,1... | collective-permute-start | bytes 786440 | tf_op jit(solution)/shard_map/ppermute | solution.py:430
  119.1 18.8 %collective-permute-start.17 = (bf16[2,128,512]{2,1,0:T(8,128)(2,1)S(1)}, bf16[2,128,512]{2,1,0:T(8,128)(2,1)S(1)}, u32[]{:S(2)}, u32[]{:S(2)}) collective-permute-start(bf16[2,128,512]{2,1,0:T(8,128)(2,1)S(1)} %collective-permute-done.16.kv_ref), channel_id=1, source_target_pairs={{0,64},{64,128},{128,192},{192,0},{1,65},{65,129},{129,193},{193,1... | collective-permute-start | bytes 786440 | tf_op jit(solution)/shard_map/ppermute | solution.py:431
  121.3 16.7 %collective-permute-start.19 = (bf16[2,128,512]{2,1,0:T(8,128)(2,1)S(1)}, bf16[2,128,512]{2,1,0:T(8,128)(2,1)S(1)}, u32[]{:S(2)}, u32[]{:S(2)}) collective-permute-start(bf16[2,128,512]{2,1,0:T(8,128)(2,1)S(1)} %collective-permute-done.18.kv2_ref), channel_id=1, source_target_pairs={{64,0},{128,64},{192,128},{0,192},{65,1},{129,65},{193,129},{1,193... | collective-permute-start | bytes 786440 | tf_op jit(solution)/shard_map/ppermute | solution.py:431
  137.1 29.6 %collective-permute-start.22 = (bf16[512,1024]{1,0:T(8,128)(2,1)}, bf16[512,1024]{1,0:T(8,128)(2,1)}, u32[]{:S(2)}, u32[]{:S(2)}) collective-permute-start(bf16[512,1024]{1,0:T(8,128)(2,1)} %all-gather.2.cloned.1.call-done), channel_id=1, source_target_pairs={{0,17},{17,0},{1,16},{16,1},{2,19},{19,2},{3,18},{18,3},{4,21},{21... | collective-permute-start | bytes 3145736 | tf_op jit(solution)/shard_map/ppermute | solution.py:22
  145.8 19.9 %all-to-all-start.1 = ((bf16[32,32,128]{2,1,0:T(8,128)(2,1)}), bf16[32,32,128]{2,1,0:T(8,128)(2,1)S(1)}, u32[]{:S(2)}, u32[]{:S(2)}) async-start(bf16[32,32,128]{2,1,0:T(8,128)(2,1)} %shard_map.134), calls=%async_computation.2 | async-start | bytes 524288 | tf_op jit(solution)/shard_map/all_to_all | solution.py:439
  150.9 17.3 %copy-start.10 = (bf16[512,1024]{1,0:T(8,128)(2,1)S(1)}, bf16[512,1024]{1,0:T(8,128)(2,1)}, u32[]{:S(2)}) copy-start(bf16[512,1024]{1,0:T(8,128)(2,1)} %all-gather.2.cloned.1.call-done) | copy-start | bytes 3145732
  (11 other events, 65.4 us)
Sparse Core Ops, SparseCore 0:
  84.1 35.2 all-gather.1
  122.0 46.1 reduce-scatter.1

commit v3 on v2

--- a/solution.py
+++ b/solution.py
@@ -79,7 +79,7 @@
 
 
 def embed_kernel(
-    ids_ref, f_ref, row_ref, low_ref, high_ref, w_ref, pos_ref, out_ref, xf, rhs, acc
+    ids_ref, f_ref, row_ref, low_ref, high_ref, w_ref, w2_ref, pos_ref, out_ref, xf, rhs, acc
 ):
     step = pl.program_id(0)
     section = ids_ref[0]
@@ -103,10 +103,10 @@
         xf[slot, 8:72, :channels] = value.astype(jnp.float32)
         xf[slot, 7:8, :channels] = low_ref[0, slot : slot + 1]
         xf[slot, 72:73, :channels] = high_ref[0, slot : slot + 1]
-    taps = w_ref.shape[1]
+    half = w_ref.shape[1]
     columns = []
-    for b in range(taps):
-        rhs[b * 128 : b * 128 + channels, :] = w_ref[0, b]
+    for b in range(2 * half):
+        rhs[b * 128 : b * 128 + channels, :] = (w_ref if b < half else w2_ref)[0, b % half]
         column = xf[:, pl.ds(7 + b, 8, stride=8), :]
         columns.append(column.reshape(256, 128).astype(jnp.bfloat16))
     lhs = jnp.concatenate(columns, 1)
@@ -139,7 +139,8 @@
                 pl.BlockSpec(row.shape, whole(3)),
                 pl.BlockSpec((1, 32, channels), lambda i, s: (i, 0, 0)),
                 pl.BlockSpec((1, 32, channels), lambda i, s: (i, 0, 0)),
-                pl.BlockSpec((1, cols, channels, width), lambda i, s: (i, 0, 0, 0)),
+                pl.BlockSpec((1, cols // 2, channels, width), lambda i, s: (i, 0, 0, 0)),
+                pl.BlockSpec((1, cols // 2, channels, width), lambda i, s: (i, 1, 0, 0)),
                 pl.BlockSpec(pos.shape, whole(3)),
             ],
             out_specs=pl.BlockSpec((256, width), whole(2)),
@@ -154,7 +155,7 @@
         cost_estimate=pl.CostEstimate(
             flops=8 * 10**9, bytes_accessed=12 * 2**20, transcendentals=0
         ),
-    )(ids, f.reshape(members, 8, rows // 8, wide, channels), row, low, high, weight, pos)
+    )(ids, f.reshape(members, 8, rows // 8, wide, channels), row, low, high, weight, weight, pos)
 
 
 def attend_kernel(last, ids_ref, q_ref, kv_ref, kv2_ref, *refs):
@@ -371,9 +372,10 @@
     row, low, high = halo(f, ids, yl)
     part = embed(f, row, low, high, embed_weight, pos_embed, ids)
     part = lax.all_to_all(part, ("yh", "yl"), 0, 0, tiled=True)
-    part, terms, w_qkv, w_gate_up, w_down = lax.optimization_barrier(
-        (part, terms, w_qkv, w_gate_up, w_down)
+    part, terms, w_qkv, w_gate_up, w_down, w_out = lax.optimization_barrier(
+        (part, terms, w_qkv, w_gate_up, w_down, w_out)
     )
+    w_out_half = lax.all_gather(w_out, "z", axis=0, tiled=True)
     qkv_other = other_half_weights(jnp.concatenate([w_qkv.reshape(-1, width), terms], 0))
     units = w_down.shape[0] // 2
     some_gu = lax.dynamic_slice_in_dim(w_gate_up, core * units, units, 1)
@@ -402,8 +404,7 @@
     normed = (centered * lax.rsqrt(variance + layer_epsilon) * norm_gain).astype(bf16)
 
     normed_all, qkv_other = ring_z(normed, qkv_other)
-    normed_all, mlp_other, w_out = lax.optimization_barrier((normed_all, mlp_other, w_out))
-    w_out_half = lax.all_gather(w_out, "z", axis=0, tiled=True)
+    normed_all, mlp_other = lax.optimization_barrier((normed_all, mlp_other))
 
     mine, mine_yh, theirs, theirs_yh = project(
         normed_all, w_qkv.reshape(3 * HEAD, width), qkv_other, gain_both, ids
@@ -431,10 +432,10 @@
     far = [lax.ppermute(near[0], "x", x_up), lax.ppermute(near[1], "x", x_down)]
 
     acc = attend(ids, q, (first, second))
+    acc, w_out_half = lax.optimization_barrier((acc, w_out_half))
+    w_out_other = other_half_weights(w_out_half)
     acc = attend(ids, q, near, acc)
     acc = attend(ids, q, late, acc)
-    acc, w_out_half = lax.optimization_barrier((acc, w_out_half))
-    w_out_other = other_half_weights(w_out_half)
     attended = attend(ids, q, far, acc, last=True)
     attended = lax.all_to_all(attended, ("core", "yh", "z"), 0, 0, tiled=True)
     attended = attended.reshape(CORE, YH, Z, 32, 2, HEAD)

time: 180 us -> 176 us (0.978)
  waiting for transfers between devices: 48.4 us -> 45.4 us
    ppermute x2, starting transfers between devices: 1.54 us -> 5.52 us  [shards(): near = [lax.ppermute(first, 'x', x_up), lax.ppermute(second, 'x', x_down)]]
    all_to_all x1, waiting for transfers between devices: 14.8 us -> 11.8 us  [shards(): attended = lax.all_to_all(attended, ('core', 'yh', 'z'), 0, 0, tiled=True)]
    ppermute x2, starting transfers between devices: 5.28 us -> 2.75 us  [shards(): late = [lax.ppermute(second, 'x', x_up), lax.ppermute(first, 'x', x_down)]]
    dynamic_update_slice x7, local copies, waits for them, and re-layouts: 2.05 us -> 3.95 us  [place(): lax.dynamic_update_slice(out, shard, (part * size, 0, at % Z * cols, 0))]
    ppermute x3, waiting for transfers between devices: 0.79 us -> 2.62 us  [ring_z(): downs[p] = lax.ppermute(downs[p], 'z', backward)]
    ppermute x2, starting transfers between devices: 3.49 us -> 1.67 us  [shards(): far = [lax.ppermute(near[0], 'x', x_up), lax.ppermute(near[1], 'x', x_down)]]
  transfers between devices with their start and end apart: 27 -> 27, of which waited for: 13 -> 12; matrix products, arithmetic and copies ran while one was open for 6% -> 7% of each run, Pallas kernels for 19% -> 19%
where the time goes in v3:
time: 176 us; the launch traced here: 175 us
  starting transfers between devices  50.4 us (29%)
  waiting for transfers between devices  45.4 us (26%)
  Pallas kernels  43.6 us (25%)
  local copies, waits for them, and re-layouts  14.7 us (8%)
  between operations  14 us (8%)
  other arithmetic  5.88 us (3%)
    pallas_call x4, Pallas kernels, attend(): pl.pallas_call(functools.partial(attend_kernel, last), grid_spec=pltpu.Pr...  23.6 us
    ppermute x4, waiting for transfers between devices, ring_z(): ups[p] = lax.ppermute(ups[p], 'z', forward)  14.4 us
    all_to_all x1, waiting for transfers between devices, shards(): attended = lax.all_to_all(attended, ('core', 'yh', 'z'), 0, 0, tiled=True)  11.8 us
    ppermute x3, starting transfers between devices, ring_z(): downs[p] = lax.ppermute(downs[p], 'z', backward)  9.76 us
    pallas_call x1, Pallas kernels, embed(): pl.pallas_call(embed_kernel, grid_spec=pltpu.PrefetchScalarGridSpec(num_s...  9.18 us
    all_to_all x1, waiting for transfers between devices, shards(): part = lax.all_to_all(part, ('yh', 'yl'), 0, 0, tiled=True)  8.88 us
    ppermute x2, starting transfers between devices, column(): edge = lax.ppermute(edge, LON, pairs)  8.38 us
    pallas_call x1, Pallas kernels, mlp(): pl.pallas_call(mlp_kernel, grid_spec=pltpu.PrefetchScalarGridSpec(num_sca...  5.86 us
  transfers between devices with their start and end apart: 27, of which 12 were waited for; matrix products, arithmetic and copies ran while one was open for 7% of the time, Pallas kernels for 19%

profile of v3, /device:TPU:1, one launch (start us, length us, event | category | flops | bytes accessed | tf_op | source)
XLA Modules:
  0.0 174.8 jit_solution(18238595020061262714)
XLA Ops:
  6.6 2.2 %copy-done.1 = bf16[4,69,64,64]{1,3,2,0:T(8,128)(2,1)S(1)} copy-done((bf16[4,69,64,64]{1,3,2,0:T(8,128)(2,1)S(1)}, bf16[4,69,64,64]{1,3,2,0:T(8,128)(2,1)}, u32[]{:S(2)}) %copy-start.1) | copy-done | bytes 2261016
  10.2 4.5 %collective-permute-start = (bf16[4,64,69]{2,1,0:T(8,128)(2,1)S(1)}, bf16[4,64,69]{2,1,0:T(8,128)(2,1)S(1)}, u32[]{:S(2)}, u32[]{:S(2)}) collective-permute-start(bf16[4,64,69]{2,1,0:T(8,128)(2,1)S(1)} %get-tuple-element.29), channel_id=1, source_target_pairs={{0,32},{32,64},{64,96},{96,128},{128,160},{160,192},{192,224},{33,... | collective-permute-start | bytes 105992 | tf_op jit(solution)/shard_map/ppermute | solution.py:68
  16.0 1.7 collective-permute-start.1
  17.8 6.7 %collective-permute-start.2 = (bf16[4,65,69]{2,1,0:T(8,128)(2,1)S(1)}, bf16[4,65,69]{2,1,0:T(8,128)(2,1)S(1)}, u32[]{:S(2)}, u32[]{:S(2)}) collective-permute-start(bf16[4,65,69]{2,1,0:T(8,128)(2,1)S(1)} %pad_maximum_fusion.5), channel_id=1, source_target_pairs={{2,0},{4,2},{6,4},{8,6},{10,8},{12,10},{14,12},{16,14},{18,16},{20... | collective-permute-start | bytes 107648 | tf_op jit(solution)/shard_map/ppermute | solution.py:72
  24.5 1.5 collective-permute-done.1
  26.4 9.2 %shard_map.128 = bf16[256,1024]{1,0:T(8,128)(2,1)} custom-call(s32[4]{0:T(128)S(1)} %pad_add_fusion.s_ref.ids_ref, bf16[4,8,8,64,69]{4,3,2,1,0:T(8,128)(2,1)} %bitcast.72, bf16[4,64,69]{2,1,0:T(8,128)(2,1)S(1)} %collective-permute-done.row_ref, f32[5,32,69]{2,1,0:T(8,128)S(1)} %bitcast.83, f32[5,32,69]{2,1,0:T(8,128)S(1)} %bitcast.82, ...), custom_call_target="tpu_custom_call" | custom-call | flops 8000000000 | bytes 12582912 | tf_op jit(solution)/shard_map/pallas_call | solution.py:129
  35.6 3.5 %all-to-all-start = ((bf16[4,64,1024]{2,1,0:T(8,128)(2,1)}), bf16[4,64,1024]{2,1,0:T(8,128)(2,1)S(1)}, u32[]{:S(2)}, u32[]{:S(2)}) async-start(bf16[4,64,1024]{2,1,0:T(8,128)(2,1)} %bitcast.12), calls=%async_computation | async-start | bytes 1048576 | tf_op jit(solution)/shard_map/all_to_all | solution.py:374
  39.5 8.9 %all-to-all-done = bf16[4,64,1024]{2,1,0:T(8,128)(2,1)S(1)} async-done(((bf16[4,64,1024]{2,1,0:T(8,128)(2,1)}), bf16[4,64,1024]{2,1,0:T(8,128)(2,1)S(1)}, u32[]{:S(2)}, u32[]{:S(2)}) %all-to-all-start) | async-done | bytes 524320 | tf_op jit(solution)/shard_map/all_to_all | solution.py:374
  50.2 4.3 %collective-permute-start.4 = (bf16[8,2,8,1024]{3,2,1,0:T(8,128)(2,1)}, bf16[8,2,8,1024]{3,2,1,0:T(8,128)(2,1)}, u32[]{:S(2)}, u32[]{:S(2)}) collective-permute-start(bf16[8,2,8,1024]{3,2,1,0:T(8,128)(2,1)} %get-tuple-element.54), channel_id=1, source_target_pairs={{2,0},{4,2},{6,4},{8,6},{10,8},{12,10},{14,12},{0,14},{3,1},{5,3},... | collective-permute-start | bytes 786440 | tf_op jit(solution)/shard_map/ppermute | solution.py:254
  56.2 4.9 %collective-permute-done.3 = bf16[8,2,8,1024]{3,2,1,0:T(8,128)(2,1)} collective-permute-done((bf16[8,2,8,1024]{3,2,1,0:T(8,128)(2,1)}, bf16[8,2,8,1024]{3,2,1,0:T(8,128)(2,1)}, u32[]{:S(2)}, u32[]{:S(2)}) %collective-permute-start.3) | collective-permute-done | bytes 262176 | tf_op jit(solution)/shard_map/ppermute | solution.py:252
  61.1 2.7 %collective-permute-start.6 = (bf16[8,2,8,1024]{3,2,1,0:T(8,128)(2,1)}, bf16[8,2,8,1024]{3,2,1,0:T(8,128)(2,1)}, u32[]{:S(2)}, u32[]{:S(2)}) collective-permute-start(bf16[8,2,8,1024]{3,2,1,0:T(8,128)(2,1)} %collective-permute-done.4), channel_id=1, source_target_pairs={{2,0},{4,2},{6,4},{8,6},{10,8},{12,10},{14,12},{0,14},{3,1},{5,3},... | collective-permute-start | bytes 786440 | tf_op jit(solution)/shard_map/ppermute | solution.py:254
  67.5 2.0 %collective-permute-done.5 = bf16[8,2,8,1024]{3,2,1,0:T(8,128)(2,1)} collective-permute-done((bf16[8,2,8,1024]{3,2,1,0:T(8,128)(2,1)}, bf16[8,2,8,1024]{3,2,1,0:T(8,128)(2,1)}, u32[]{:S(2)}, u32[]{:S(2)}) %collective-permute-start.5) | collective-permute-done | bytes 262176 | tf_op jit(solution)/shard_map/ppermute | solution.py:252
  71.4 2.8 %collective-permute-start.9 = (bf16[8,2,8,1024]{3,2,1,0:T(8,128)(2,1)}, bf16[8,2,8,1024]{3,2,1,0:T(8,128)(2,1)S(1)}, u32[]{:S(2)}, u32[]{:S(2)}) collective-permute-start(bf16[8,2,8,1024]{3,2,1,0:T(8,128)(2,1)} %collective-permute-done.6), channel_id=1, source_target_pairs={{2,0},{4,2},{6,4},{8,6},{10,8},{12,10},{14,12},{0,14},{3,1},{5,3},... | collective-permute-start | bytes 786440 | tf_op jit(solution)/shard_map/ppermute | solution.py:254
  75.2 1.7 collective-permute-done.8
  77.9 2.6 %collective-permute-done.9 = bf16[8,2,8,1024]{3,2,1,0:T(8,128)(2,1)S(1)} collective-permute-done((bf16[8,2,8,1024]{3,2,1,0:T(8,128)(2,1)}, bf16[8,2,8,1024]{3,2,1,0:T(8,128)(2,1)S(1)}, u32[]{:S(2)}, u32[]{:S(2)}) %collective-permute-start.9) | collective-permute-done | bytes 262176 | tf_op jit(solution)/shard_map/ppermute | solution.py:254
  80.5 5.8 %collective-permute-done.10 = bf16[8,2,8,1024]{3,2,1,0:T(8,128)(2,1)S(1)} collective-permute-done((bf16[8,2,8,1024]{3,2,1,0:T(8,128)(2,1)S(1)}, bf16[8,2,8,1024]{3,2,1,0:T(8,128)(2,1)S(1)}, u32[]{:S(2)}, u32[]{:S(2)}) %collective-permute-start.10) | collective-permute-done | bytes 262176 | tf_op jit(solution)/shard_map/ppermute | solution.py:252
  86.4 4.2 %collective-permute-start.15 = (bf16[384,1024]{1,0:T(8,128)(2,1)}, bf16[384,1024]{1,0:T(8,128)(2,1)}, u32[]{:S(2)}, u32[]{:S(2)}) collective-permute-start(bf16[384,1024]{1,0:T(8,128)(2,1)} %collective-permute-done.11.some_ref), channel_id=1, source_target_pairs={{0,32},{32,0},{1,33},{33,1},{2,34},{34,2},{3,35},{35,3},{4,36},{36... | collective-permute-start | bytes 2359304 | tf_op jit(solution)/shard_map/ppermute | solution.py:417
  91.5 3.5 %shard_map.129 = (bf16[192,512]{1,0:T(8,128)(2,1)S(1)}, bf16[192,512]{1,0:T(8,128)(2,1)}, bf16[192,512]{1,0:T(8,128)(2,1)}, bf16[192,512]{1,0:T(8,128)(2,1)S(1)}) custom-call(s32[4]{0:T(128)S(1)} %pad_add_fusion.s_ref.ids_ref, bf16[8,2,64,1024]{3,2,1,0:T(8,128)(2,1)S(1)} %constant_dynamic-update-slice_fusion.x_ref, bf16[192,1024]{1,0:T(8,128)(2,1)S(1)} %bitcast.81, ...), custom_call_target="tpu_custom_call" | custom-call | flops 3000000000 | bytes 4194304 | tf_op jit(solution)/shard_map/pallas_call | solution.py:288
  95.1 3.6 %collective-permute-start.14 = (bf16[192,512]{1,0:T(8,128)(2,1)S(1)}, bf16[192,512]{1,0:T(8,128)(2,1)}, u32[]{:S(2)}, u32[]{:S(2)}) collective-permute-start(bf16[192,512]{1,0:T(8,128)(2,1)S(1)} %get-tuple-element.43), channel_id=1, source_target_pairs={{0,48},{48,0},{16,32},{32,16},{1,49},{49,1},{17,33},{33,17},{2,50}... | collective-permute-start | bytes 589832 | tf_op jit(solution)/shard_map/ppermute | solution.py:415
  98.7 5.9 %shard_map.130 = bf16[8,2,64,1024]{3,2,1,0:T(8,128)(2,1)S(1)} custom-call(s32[4]{0:T(128)S(1)} %pad_add_fusion.s_ref.ids_ref, bf16[8,2,64,1024]{3,2,1,0:T(8,128)(2,1)S(1)} %constant_dynamic-update-slice_fusion.x_ref, bf16[8,2,8,1024]{3,2,1,0:T(8,128)(2,1)S(1)} %get-tuple-element.64.tok_ref, bf16[2,256,1024]{2,1,0:T(8,128)(2,1)S(1)} %copy-done.4, ...), custom_call_target="tpu_custom_call" | custom-call | flops 6000000000 | bytes 8388608 | tf_op jit(solution)/shard_map/pallas_call | solution.py:327
  105.9 1.8 %collective-permute-done.14 = bf16[192,512]{1,0:T(8,128)(2,1)} collective-permute-done((bf16[192,512]{1,0:T(8,128)(2,1)S(1)}, bf16[192,512]{1,0:T(8,128)(2,1)}, u32[]{:S(2)}, u32[]{:S(2)}) %collective-permute-start.14) | collective-permute-done | bytes 196640 | tf_op jit(solution)/shard_map/ppermute | solution.py:415
  108.8 5.4 %collective-permute-start.18 = (bf16[2,128,512]{2,1,0:T(8,128)(2,1)S(1)}, bf16[2,128,512]{2,1,0:T(8,128)(2,1)S(1)}, u32[]{:S(2)}, u32[]{:S(2)}) collective-permute-start(bf16[2,128,512]{2,1,0:T(8,128)(2,1)S(1)} %pad_maximum_fusion.3.kv2_ref), channel_id=1, source_target_pairs={{64,0},{128,64},{192,128},{0,192},{65,1},{129,65},{193,129},{1,193... | collective-permute-start | bytes 786440 | tf_op jit(solution)/shard_map/ppermute | solution.py:430
  114.4 2.8 %collective-permute-start.21 = (bf16[2,128,512]{2,1,0:T(8,128)(2,1)S(1)}, bf16[2,128,512]{2,1,0:T(8,128)(2,1)S(1)}, u32[]{:S(2)}, u32[]{:S(2)}) collective-permute-start(bf16[2,128,512]{2,1,0:T(8,128)(2,1)S(1)} %pad_maximum_fusion.2.kv_ref), channel_id=1, source_target_pairs={{64,0},{128,64},{192,128},{0,192},{65,1},{129,65},{193,129},{1,193... | collective-permute-start | bytes 786440 | tf_op jit(solution)/shard_map/ppermute | solution.py:431
  118.3 5.7 %shard_map.131.refs_0_ = f32[2048,128]{1,0:T(8,128)S(1)} custom-call(s32[4]{0:T(128)S(1)} %pad_add_fusion.s_ref.ids_ref, bf16[2048,64]{1,0:T(8,128)(2,1)S(1)} %bitcast.76, bf16[2,128,512]{2,1,0:T(8,128)(2,1)S(1)} %pad_maximum_fusion.2.kv_ref, bf16[2,128,512]{2,1,0:T(8,128)(2,1)S(1)} %pad_maximum_fusion.3.kv2_ref), custom_call_target="tpu_custom_call" | custom-call | flops 3221225472 | bytes 4194304 | tf_op jit(solution)/shard_map/pallas_call | solution.py:217
  125.0 1.7 collective-permute-start.19
  126.6 2.3 %collective-permute-done.16.kv_ref = bf16[2,128,512]{2,1,0:T(8,128)(2,1)S(1)} collective-permute-done((bf16[2,128,512]{2,1,0:T(8,128)(2,1)S(1)}, bf16[2,128,512]{2,1,0:T(8,128)(2,1)S(1)}, u32[]{:S(2)}, u32[]{:S(2)}) %collective-permute-start.16) | collective-permute-done | bytes 262176 | tf_op jit(solution)/shard_map/ppermute | solution.py:430
  130.2 5.7 %shard_map.132.refs_0_ = f32[2048,128]{1,0:T(8,128)S(1)} custom-call(s32[4]{0:T(128)S(1)} %pad_add_fusion.s_ref.ids_ref, bf16[2048,64]{1,0:T(8,128)(2,1)S(1)} %bitcast.77, bf16[2,128,512]{2,1,0:T(8,128)(2,1)S(1)} %collective-permute-done.16.kv_ref, bf16[2,128,512]{2,1,0:T(8,128)(2,1)S(1)} %collective-permute-done.18.kv2_ref, f32[2048,128]{1,0:T(8,128)S(1)} %copy-done.9), custom_call_target="tpu_custom_call" | custom-call | flops 3221225472 | bytes 4194304 | tf_op jit(solution)/shard_map/pallas_call | solution.py:217
  135.9 5.7 %shard_map.133.refs_0_ = f32[2048,128]{1,0:T(8,128)S(1)} custom-call(s32[4]{0:T(128)S(1)} %pad_add_fusion.s_ref.ids_ref, bf16[2048,64]{1,0:T(8,128)(2,1)S(1)} %bitcast.78, bf16[2,128,512]{2,1,0:T(8,128)(2,1)S(1)} %collective-permute-done.20.kv_ref, bf16[2,128,512]{2,1,0:T(8,128)(2,1)S(1)} %collective-permute-done.21.kv2_ref, f32[2048,128]{1,0:T(8,128)S(1)} %shard_map.132.refs_0_), custom_call_target="tpu_custom_call" | custom-call | flops 3221225472 | bytes 4194304 | tf_op jit(solution)/shard_map/pallas_call | solution.py:217
  141.6 6.6 %shard_map.134 = bf16[32,32,128]{2,1,0:T(8,128)(2,1)} custom-call(s32[4]{0:T(128)S(1)} %pad_add_fusion.s_ref.ids_ref, bf16[2048,64]{1,0:T(8,128)(2,1)S(1)} %bitcast.79, bf16[2,128,512]{2,1,0:T(8,128)(2,1)S(1)} %collective-permute-done.17.kv_ref, bf16[2,128,512]{2,1,0:T(8,128)(2,1)S(1)} %collective-permute-done.19.kv2_ref, f32[2048,128]{1,0:T(8,128)S(1)} %shard_map.133.refs_0_), custom_call_target="tpu_custom_call" | custom-call | flops 3221225472 | bytes 4194304 | tf_op jit(solution)/shard_map/pallas_call | solution.py:217
  148.2 4.6 %all-to-all-start.1 = ((bf16[32,32,128]{2,1,0:T(8,128)(2,1)}), bf16[32,32,128]{2,1,0:T(8,128)(2,1)S(1)}, u32[]{:S(2)}, u32[]{:S(2)}) async-start(bf16[32,32,128]{2,1,0:T(8,128)(2,1)} %shard_map.134), calls=%async_computation.2 | async-start | bytes 524288 | tf_op jit(solution)/shard_map/all_to_all | solution.py:440
  152.8 11.8 %all-to-all-done.1 = bf16[32,32,128]{2,1,0:T(8,128)(2,1)S(1)} async-done(((bf16[32,32,128]{2,1,0:T(8,128)(2,1)}), bf16[32,32,128]{2,1,0:T(8,128)(2,1)S(1)}, u32[]{:S(2)}, u32[]{:S(2)}) %all-to-all-start.1) | async-done | bytes 262176 | tf_op jit(solution)/shard_map/all_to_all | solution.py:440
  166.2 1.7 fusion.3
  (129 shorter events, 22.9 us)
Async XLA Ops:
  6.5 32.8 %copy-start = (bf16[50,1024]{1,0:T(8,128)(2,1)S(1)}, bf16[50,1024]{1,0:T(8,128)(2,1)}, u32[]{:S(2)}) copy-start(bf16[50,1024]{1,0:T(8,128)(2,1)} %param.18) | copy-start | bytes 307204
  8.8 17.6 %copy-start.7 = (bf16[8,8,1024]{2,1,0:T(8,128)(2,1)S(1)}, bf16[8,8,1024]{2,1,0:T(8,128)(2,1)}, u32[]{:S(2)}) copy-start(bf16[8,8,1024]{2,1,0:T(8,128)(2,1)} %pos_ref.1) | copy-start | bytes 393220
  10.2 5.8 %collective-permute-start = (bf16[4,64,69]{2,1,0:T(8,128)(2,1)S(1)}, bf16[4,64,69]{2,1,0:T(8,128)(2,1)S(1)}, u32[]{:S(2)}, u32[]{:S(2)}) collective-permute-start(bf16[4,64,69]{2,1,0:T(8,128)(2,1)S(1)} %get-tuple-element.29), channel_id=1, source_target_pairs={{0,32},{32,64},{64,96},{96,128},{128,160},{160,192},{192,224},{33,... | collective-permute-start | bytes 105992 | tf_op jit(solution)/shard_map/ppermute | solution.py:68
  16.0 10.0 %collective-permute-start.1 = (bf16[4,65,69]{2,1,0:T(8,128)(2,1)S(1)}, bf16[4,65,69]{2,1,0:T(8,128)(2,1)S(1)}, u32[]{:S(2)}, u32[]{:S(2)}) collective-permute-start(bf16[4,65,69]{2,1,0:T(8,128)(2,1)S(1)} %pad_maximum_fusion.4), channel_id=1, source_target_pairs={{0,2},{2,4},{4,6},{6,8},{8,10},{10,12},{12,14},{14,16},{16,18},{18... | collective-permute-start | bytes 107648 | tf_op jit(solution)/shard_map/ppermute | solution.py:72
  17.8 8.3 %collective-permute-start.2 = (bf16[4,65,69]{2,1,0:T(8,128)(2,1)S(1)}, bf16[4,65,69]{2,1,0:T(8,128)(2,1)S(1)}, u32[]{:S(2)}, u32[]{:S(2)}) collective-permute-start(bf16[4,65,69]{2,1,0:T(8,128)(2,1)S(1)} %pad_maximum_fusion.5), channel_id=1, source_target_pairs={{2,0},{4,2},{6,4},{8,6},{10,8},{12,10},{14,12},{16,14},{18,16},{20... | collective-permute-start | bytes 107648 | tf_op jit(solution)/shard_map/ppermute | solution.py:72
  26.4 12.9 %copy-start.15 = (s32[2]{0:T(128)S(1)}, s32[2]{0:T(128)}, u32[]{:S(2)}) copy-start(s32[2]{0:T(128)} %param.17) | copy-start | bytes 28
  35.6 12.8 %all-to-all-start = ((bf16[4,64,1024]{2,1,0:T(8,128)(2,1)}), bf16[4,64,1024]{2,1,0:T(8,128)(2,1)S(1)}, u32[]{:S(2)}, u32[]{:S(2)}) async-start(bf16[4,64,1024]{2,1,0:T(8,128)(2,1)} %bitcast.12), calls=%async_computation | async-start | bytes 1048576 | tf_op jit(solution)/shard_map/all_to_all | solution.py:374
  39.1 85.9 %all-gather.2.cloned.1.call-start = ((), (), s32[]{:S(2)}) async-start(), calls=%async_computation.4 | async-start | bytes 1179648 | tf_op jit(solution)/shard_map/all_gather | solution.py:378
  49.1 14.8 %copy-start.5 = (bf16[256,1024]{1,0:T(8,128)(2,1)S(1)}, bf16[256,1024]{1,0:T(8,128)(2,1)}, u32[]{:S(2)}) copy-start(bf16[256,1024]{1,0:T(8,128)(2,1)} %down_ref) | copy-start | bytes 1572868
  50.2 10.9 %collective-permute-start.3 = (bf16[8,2,8,1024]{3,2,1,0:T(8,128)(2,1)}, bf16[8,2,8,1024]{3,2,1,0:T(8,128)(2,1)}, u32[]{:S(2)}, u32[]{:S(2)}) collective-permute-start(bf16[8,2,8,1024]{3,2,1,0:T(8,128)(2,1)} %get-tuple-element.54), channel_id=1, source_target_pairs={{0,2},{2,4},{4,6},{6,8},{8,10},{10,12},{12,14},{14,0},{1,3},{3,5},... | collective-permute-start | bytes 786440 | tf_op jit(solution)/shard_map/ppermute | solution.py:252
  50.2 10.9 %collective-permute-start.4 = (bf16[8,2,8,1024]{3,2,1,0:T(8,128)(2,1)}, bf16[8,2,8,1024]{3,2,1,0:T(8,128)(2,1)}, u32[]{:S(2)}, u32[]{:S(2)}) collective-permute-start(bf16[8,2,8,1024]{3,2,1,0:T(8,128)(2,1)} %get-tuple-element.54), channel_id=1, source_target_pairs={{2,0},{4,2},{6,4},{8,6},{10,8},{12,10},{14,12},{0,14},{3,1},{5,3},... | collective-permute-start | bytes 786440 | tf_op jit(solution)/shard_map/ppermute | solution.py:254
  55.4 12.1 %collective-permute-start.7 = (bf16[208,1024]{1,0:T(8,128)(2,1)}, bf16[208,1024]{1,0:T(8,128)(2,1)}, u32[]{:S(2)}, u32[]{:S(2)}) collective-permute-start(bf16[208,1024]{1,0:T(8,128)(2,1)} %pad_maximum_fusion.1), channel_id=1, source_target_pairs={{0,17},{17,0},{1,16},{16,1},{2,19},{19,2},{3,18},{18,3},{4,21},{21... | collective-permute-start | bytes 1277960 | tf_op jit(solution)/shard_map/ppermute | solution.py:22
  61.1 8.3 %collective-permute-start.5 = (bf16[8,2,8,1024]{3,2,1,0:T(8,128)(2,1)}, bf16[8,2,8,1024]{3,2,1,0:T(8,128)(2,1)}, u32[]{:S(2)}, u32[]{:S(2)}) collective-permute-start(bf16[8,2,8,1024]{3,2,1,0:T(8,128)(2,1)} %collective-permute-done.3), channel_id=1, source_target_pairs={{0,2},{2,4},{4,6},{6,8},{8,10},{10,12},{12,14},{14,0},{1,3},{3,5},... | collective-permute-start | bytes 786440 | tf_op jit(solution)/shard_map/ppermute | solution.py:252
  61.1 8.3 %collective-permute-start.6 = (bf16[8,2,8,1024]{3,2,1,0:T(8,128)(2,1)}, bf16[8,2,8,1024]{3,2,1,0:T(8,128)(2,1)}, u32[]{:S(2)}, u32[]{:S(2)}) collective-permute-start(bf16[8,2,8,1024]{3,2,1,0:T(8,128)(2,1)} %collective-permute-done.4), channel_id=1, source_target_pairs={{2,0},{4,2},{6,4},{8,6},{10,8},{12,10},{14,12},{0,14},{3,1},{5,3},... | collective-permute-start | bytes 786440 | tf_op jit(solution)/shard_map/ppermute | solution.py:254
  65.9 20.5 %collective-permute-start.11 = (bf16[384,1024]{1,0:T(8,128)(2,1)}, bf16[384,1024]{1,0:T(8,128)(2,1)}, u32[]{:S(2)}, u32[]{:S(2)}) collective-permute-start(bf16[384,1024]{1,0:T(8,128)(2,1)} %pad_maximum_fusion), channel_id=1, source_target_pairs={{0,17},{17,0},{1,16},{16,1},{2,19},{19,2},{3,18},{18,3},{4,21},{21... | collective-permute-start | bytes 2359304 | tf_op jit(solution)/shard_map/ppermute | solution.py:22
  66.8 99.4 %reduce-scatter.2.cloned.1.call-start = ((), (), s32[]{:S(2)}) async-start(), calls=%async_computation.3 | async-start | bytes 2359296 | tf_op jit(solution)/shard_map/reduce_scatter | solution.py:422
  69.5 7.4 %collective-permute-start.8 = (bf16[8,2,8,1024]{3,2,1,0:T(8,128)(2,1)}, bf16[8,2,8,1024]{3,2,1,0:T(8,128)(2,1)S(1)}, u32[]{:S(2)}, u32[]{:S(2)}) collective-permute-start(bf16[8,2,8,1024]{3,2,1,0:T(8,128)(2,1)} %collective-permute-done.5), channel_id=1, source_target_pairs={{0,2},{2,4},{4,6},{6,8},{8,10},{10,12},{12,14},{14,0},{1,3},{3,5},... | collective-permute-start | bytes 786440 | tf_op jit(solution)/shard_map/ppermute | solution.py:252
  71.4 9.1 %collective-permute-start.9 = (bf16[8,2,8,1024]{3,2,1,0:T(8,128)(2,1)}, bf16[8,2,8,1024]{3,2,1,0:T(8,128)(2,1)S(1)}, u32[]{:S(2)}, u32[]{:S(2)}) collective-permute-start(bf16[8,2,8,1024]{3,2,1,0:T(8,128)(2,1)} %collective-permute-done.6), channel_id=1, source_target_pairs={{2,0},{4,2},{6,4},{8,6},{10,8},{12,10},{14,12},{0,14},{3,1},{5,3},... | collective-permute-start | bytes 786440 | tf_op jit(solution)/shard_map/ppermute | solution.py:254
  76.9 9.4 %collective-permute-start.10 = (bf16[8,2,8,1024]{3,2,1,0:T(8,128)(2,1)S(1)}, bf16[8,2,8,1024]{3,2,1,0:T(8,128)(2,1)S(1)}, u32[]{:S(2)}, u32[]{:S(2)}) collective-permute-start(bf16[8,2,8,1024]{3,2,1,0:T(8,128)(2,1)S(1)} %collective-permute-done.8), channel_id=1, source_target_pairs={{0,2},{2,4},{4,6},{6,8},{8,10},{10,12},{12,14},{14,0},{1,3},{3,5},... | collective-permute-start | bytes 786440 | tf_op jit(solution)/shard_map/ppermute | solution.py:252
  86.4 12.4 %collective-permute-start.15 = (bf16[384,1024]{1,0:T(8,128)(2,1)}, bf16[384,1024]{1,0:T(8,128)(2,1)}, u32[]{:S(2)}, u32[]{:S(2)}) collective-permute-start(bf16[384,1024]{1,0:T(8,128)(2,1)} %collective-permute-done.11.some_ref), channel_id=1, source_target_pairs={{0,32},{32,0},{1,33},{33,1},{2,34},{34,2},{3,35},{35,3},{4,36},{36... | collective-permute-start | bytes 2359304 | tf_op jit(solution)/shard_map/ppermute | solution.py:417
  95.1 10.9 %collective-permute-start.12 = (bf16[192,512]{1,0:T(8,128)(2,1)}, bf16[192,512]{1,0:T(8,128)(2,1)S(1)}, u32[]{:S(2)}, u32[]{:S(2)}) collective-permute-start(bf16[192,512]{1,0:T(8,128)(2,1)} %get-tuple-element.41), channel_id=1, source_target_pairs={{0,32},{32,0},{16,48},{48,16},{1,33},{33,1},{17,49},{49,17},{2,34}... | collective-permute-start | bytes 589832 | tf_op jit(solution)/shard_map/ppermute | solution.py:413
  95.1 10.8 %collective-permute-start.13 = (bf16[192,512]{1,0:T(8,128)(2,1)}, bf16[192,512]{1,0:T(8,128)(2,1)S(1)}, u32[]{:S(2)}, u32[]{:S(2)}) collective-permute-start(bf16[192,512]{1,0:T(8,128)(2,1)} %get-tuple-element.42), channel_id=1, source_target_pairs={{0,16},{16,0},{32,48},{48,32},{1,17},{17,1},{33,49},{49,33},{2,18}... | collective-permute-start | bytes 589832 | tf_op jit(solution)/shard_map/ppermute | solution.py:414
  95.1 12.7 %collective-permute-start.14 = (bf16[192,512]{1,0:T(8,128)(2,1)S(1)}, bf16[192,512]{1,0:T(8,128)(2,1)}, u32[]{:S(2)}, u32[]{:S(2)}) collective-permute-start(bf16[192,512]{1,0:T(8,128)(2,1)S(1)} %get-tuple-element.43), channel_id=1, source_target_pairs={{0,48},{48,0},{16,32},{32,16},{1,49},{49,1},{17,33},{33,17},{2,50}... | collective-permute-start | bytes 589832 | tf_op jit(solution)/shard_map/ppermute | solution.py:415
  108.8 16.2 %collective-permute-start.18 = (bf16[2,128,512]{2,1,0:T(8,128)(2,1)S(1)}, bf16[2,128,512]{2,1,0:T(8,128)(2,1)S(1)}, u32[]{:S(2)}, u32[]{:S(2)}) collective-permute-start(bf16[2,128,512]{2,1,0:T(8,128)(2,1)S(1)} %pad_maximum_fusion.3.kv2_ref), channel_id=1, source_target_pairs={{64,0},{128,64},{192,128},{0,192},{65,1},{129,65},{193,129},{1,193... | collective-permute-start | bytes 786440 | tf_op jit(solution)/shard_map/ppermute | solution.py:430
  114.2 21.6 %collective-permute-start.20 = (bf16[2,128,512]{2,1,0:T(8,128)(2,1)S(1)}, bf16[2,128,512]{2,1,0:T(8,128)(2,1)S(1)}, u32[]{:S(2)}, u32[]{:S(2)}) collective-permute-start(bf16[2,128,512]{2,1,0:T(8,128)(2,1)S(1)} %pad_maximum_fusion.3.kv2_ref), channel_id=1, source_target_pairs={{0,64},{64,128},{128,192},{192,0},{1,65},{65,129},{129,193},{193,1... | collective-permute-start | bytes 786440 | tf_op jit(solution)/shard_map/ppermute | solution.py:431
  114.3 14.7 %collective-permute-start.16 = (bf16[2,128,512]{2,1,0:T(8,128)(2,1)S(1)}, bf16[2,128,512]{2,1,0:T(8,128)(2,1)S(1)}, u32[]{:S(2)}, u32[]{:S(2)}) collective-permute-start(bf16[2,128,512]{2,1,0:T(8,128)(2,1)S(1)} %pad_maximum_fusion.2.kv_ref), channel_id=1, source_target_pairs={{0,64},{64,128},{128,192},{192,0},{1,65},{65,129},{129,193},{193,1... | collective-permute-start | bytes 786440 | tf_op jit(solution)/shard_map/ppermute | solution.py:430
  114.4 21.5 %collective-permute-start.21 = (bf16[2,128,512]{2,1,0:T(8,128)(2,1)S(1)}, bf16[2,128,512]{2,1,0:T(8,128)(2,1)S(1)}, u32[]{:S(2)}, u32[]{:S(2)}) collective-permute-start(bf16[2,128,512]{2,1,0:T(8,128)(2,1)S(1)} %pad_maximum_fusion.2.kv_ref), channel_id=1, source_target_pairs={{64,0},{128,64},{192,128},{0,192},{65,1},{129,65},{193,129},{1,193... | collective-permute-start | bytes 786440 | tf_op jit(solution)/shard_map/ppermute | solution.py:431
  125.0 40.9 %collective-permute-start.22 = (bf16[512,1024]{1,0:T(8,128)(2,1)}, bf16[512,1024]{1,0:T(8,128)(2,1)S(1)}, u32[]{:S(2)}, u32[]{:S(2)}) collective-permute-start(bf16[512,1024]{1,0:T(8,128)(2,1)} %all-gather.2.cloned.1.call-done), channel_id=1, source_target_pairs={{0,17},{17,0},{1,16},{16,1},{2,19},{19,2},{3,18},{18,3},{4,21},{21... | collective-permute-start | bytes 3145736 | tf_op jit(solution)/shard_map/ppermute | solution.py:22
  125.0 16.6 %collective-permute-start.19 = (bf16[2,128,512]{2,1,0:T(8,128)(2,1)S(1)}, bf16[2,128,512]{2,1,0:T(8,128)(2,1)S(1)}, u32[]{:S(2)}, u32[]{:S(2)}) collective-permute-start(bf16[2,128,512]{2,1,0:T(8,128)(2,1)S(1)} %collective-permute-done.18.kv2_ref), channel_id=1, source_target_pairs={{64,0},{128,64},{192,128},{0,192},{65,1},{129,65},{193,129},{1,193... | collective-permute-start | bytes 786440 | tf_op jit(solution)/shard_map/ppermute | solution.py:432
  129.0 12.6 %collective-permute-start.17 = (bf16[2,128,512]{2,1,0:T(8,128)(2,1)S(1)}, bf16[2,128,512]{2,1,0:T(8,128)(2,1)S(1)}, u32[]{:S(2)}, u32[]{:S(2)}) collective-permute-start(bf16[2,128,512]{2,1,0:T(8,128)(2,1)S(1)} %collective-permute-done.16.kv_ref), channel_id=1, source_target_pairs={{0,64},{64,128},{128,192},{192,0},{1,65},{65,129},{129,193},{193,1... | collective-permute-start | bytes 786440 | tf_op jit(solution)/shard_map/ppermute | solution.py:432
  148.2 17.3 %copy-start.10 = (bf16[512,1024]{1,0:T(8,128)(2,1)S(1)}, bf16[512,1024]{1,0:T(8,128)(2,1)}, u32[]{:S(2)}) copy-start(bf16[512,1024]{1,0:T(8,128)(2,1)} %all-gather.2.cloned.1.call-done) | copy-start | bytes 3145732
  148.2 16.4 %all-to-all-start.1 = ((bf16[32,32,128]{2,1,0:T(8,128)(2,1)}), bf16[32,32,128]{2,1,0:T(8,128)(2,1)S(1)}, u32[]{:S(2)}, u32[]{:S(2)}) async-start(bf16[32,32,128]{2,1,0:T(8,128)(2,1)} %shard_map.134), calls=%async_computation.2 | async-start | bytes 524288 | tf_op jit(solution)/shard_map/all_to_all | solution.py:440
  (11 other events, 65.0 us)
Sparse Core Ops, SparseCore 0:
  66.9 32.9 all-gather.1
  107.9 35.1 reduce-scatter.1

commit v4 on v3

--- a/solution.py
+++ b/solution.py
@@ -247,17 +247,22 @@
     out = place(out, own, 0, z)
     ups = [own[p * size : (p + 1) * size] for p in range(parts)]
     downs = list(ups)
-    for step in range(1, Z // 2 + 1):
+    for step in range(1, Z // 2):
         for p in range(parts):
             ups[p] = lax.ppermute(ups[p], "z", forward)
-            if step < Z // 2:
-                downs[p] = lax.ppermute(downs[p], "z", backward)
+            downs[p] = lax.ppermute(downs[p], "z", backward)
         if step == 2:
             ups, downs, beside = lax.optimization_barrier((ups, downs, beside))
         for p in range(parts):
             out = place(out, ups[p], p, z - step + Z)
-            if step < Z // 2:
-                out = place(out, downs[p], p, z + step)
+            out = place(out, downs[p], p, z + step)
+    far = size // 2
+    for p in range(parts):
+        up = lax.ppermute(ups[p][:far], "z", forward)
+        down = lax.ppermute(downs[p][far:], "z", backward)
+        at = ((z + Z // 2) % Z) * cols
+        out = lax.dynamic_update_slice(out, up, (p * size, 0, at, 0))
+        out = lax.dynamic_update_slice(out, down, (p * size + far, 0, at, 0))
     return out, beside
 
 
@@ -432,9 +437,9 @@
     far = [lax.ppermute(near[0], "x", x_up), lax.ppermute(near[1], "x", x_down)]
 
     acc = attend(ids, q, (first, second))
-    acc, w_out_half = lax.optimization_barrier((acc, w_out_half))
+    then_ids, w_out_half = lax.optimization_barrier((ids, w_out_half))
     w_out_other = other_half_weights(w_out_half)
-    acc = attend(ids, q, near, acc)
+    acc = attend(then_ids, q, near, acc)
     acc = attend(ids, q, late, acc)
     attended = attend(ids, q, far, acc, last=True)
     attended = lax.all_to_all(attended, ("core", "yh", "z"), 0, 0, tiled=True)

time: 176 us -> 174 us (0.989)
  waiting for transfers between devices: 45.4 us -> 39.3 us
  starting transfers between devices: 50.4 us -> 54.6 us
    ppermute x4 -> x3, waiting for transfers between devices: 14.4 us -> 7.55 us  [ring_z(): ups[p] = lax.ppermute(ups[p], 'z', forward)]
    ppermute x0 -> x2, starting transfers between devices: none -> 3.75 us  [the longest x1 3.49 us: ring_z(): down = lax.ppermute(downs[p][far:], 'z', backward)]
    ppermute x0 -> x2, waiting for transfers between devices: none -> 2.22 us  [the longest x1 1.52 us: ring_z(): up = lax.ppermute(ups[p][:far], 'z', forward)]
    ppermute x3, waiting for transfers between devices: 2.62 us -> 0.52 us  [ring_z(): downs[p] = lax.ppermute(downs[p], 'z', backward)]
    dynamic_update_slice x7 -> x6, local copies, waits for them, and re-layouts: 3.95 us -> 3.94 us  [place(): lax.dynamic_update_slice(out, shard, (part * size, 0, at % Z * cols, 0))]
  transfers between devices with their start and end apart: 27 -> 28, of which waited for: 12 -> 14; matrix products, arithmetic and copies ran while one was open for 7% -> 7% of each run, Pallas kernels for 19% -> 19%
where the time goes in v4:
time: 174 us; the launch traced here: 173 us
  starting transfers between devices  54.6 us (31%)
  Pallas kernels  43.6 us (25%)
  waiting for transfers between devices  39.3 us (23%)
  local copies, waits for them, and re-layouts  14.8 us (9%)
  between operations  14 us (8%)
  other arithmetic  5.9 us (3%)
    pallas_call x4, Pallas kernels, attend(): pl.pallas_call(functools.partial(attend_kernel, last), grid_spec=pltpu.Pr...  23.6 us
    all_to_all x1, waiting for transfers between devices, shards(): attended = lax.all_to_all(attended, ('core', 'yh', 'z'), 0, 0, tiled=True)  11.8 us
    ppermute x3, starting transfers between devices, ring_z(): downs[p] = lax.ppermute(downs[p], 'z', backward)  9.68 us
    pallas_call x1, Pallas kernels, embed(): pl.pallas_call(embed_kernel, grid_spec=pltpu.PrefetchScalarGridSpec(num_s...  9.19 us
    all_to_all x1, waiting for transfers between devices, shards(): part = lax.all_to_all(part, ('yh', 'yl'), 0, 0, tiled=True)  8.88 us
    ppermute x2, starting transfers between devices, column(): edge = lax.ppermute(edge, LON, pairs)  8.38 us
    ppermute x3, waiting for transfers between devices, ring_z(): ups[p] = lax.ppermute(ups[p], 'z', forward)  7.55 us
    all_to_all x1, starting transfers between devices, shards(): attended = lax.all_to_all(attended, ('core', 'yh', 'z'), 0, 0, tiled=True)  6.16 us
  transfers between devices with their start and end apart: 28, of which 14 were waited for; matrix products, arithmetic and copies ran while one was open for 7% of the time, Pallas kernels for 19%

profile of v4, /device:TPU:1, one launch (start us, length us, event | category | flops | bytes accessed | tf_op | source)
XLA Modules:
  0.0 172.9 jit_solution(7805036715157746632)
XLA Ops:
  6.6 2.2 %copy-done.1 = bf16[4,69,64,64]{1,3,2,0:T(8,128)(2,1)S(1)} copy-done((bf16[4,69,64,64]{1,3,2,0:T(8,128)(2,1)S(1)}, bf16[4,69,64,64]{1,3,2,0:T(8,128)(2,1)}, u32[]{:S(2)}) %copy-start.1) | copy-done | bytes 2261016
  8.8 1.4 shard_map.127
  10.2 4.5 %collective-permute-start = (bf16[4,64,69]{2,1,0:T(8,128)(2,1)S(1)}, bf16[4,64,69]{2,1,0:T(8,128)(2,1)S(1)}, u32[]{:S(2)}, u32[]{:S(2)}) collective-permute-start(bf16[4,64,69]{2,1,0:T(8,128)(2,1)S(1)} %get-tuple-element.29), channel_id=1, source_target_pairs={{0,32},{32,64},{64,96},{96,128},{128,160},{160,192},{192,224},{33,... | collective-permute-start | bytes 105992 | tf_op jit(solution)/shard_map/ppermute | solution.py:68
  16.0 1.7 collective-permute-start.1
  17.8 6.7 %collective-permute-start.2 = (bf16[4,65,69]{2,1,0:T(8,128)(2,1)S(1)}, bf16[4,65,69]{2,1,0:T(8,128)(2,1)S(1)}, u32[]{:S(2)}, u32[]{:S(2)}) collective-permute-start(bf16[4,65,69]{2,1,0:T(8,128)(2,1)S(1)} %pad_maximum_fusion.5), channel_id=1, source_target_pairs={{2,0},{4,2},{6,4},{8,6},{10,8},{12,10},{14,12},{16,14},{18,16},{20... | collective-permute-start | bytes 107648 | tf_op jit(solution)/shard_map/ppermute | solution.py:72
  24.5 1.5 collective-permute-done.1
  26.4 9.2 %shard_map.128 = bf16[256,1024]{1,0:T(8,128)(2,1)} custom-call(s32[4]{0:T(128)S(1)} %pad_add_fusion.s_ref.ids_ref, bf16[4,8,8,64,69]{4,3,2,1,0:T(8,128)(2,1)} %bitcast.72, bf16[4,64,69]{2,1,0:T(8,128)(2,1)S(1)} %collective-permute-done.row_ref, f32[5,32,69]{2,1,0:T(8,128)S(1)} %bitcast.83, f32[5,32,69]{2,1,0:T(8,128)S(1)} %bitcast.82, ...), custom_call_target="tpu_custom_call" | custom-call | flops 8000000000 | bytes 12582912 | tf_op jit(solution)/shard_map/pallas_call | solution.py:129
  35.6 3.5 %all-to-all-start = ((bf16[4,64,1024]{2,1,0:T(8,128)(2,1)}), bf16[4,64,1024]{2,1,0:T(8,128)(2,1)S(1)}, u32[]{:S(2)}, u32[]{:S(2)}) async-start(bf16[4,64,1024]{2,1,0:T(8,128)(2,1)} %bitcast.12), calls=%async_computation | async-start | bytes 1048576 | tf_op jit(solution)/shard_map/all_to_all | solution.py:379
  39.6 8.9 %all-to-all-done = bf16[4,64,1024]{2,1,0:T(8,128)(2,1)S(1)} async-done(((bf16[4,64,1024]{2,1,0:T(8,128)(2,1)}), bf16[4,64,1024]{2,1,0:T(8,128)(2,1)S(1)}, u32[]{:S(2)}, u32[]{:S(2)}) %all-to-all-start) | async-done | bytes 524320 | tf_op jit(solution)/shard_map/all_to_all | solution.py:379
  50.3 4.3 %collective-permute-start.4 = (bf16[8,2,8,1024]{3,2,1,0:T(8,128)(2,1)}, bf16[8,2,8,1024]{3,2,1,0:T(8,128)(2,1)}, u32[]{:S(2)}, u32[]{:S(2)}) collective-permute-start(bf16[8,2,8,1024]{3,2,1,0:T(8,128)(2,1)} %get-tuple-element.54), channel_id=1, source_target_pairs={{2,0},{4,2},{6,4},{8,6},{10,8},{12,10},{14,12},{0,14},{3,1},{5,3},... | collective-permute-start | bytes 786440 | tf_op jit(solution)/shard_map/ppermute | solution.py:253
  57.4 3.8 %collective-permute-done.3 = bf16[8,2,8,1024]{3,2,1,0:T(8,128)(2,1)} collective-permute-done((bf16[8,2,8,1024]{3,2,1,0:T(8,128)(2,1)}, bf16[8,2,8,1024]{3,2,1,0:T(8,128)(2,1)}, u32[]{:S(2)}, u32[]{:S(2)}) %collective-permute-start.3) | collective-permute-done | bytes 262176 | tf_op jit(solution)/shard_map/ppermute | solution.py:252
  61.2 2.7 %collective-permute-start.6 = (bf16[8,2,8,1024]{3,2,1,0:T(8,128)(2,1)}, bf16[8,2,8,1024]{3,2,1,0:T(8,128)(2,1)}, u32[]{:S(2)}, u32[]{:S(2)}) collective-permute-start(bf16[8,2,8,1024]{3,2,1,0:T(8,128)(2,1)} %collective-permute-done.4), channel_id=1, source_target_pairs={{2,0},{4,2},{6,4},{8,6},{10,8},{12,10},{14,12},{0,14},{3,1},{5,3},... | collective-permute-start | bytes 786440 | tf_op jit(solution)/shard_map/ppermute | solution.py:253
  67.5 2.0 %collective-permute-done.5 = bf16[8,2,8,1024]{3,2,1,0:T(8,128)(2,1)} collective-permute-done((bf16[8,2,8,1024]{3,2,1,0:T(8,128)(2,1)}, bf16[8,2,8,1024]{3,2,1,0:T(8,128)(2,1)}, u32[]{:S(2)}, u32[]{:S(2)}) %collective-permute-start.5) | collective-permute-done | bytes 262176 | tf_op jit(solution)/shard_map/ppermute | solution.py:252
  69.5 2.7 %collective-permute-start.9 = (bf16[8,2,8,1024]{3,2,1,0:T(8,128)(2,1)}, bf16[8,2,8,1024]{3,2,1,0:T(8,128)(2,1)S(1)}, u32[]{:S(2)}, u32[]{:S(2)}) collective-permute-start(bf16[8,2,8,1024]{3,2,1,0:T(8,128)(2,1)} %collective-permute-done.6), channel_id=1, source_target_pairs={{2,0},{4,2},{6,4},{8,6},{10,8},{12,10},{14,12},{0,14},{3,1},{5,3},... | collective-permute-start | bytes 786440 | tf_op jit(solution)/shard_map/ppermute | solution.py:253
  75.1 1.8 %collective-permute-done.8 = bf16[8,2,8,1024]{3,2,1,0:T(8,128)(2,1)S(1)} collective-permute-done((bf16[8,2,8,1024]{3,2,1,0:T(8,128)(2,1)}, bf16[8,2,8,1024]{3,2,1,0:T(8,128)(2,1)S(1)}, u32[]{:S(2)}, u32[]{:S(2)}) %collective-permute-start.8) | collective-permute-done | bytes 262176 | tf_op jit(solution)/shard_map/ppermute | solution.py:252
  77.7 3.5 %collective-permute-start.11 = (bf16[4,2,8,1024]{3,2,1,0:T(8,128)(2,1)S(1)}, bf16[4,2,8,1024]{3,2,1,0:T(8,128)(2,1)S(1)}, u32[]{:S(2)}, u32[]{:S(2)}) collective-permute-start(bf16[4,2,8,1024]{3,2,1,0:T(8,128)(2,1)S(1)} %slice.108), channel_id=1, source_target_pairs={{2,0},{4,2},{6,4},{8,6},{10,8},{12,10},{14,12},{0,14},{3,1},{5,3},... | collective-permute-start | bytes 393224 | tf_op jit(solution)/shard_map/ppermute | solution.py:262
  81.2 1.5 collective-permute-done.10
  83.8 4.1 %collective-permute-start.16 = (bf16[384,1024]{1,0:T(8,128)(2,1)}, bf16[384,1024]{1,0:T(8,128)(2,1)}, u32[]{:S(2)}, u32[]{:S(2)}) collective-permute-start(bf16[384,1024]{1,0:T(8,128)(2,1)} %collective-permute-done.12.some_ref), channel_id=1, source_target_pairs={{0,32},{32,0},{1,33},{33,1},{2,34},{34,2},{3,35},{35,3},{4,36},{36... | collective-permute-start | bytes 2359304 | tf_op jit(solution)/shard_map/ppermute | solution.py:422
  88.9 3.5 %shard_map.129 = (bf16[192,512]{1,0:T(8,128)(2,1)S(1)}, bf16[192,512]{1,0:T(8,128)(2,1)}, bf16[192,512]{1,0:T(8,128)(2,1)}, bf16[192,512]{1,0:T(8,128)(2,1)S(1)}) custom-call(s32[4]{0:T(128)S(1)} %pad_add_fusion.s_ref.ids_ref, bf16[8,2,64,1024]{3,2,1,0:T(8,128)(2,1)S(1)} %constant_dynamic-update-slice_fusion.x_ref, bf16[192,1024]{1,0:T(8,128)(2,1)S(1)} %bitcast.81, ...), custom_call_target="tpu_custom_call" | custom-call | flops 3000000000 | bytes 4194304 | tf_op jit(solution)/shard_map/pallas_call | solution.py:293
  92.4 3.6 %collective-permute-start.15 = (bf16[192,512]{1,0:T(8,128)(2,1)S(1)}, bf16[192,512]{1,0:T(8,128)(2,1)}, u32[]{:S(2)}, u32[]{:S(2)}) collective-permute-start(bf16[192,512]{1,0:T(8,128)(2,1)S(1)} %get-tuple-element.43), channel_id=1, source_target_pairs={{0,48},{48,0},{16,32},{32,16},{1,49},{49,1},{17,33},{33,17},{2,50}... | collective-permute-start | bytes 589832 | tf_op jit(solution)/shard_map/ppermute | solution.py:420
  96.1 5.9 %shard_map.130 = bf16[8,2,64,1024]{3,2,1,0:T(8,128)(2,1)S(1)} custom-call(s32[4]{0:T(128)S(1)} %pad_add_fusion.s_ref.ids_ref, bf16[8,2,64,1024]{3,2,1,0:T(8,128)(2,1)S(1)} %constant_dynamic-update-slice_fusion.x_ref, bf16[8,2,8,1024]{3,2,1,0:T(8,128)(2,1)S(1)} %get-tuple-element.64.tok_ref, bf16[2,256,1024]{2,1,0:T(8,128)(2,1)S(1)} %copy-done.4, ...), custom_call_target="tpu_custom_call" | custom-call | flops 6000000000 | bytes 8388608 | tf_op jit(solution)/shard_map/pallas_call | solution.py:332
  103.3 1.8 %collective-permute-done.15 = bf16[192,512]{1,0:T(8,128)(2,1)} collective-permute-done((bf16[192,512]{1,0:T(8,128)(2,1)S(1)}, bf16[192,512]{1,0:T(8,128)(2,1)}, u32[]{:S(2)}, u32[]{:S(2)}) %collective-permute-start.15) | collective-permute-done | bytes 196640 | tf_op jit(solution)/shard_map/ppermute | solution.py:420
  106.1 4.5 %collective-permute-start.19 = (bf16[2,128,512]{2,1,0:T(8,128)(2,1)S(1)}, bf16[2,128,512]{2,1,0:T(8,128)(2,1)S(1)}, u32[]{:S(2)}, u32[]{:S(2)}) collective-permute-start(bf16[2,128,512]{2,1,0:T(8,128)(2,1)S(1)} %pad_maximum_fusion.3.kv2_ref), channel_id=1, source_target_pairs={{64,0},{128,64},{192,128},{0,192},{65,1},{129,65},{193,129},{1,193... | collective-permute-start | bytes 786440 | tf_op jit(solution)/shard_map/ppermute | solution.py:435
  110.8 2.8 %collective-permute-start.22 = (bf16[2,128,512]{2,1,0:T(8,128)(2,1)S(1)}, bf16[2,128,512]{2,1,0:T(8,128)(2,1)S(1)}, u32[]{:S(2)}, u32[]{:S(2)}) collective-permute-start(bf16[2,128,512]{2,1,0:T(8,128)(2,1)S(1)} %pad_maximum_fusion.2.kv_ref), channel_id=1, source_target_pairs={{64,0},{128,64},{192,128},{0,192},{65,1},{129,65},{193,129},{1,193... | collective-permute-start | bytes 786440 | tf_op jit(solution)/shard_map/ppermute | solution.py:436
  114.7 5.7 %shard_map.131.refs_0_ = f32[2048,128]{1,0:T(8,128)S(1)} custom-call(s32[4]{0:T(128)S(1)} %pad_add_fusion.s_ref.ids_ref, bf16[2048,64]{1,0:T(8,128)(2,1)S(1)} %bitcast.76, bf16[2,128,512]{2,1,0:T(8,128)(2,1)S(1)} %pad_maximum_fusion.2.kv_ref, bf16[2,128,512]{2,1,0:T(8,128)(2,1)S(1)} %pad_maximum_fusion.3.kv2_ref), custom_call_target="tpu_custom_call" | custom-call | flops 3221225472 | bytes 4194304 | tf_op jit(solution)/shard_map/pallas_call | solution.py:217
  123.0 2.5 %collective-permute-done.17.kv_ref = bf16[2,128,512]{2,1,0:T(8,128)(2,1)S(1)} collective-permute-done((bf16[2,128,512]{2,1,0:T(8,128)(2,1)S(1)}, bf16[2,128,512]{2,1,0:T(8,128)(2,1)S(1)}, u32[]{:S(2)}, u32[]{:S(2)}) %collective-permute-start.17) | collective-permute-done | bytes 262176 | tf_op jit(solution)/shard_map/ppermute | solution.py:435
  126.7 5.7 %shard_map.132.refs_0_ = f32[2048,128]{1,0:T(8,128)S(1)} custom-call(s32[4]{0:T(128)S(1)} %pad_add_fusion.s_ref.ids_ref, bf16[2048,64]{1,0:T(8,128)(2,1)S(1)} %bitcast.77, bf16[2,128,512]{2,1,0:T(8,128)(2,1)S(1)} %collective-permute-done.17.kv_ref, bf16[2,128,512]{2,1,0:T(8,128)(2,1)S(1)} %collective-permute-done.19.kv2_ref, f32[2048,128]{1,0:T(8,128)S(1)} %copy-done.9), custom_call_target="tpu_custom_call" | custom-call | flops 3221225472 | bytes 4194304 | tf_op jit(solution)/shard_map/pallas_call | solution.py:217
  132.4 5.7 %shard_map.133.refs_0_ = f32[2048,128]{1,0:T(8,128)S(1)} custom-call(s32[4]{0:T(128)S(1)} %pad_add_fusion.s_ref.ids_ref, bf16[2048,64]{1,0:T(8,128)(2,1)S(1)} %bitcast.78, bf16[2,128,512]{2,1,0:T(8,128)(2,1)S(1)} %collective-permute-done.21.kv_ref, bf16[2,128,512]{2,1,0:T(8,128)(2,1)S(1)} %collective-permute-done.22.kv2_ref, f32[2048,128]{1,0:T(8,128)S(1)} %shard_map.132.refs_0_), custom_call_target="tpu_custom_call" | custom-call | flops 3221225472 | bytes 4194304 | tf_op jit(solution)/shard_map/pallas_call | solution.py:217
  138.1 6.6 %shard_map.134 = bf16[32,32,128]{2,1,0:T(8,128)(2,1)} custom-call(s32[4]{0:T(128)S(1)} %pad_add_fusion.s_ref.ids_ref, bf16[2048,64]{1,0:T(8,128)(2,1)S(1)} %bitcast.79, bf16[2,128,512]{2,1,0:T(8,128)(2,1)S(1)} %collective-permute-done.18.kv_ref, bf16[2,128,512]{2,1,0:T(8,128)(2,1)S(1)} %collective-permute-done.20.kv2_ref, f32[2048,128]{1,0:T(8,128)S(1)} %shard_map.133.refs_0_), custom_call_target="tpu_custom_call" | custom-call | flops 3221225472 | bytes 4194304 | tf_op jit(solution)/shard_map/pallas_call | solution.py:217
  144.7 6.2 %all-to-all-start.1 = ((bf16[32,32,128]{2,1,0:T(8,128)(2,1)}), bf16[32,32,128]{2,1,0:T(8,128)(2,1)S(1)}, u32[]{:S(2)}, u32[]{:S(2)}) async-start(bf16[32,32,128]{2,1,0:T(8,128)(2,1)} %shard_map.134), calls=%async_computation.2 | async-start | bytes 524288 | tf_op jit(solution)/shard_map/all_to_all | solution.py:445
  150.9 11.8 %all-to-all-done.1 = bf16[32,32,128]{2,1,0:T(8,128)(2,1)S(1)} async-done(((bf16[32,32,128]{2,1,0:T(8,128)(2,1)}), bf16[32,32,128]{2,1,0:T(8,128)(2,1)S(1)}, u32[]{:S(2)}, u32[]{:S(2)}) %all-to-all-start.1) | async-done | bytes 262176 | tf_op jit(solution)/shard_map/all_to_all | solution.py:445
  164.3 1.7 fusion.3
  (134 shorter events, 25.1 us)
Async XLA Ops:
  6.5 32.8 %copy-start = (bf16[50,1024]{1,0:T(8,128)(2,1)S(1)}, bf16[50,1024]{1,0:T(8,128)(2,1)}, u32[]{:S(2)}) copy-start(bf16[50,1024]{1,0:T(8,128)(2,1)} %param.18) | copy-start | bytes 307204
  8.8 17.6 %copy-start.7 = (bf16[8,8,1024]{2,1,0:T(8,128)(2,1)S(1)}, bf16[8,8,1024]{2,1,0:T(8,128)(2,1)}, u32[]{:S(2)}) copy-start(bf16[8,8,1024]{2,1,0:T(8,128)(2,1)} %pos_ref.1) | copy-start | bytes 393220
  10.2 5.8 %collective-permute-start = (bf16[4,64,69]{2,1,0:T(8,128)(2,1)S(1)}, bf16[4,64,69]{2,1,0:T(8,128)(2,1)S(1)}, u32[]{:S(2)}, u32[]{:S(2)}) collective-permute-start(bf16[4,64,69]{2,1,0:T(8,128)(2,1)S(1)} %get-tuple-element.29), channel_id=1, source_target_pairs={{0,32},{32,64},{64,96},{96,128},{128,160},{160,192},{192,224},{33,... | collective-permute-start | bytes 105992 | tf_op jit(solution)/shard_map/ppermute | solution.py:68
  16.0 10.0 %collective-permute-start.1 = (bf16[4,65,69]{2,1,0:T(8,128)(2,1)S(1)}, bf16[4,65,69]{2,1,0:T(8,128)(2,1)S(1)}, u32[]{:S(2)}, u32[]{:S(2)}) collective-permute-start(bf16[4,65,69]{2,1,0:T(8,128)(2,1)S(1)} %pad_maximum_fusion.4), channel_id=1, source_target_pairs={{0,2},{2,4},{4,6},{6,8},{8,10},{10,12},{12,14},{14,16},{16,18},{18... | collective-permute-start | bytes 107648 | tf_op jit(solution)/shard_map/ppermute | solution.py:72
  17.8 8.3 %collective-permute-start.2 = (bf16[4,65,69]{2,1,0:T(8,128)(2,1)S(1)}, bf16[4,65,69]{2,1,0:T(8,128)(2,1)S(1)}, u32[]{:S(2)}, u32[]{:S(2)}) collective-permute-start(bf16[4,65,69]{2,1,0:T(8,128)(2,1)S(1)} %pad_maximum_fusion.5), channel_id=1, source_target_pairs={{2,0},{4,2},{6,4},{8,6},{10,8},{12,10},{14,12},{16,14},{18,16},{20... | collective-permute-start | bytes 107648 | tf_op jit(solution)/shard_map/ppermute | solution.py:72
  35.6 12.8 %all-to-all-start = ((bf16[4,64,1024]{2,1,0:T(8,128)(2,1)}), bf16[4,64,1024]{2,1,0:T(8,128)(2,1)S(1)}, u32[]{:S(2)}, u32[]{:S(2)}) async-start(bf16[4,64,1024]{2,1,0:T(8,128)(2,1)} %bitcast.12), calls=%async_computation | async-start | bytes 1048576 | tf_op jit(solution)/shard_map/all_to_all | solution.py:379
  39.1 82.3 %all-gather.2.cloned.1.call-start = ((), (), s32[]{:S(2)}) async-start(), calls=%async_computation.4 | async-start | bytes 1179648 | tf_op jit(solution)/shard_map/all_gather | solution.py:383
  49.4 14.4 %copy-start.5 = (bf16[256,1024]{1,0:T(8,128)(2,1)S(1)}, bf16[256,1024]{1,0:T(8,128)(2,1)}, u32[]{:S(2)}) copy-start(bf16[256,1024]{1,0:T(8,128)(2,1)} %down_ref) | copy-start | bytes 1572868
  50.2 10.9 %collective-permute-start.3 = (bf16[8,2,8,1024]{3,2,1,0:T(8,128)(2,1)}, bf16[8,2,8,1024]{3,2,1,0:T(8,128)(2,1)}, u32[]{:S(2)}, u32[]{:S(2)}) collective-permute-start(bf16[8,2,8,1024]{3,2,1,0:T(8,128)(2,1)} %get-tuple-element.54), channel_id=1, source_target_pairs={{0,2},{2,4},{4,6},{6,8},{8,10},{10,12},{12,14},{14,0},{1,3},{3,5},... | collective-permute-start | bytes 786440 | tf_op jit(solution)/shard_map/ppermute | solution.py:252
  50.3 10.9 %collective-permute-start.4 = (bf16[8,2,8,1024]{3,2,1,0:T(8,128)(2,1)}, bf16[8,2,8,1024]{3,2,1,0:T(8,128)(2,1)}, u32[]{:S(2)}, u32[]{:S(2)}) collective-permute-start(bf16[8,2,8,1024]{3,2,1,0:T(8,128)(2,1)} %get-tuple-element.54), channel_id=1, source_target_pairs={{2,0},{4,2},{6,4},{8,6},{10,8},{12,10},{14,12},{0,14},{3,1},{5,3},... | collective-permute-start | bytes 786440 | tf_op jit(solution)/shard_map/ppermute | solution.py:253
  55.4 12.1 %collective-permute-start.7 = (bf16[208,1024]{1,0:T(8,128)(2,1)}, bf16[208,1024]{1,0:T(8,128)(2,1)}, u32[]{:S(2)}, u32[]{:S(2)}) collective-permute-start(bf16[208,1024]{1,0:T(8,128)(2,1)} %pad_maximum_fusion.1), channel_id=1, source_target_pairs={{0,17},{17,0},{1,16},{16,1},{2,19},{19,2},{3,18},{18,3},{4,21},{21... | collective-permute-start | bytes 1277960 | tf_op jit(solution)/shard_map/ppermute | solution.py:22
  61.1 8.3 %collective-permute-start.5 = (bf16[8,2,8,1024]{3,2,1,0:T(8,128)(2,1)}, bf16[8,2,8,1024]{3,2,1,0:T(8,128)(2,1)}, u32[]{:S(2)}, u32[]{:S(2)}) collective-permute-start(bf16[8,2,8,1024]{3,2,1,0:T(8,128)(2,1)} %collective-permute-done.3), channel_id=1, source_target_pairs={{0,2},{2,4},{4,6},{6,8},{8,10},{10,12},{12,14},{14,0},{1,3},{3,5},... | collective-permute-start | bytes 786440 | tf_op jit(solution)/shard_map/ppermute | solution.py:252
  61.2 8.3 %collective-permute-start.6 = (bf16[8,2,8,1024]{3,2,1,0:T(8,128)(2,1)}, bf16[8,2,8,1024]{3,2,1,0:T(8,128)(2,1)}, u32[]{:S(2)}, u32[]{:S(2)}) collective-permute-start(bf16[8,2,8,1024]{3,2,1,0:T(8,128)(2,1)} %collective-permute-done.4), channel_id=1, source_target_pairs={{2,0},{4,2},{6,4},{8,6},{10,8},{12,10},{14,12},{0,14},{3,1},{5,3},... | collective-permute-start | bytes 786440 | tf_op jit(solution)/shard_map/ppermute | solution.py:253
  64.8 19.0 %collective-permute-start.12 = (bf16[384,1024]{1,0:T(8,128)(2,1)}, bf16[384,1024]{1,0:T(8,128)(2,1)}, u32[]{:S(2)}, u32[]{:S(2)}) collective-permute-start(bf16[384,1024]{1,0:T(8,128)(2,1)} %pad_maximum_fusion), channel_id=1, source_target_pairs={{0,17},{17,0},{1,16},{16,1},{2,19},{19,2},{3,18},{18,3},{4,21},{21... | collective-permute-start | bytes 2359304 | tf_op jit(solution)/shard_map/ppermute | solution.py:22
  65.7 98.6 %reduce-scatter.2.cloned.1.call-start = ((), (), s32[]{:S(2)}) async-start(), calls=%async_computation.3 | async-start | bytes 2359296 | tf_op jit(solution)/shard_map/reduce_scatter | solution.py:427
  69.5 7.4 %collective-permute-start.8 = (bf16[8,2,8,1024]{3,2,1,0:T(8,128)(2,1)}, bf16[8,2,8,1024]{3,2,1,0:T(8,128)(2,1)S(1)}, u32[]{:S(2)}, u32[]{:S(2)}) collective-permute-start(bf16[8,2,8,1024]{3,2,1,0:T(8,128)(2,1)} %collective-permute-done.5), channel_id=1, source_target_pairs={{0,2},{2,4},{4,6},{6,8},{8,10},{10,12},{12,14},{14,0},{1,3},{3,5},... | collective-permute-start | bytes 786440 | tf_op jit(solution)/shard_map/ppermute | solution.py:252
  69.5 8.2 %collective-permute-start.9 = (bf16[8,2,8,1024]{3,2,1,0:T(8,128)(2,1)}, bf16[8,2,8,1024]{3,2,1,0:T(8,128)(2,1)S(1)}, u32[]{:S(2)}, u32[]{:S(2)}) collective-permute-start(bf16[8,2,8,1024]{3,2,1,0:T(8,128)(2,1)} %collective-permute-done.6), channel_id=1, source_target_pairs={{2,0},{4,2},{6,4},{8,6},{10,8},{12,10},{14,12},{0,14},{3,1},{5,3},... | collective-permute-start | bytes 786440 | tf_op jit(solution)/shard_map/ppermute | solution.py:253
  76.9 5.9 %collective-permute-start.10 = (bf16[4,2,8,1024]{3,2,1,0:T(8,128)(2,1)S(1)}, bf16[4,2,8,1024]{3,2,1,0:T(8,128)(2,1)S(1)}, u32[]{:S(2)}, u32[]{:S(2)}) collective-permute-start(bf16[4,2,8,1024]{3,2,1,0:T(8,128)(2,1)S(1)} %slice.107), channel_id=1, source_target_pairs={{0,2},{2,4},{4,6},{6,8},{8,10},{10,12},{12,14},{14,0},{1,3},{3,5},... | collective-permute-start | bytes 393224 | tf_op jit(solution)/shard_map/ppermute | solution.py:261
  77.7 5.8 %collective-permute-start.11 = (bf16[4,2,8,1024]{3,2,1,0:T(8,128)(2,1)S(1)}, bf16[4,2,8,1024]{3,2,1,0:T(8,128)(2,1)S(1)}, u32[]{:S(2)}, u32[]{:S(2)}) collective-permute-start(bf16[4,2,8,1024]{3,2,1,0:T(8,128)(2,1)S(1)} %slice.108), channel_id=1, source_target_pairs={{2,0},{4,2},{6,4},{8,6},{10,8},{12,10},{14,12},{0,14},{3,1},{5,3},... | collective-permute-start | bytes 393224 | tf_op jit(solution)/shard_map/ppermute | solution.py:262
  83.8 12.3 %collective-permute-start.16 = (bf16[384,1024]{1,0:T(8,128)(2,1)}, bf16[384,1024]{1,0:T(8,128)(2,1)}, u32[]{:S(2)}, u32[]{:S(2)}) collective-permute-start(bf16[384,1024]{1,0:T(8,128)(2,1)} %collective-permute-done.12.some_ref), channel_id=1, source_target_pairs={{0,32},{32,0},{1,33},{33,1},{2,34},{34,2},{3,35},{35,3},{4,36},{36... | collective-permute-start | bytes 2359304 | tf_op jit(solution)/shard_map/ppermute | solution.py:422
  92.4 10.8 %collective-permute-start.13 = (bf16[192,512]{1,0:T(8,128)(2,1)}, bf16[192,512]{1,0:T(8,128)(2,1)S(1)}, u32[]{:S(2)}, u32[]{:S(2)}) collective-permute-start(bf16[192,512]{1,0:T(8,128)(2,1)} %get-tuple-element.41), channel_id=1, source_target_pairs={{0,32},{32,0},{16,48},{48,16},{1,33},{33,1},{17,49},{49,17},{2,34}... | collective-permute-start | bytes 589832 | tf_op jit(solution)/shard_map/ppermute | solution.py:418
  92.4 10.8 %collective-permute-start.14 = (bf16[192,512]{1,0:T(8,128)(2,1)}, bf16[192,512]{1,0:T(8,128)(2,1)S(1)}, u32[]{:S(2)}, u32[]{:S(2)}) collective-permute-start(bf16[192,512]{1,0:T(8,128)(2,1)} %get-tuple-element.42), channel_id=1, source_target_pairs={{0,16},{16,0},{32,48},{48,32},{1,17},{17,1},{33,49},{49,33},{2,18}... | collective-permute-start | bytes 589832 | tf_op jit(solution)/shard_map/ppermute | solution.py:419
  92.4 12.7 %collective-permute-start.15 = (bf16[192,512]{1,0:T(8,128)(2,1)S(1)}, bf16[192,512]{1,0:T(8,128)(2,1)}, u32[]{:S(2)}, u32[]{:S(2)}) collective-permute-start(bf16[192,512]{1,0:T(8,128)(2,1)S(1)} %get-tuple-element.43), channel_id=1, source_target_pairs={{0,48},{48,0},{16,32},{32,16},{1,49},{49,1},{17,33},{33,17},{2,50}... | collective-permute-start | bytes 589832 | tf_op jit(solution)/shard_map/ppermute | solution.py:420
  106.1 15.5 %collective-permute-start.19 = (bf16[2,128,512]{2,1,0:T(8,128)(2,1)S(1)}, bf16[2,128,512]{2,1,0:T(8,128)(2,1)S(1)}, u32[]{:S(2)}, u32[]{:S(2)}) collective-permute-start(bf16[2,128,512]{2,1,0:T(8,128)(2,1)S(1)} %pad_maximum_fusion.3.kv2_ref), channel_id=1, source_target_pairs={{64,0},{128,64},{192,128},{0,192},{65,1},{129,65},{193,129},{1,193... | collective-permute-start | bytes 786440 | tf_op jit(solution)/shard_map/ppermute | solution.py:435
  110.7 21.7 %collective-permute-start.21 = (bf16[2,128,512]{2,1,0:T(8,128)(2,1)S(1)}, bf16[2,128,512]{2,1,0:T(8,128)(2,1)S(1)}, u32[]{:S(2)}, u32[]{:S(2)}) collective-permute-start(bf16[2,128,512]{2,1,0:T(8,128)(2,1)S(1)} %pad_maximum_fusion.3.kv2_ref), channel_id=1, source_target_pairs={{0,64},{64,128},{128,192},{192,0},{1,65},{65,129},{129,193},{193,1... | collective-permute-start | bytes 786440 | tf_op jit(solution)/shard_map/ppermute | solution.py:436
  110.7 14.8 %collective-permute-start.17 = (bf16[2,128,512]{2,1,0:T(8,128)(2,1)S(1)}, bf16[2,128,512]{2,1,0:T(8,128)(2,1)S(1)}, u32[]{:S(2)}, u32[]{:S(2)}) collective-permute-start(bf16[2,128,512]{2,1,0:T(8,128)(2,1)S(1)} %pad_maximum_fusion.2.kv_ref), channel_id=1, source_target_pairs={{0,64},{64,128},{128,192},{192,0},{1,65},{65,129},{129,193},{193,1... | collective-permute-start | bytes 786440 | tf_op jit(solution)/shard_map/ppermute | solution.py:435
  110.8 21.6 %collective-permute-start.22 = (bf16[2,128,512]{2,1,0:T(8,128)(2,1)S(1)}, bf16[2,128,512]{2,1,0:T(8,128)(2,1)S(1)}, u32[]{:S(2)}, u32[]{:S(2)}) collective-permute-start(bf16[2,128,512]{2,1,0:T(8,128)(2,1)S(1)} %pad_maximum_fusion.2.kv_ref), channel_id=1, source_target_pairs={{64,0},{128,64},{192,128},{0,192},{65,1},{129,65},{193,129},{1,193... | collective-permute-start | bytes 786440 | tf_op jit(solution)/shard_map/ppermute | solution.py:436
  121.4 42.6 %collective-permute-start.23 = (bf16[512,1024]{1,0:T(8,128)(2,1)}, bf16[512,1024]{1,0:T(8,128)(2,1)S(1)}, u32[]{:S(2)}, u32[]{:S(2)}) collective-permute-start(bf16[512,1024]{1,0:T(8,128)(2,1)} %all-gather.2.cloned.1.call-done), channel_id=1, source_target_pairs={{0,17},{17,0},{1,16},{16,1},{2,19},{19,2},{3,18},{18,3},{4,21},{21... | collective-permute-start | bytes 3145736 | tf_op jit(solution)/shard_map/ppermute | solution.py:22
  121.7 16.4 %collective-permute-start.20 = (bf16[2,128,512]{2,1,0:T(8,128)(2,1)S(1)}, bf16[2,128,512]{2,1,0:T(8,128)(2,1)S(1)}, u32[]{:S(2)}, u32[]{:S(2)}) collective-permute-start(bf16[2,128,512]{2,1,0:T(8,128)(2,1)S(1)} %collective-permute-done.19.kv2_ref), channel_id=1, source_target_pairs={{64,0},{128,64},{192,128},{0,192},{65,1},{129,65},{193,129},{1,193... | collective-permute-start | bytes 786440 | tf_op jit(solution)/shard_map/ppermute | solution.py:437
  125.5 12.6 %collective-permute-start.18 = (bf16[2,128,512]{2,1,0:T(8,128)(2,1)S(1)}, bf16[2,128,512]{2,1,0:T(8,128)(2,1)S(1)}, u32[]{:S(2)}, u32[]{:S(2)}) collective-permute-start(bf16[2,128,512]{2,1,0:T(8,128)(2,1)S(1)} %collective-permute-done.17.kv_ref), channel_id=1, source_target_pairs={{0,64},{64,128},{128,192},{192,0},{1,65},{65,129},{129,193},{193,1... | collective-permute-start | bytes 786440 | tf_op jit(solution)/shard_map/ppermute | solution.py:437
  144.7 18.9 %copy-start.10 = (bf16[512,1024]{1,0:T(8,128)(2,1)S(1)}, bf16[512,1024]{1,0:T(8,128)(2,1)}, u32[]{:S(2)}) copy-start(bf16[512,1024]{1,0:T(8,128)(2,1)} %all-gather.2.cloned.1.call-done) | copy-start | bytes 3145732
  144.7 18.0 %all-to-all-start.1 = ((bf16[32,32,128]{2,1,0:T(8,128)(2,1)}), bf16[32,32,128]{2,1,0:T(8,128)(2,1)S(1)}, u32[]{:S(2)}, u32[]{:S(2)}) async-start(bf16[32,32,128]{2,1,0:T(8,128)(2,1)} %shard_map.134), calls=%async_computation.2 | async-start | bytes 524288 | tf_op jit(solution)/shard_map/all_to_all | solution.py:445
  (12 other events, 78.0 us)
Sparse Core Ops, SparseCore 0:
  65.8 33.3 all-gather.1
  105.2 36.0 reduce-scatter.1
